TPU v7x, 32 devices: a whole 2x2x4 slice. The times are simulated.
32 devices in a mesh: groups: 2 (over y), adapter: 8 (over z, x), tensor: 2 (over core).
Axes of the slice: x: 2, y: 2, z: 4, core: 2. Of those that a mesh axis runs over, the one named last changes fastest.
Arguments:
- tokens: bfloat16 [4096, 8192], P(('groups', 'adapter'), 'tensor'), parts along dimension 0, may hold values from -6 to 6
- kv_weight: bfloat16 [8192, 1024], P(None, 'tensor'), may hold values from -0.0625 to 0.0625
- down_a: bfloat16 [32, 8192, 64], P(('groups', 'adapter')), parts along dimension 0, may hold values from -0.0625 to 0.0625
- up_weight: bfloat16 [32, 64, 1024], P(('groups', 'adapter')), parts along dimension 0, may hold values from -0.75 to 0.75
- adapter_ids: int32 [112], P(('groups', 'adapter')), parts along dimension 0, may hold values from 0 to 15, as said below
- lengths: int32 [112], P(('groups', 'adapter')), parts along dimension 0, may hold values from 1 to 73, as said below
Outputs:
- values_out: bfloat16 [4096, 1024], P(('groups', 'adapter'), 'tensor'), parts along dimension 0
There are 2 independent parts, one for each index of `groups`. A program takes and returns all parts, laid end to end along the dimension named above; an argument that names none is the same for every part. Nothing has to cross between parts.
Inputs may be any that keep to these rules, and one draw needn't show every extreme that they name: The 7 requests of one index of adapter (consecutive entries) have prompt lengths summing to 256; exactly one of them has length 73, every other one at most 31, and one of those exactly 31. `adapter_ids`: the owner of adapter a is a // 2. The 7 requests of one index of adapter name adapters of 7 different owners. In each part the request of length 73 names the same owner on every index of adapter.
All inputs are finite; a program needn't handle non-finite values.
Results may differ from a plain program's by a relative error of at most 0.0055.
Values may be sent and summed in bfloat16 or wider, within the bound.
No kernel may reach another device: no remote copies, remote signals or barrier semaphores. Data moves between devices by JAX's collectives and lax.ppermute only.
A program may use at most 128 MiB of HBM per device.

v0:
```python
import jax
import jax.numpy as jnp
from jax import lax
from jax.sharding import PartitionSpec as P

adapter_scale = 2.0


def shards(tokens, kv_weight, down_a, up_weight, adapter_ids, lengths):
    owner_count = lax.axis_size("adapter")
    core_count = lax.axis_size("tensor")
    core_index = lax.axis_index("tensor")
    adapt_dev = down_a.shape[0]
    tok_rows = tokens.shape[0]
    req_dev = lengths.shape[0]
    most_rows = 2 * tok_rows // req_dev
    head_cols = kv_weight.shape[1]
    gathered = lax.all_gather(tokens, "tensor", axis=1, tiled=True)
    base_output = jnp.dot(gathered, kv_weight, preferred_element_type=jnp.float32)
    ends = jnp.cumsum(lengths)
    starts = ends - lengths
    owners = adapter_ids // adapt_dev
    local_idx = adapter_ids % adapt_dev
    request_no = jnp.arange(req_dev, dtype=jnp.int32)
    taken = request_no % core_count == core_index
    matches = (owners[None, :] == jnp.arange(owner_count, dtype=jnp.int32)[:, None]) & taken[
        None, :
    ]
    matched = matches.astype(jnp.int32)
    first_row = jnp.sum(matched * starts[None, :], axis=1)
    owned_len = jnp.sum(matched * lengths[None, :], axis=1)
    owned_idx = jnp.sum(matched * local_idx[None, :], axis=1)
    slot_pos = jnp.arange(most_rows, dtype=jnp.int32)
    usable = slot_pos[None, :] < owned_len[:, None]
    row_index = jnp.where(usable, first_row[:, None] + slot_pos[None, :], 0)
    picked = jnp.take(gathered, row_index.reshape(-1), axis=0).reshape(
        owner_count, most_rows, gathered.shape[1]
    )
    send_rows = jnp.where(usable[:, :, None], picked, jnp.zeros((), gathered.dtype))
    send_ids = jnp.broadcast_to(owned_idx[:, None], (owner_count, most_rows))
    sent_rows = lax.all_to_all(send_rows, "adapter", split_axis=0, concat_axis=0, tiled=True)
    slot_ids = lax.all_to_all(send_ids, "adapter", split_axis=0, concat_axis=0, tiled=True)
    block_list, token_count, width = sent_rows.shape
    block_id = slot_ids[:, 0]
    order = jnp.argsort(block_id, stable=True)
    inverse_order = jnp.argsort(order, stable=True)
    sorted_rows = jnp.take(sent_rows, order, axis=0).reshape(block_list * token_count, width)
    group_lengths = jnp.sum(
        (block_id[:, None] == jnp.arange(adapt_dev, dtype=jnp.int32)[None, :]).astype(jnp.int32),
        axis=0,
    )
    group_lengths = group_lengths * token_count
    low_rank = lax.ragged_dot(
        sorted_rows, down_a, group_lengths, preferred_element_type=jnp.float32
    )
    rounded_length = low_rank.astype(jnp.bfloat16)
    adapter_delta = lax.ragged_dot(
        rounded_length, up_weight, group_lengths, preferred_element_type=jnp.float32
    )
    adapter_delta = adapter_delta.astype(jnp.bfloat16).reshape(
        block_list, token_count, up_weight.shape[2]
    )
    adapter_delta = jnp.take(adapter_delta, inverse_order, axis=0)
    returned_rows = lax.all_to_all(
        adapter_delta, "adapter", split_axis=0, concat_axis=0, tiled=True
    )
    row_no = jnp.arange(tok_rows, dtype=jnp.int32)
    request_of = jnp.sum((ends[None, :] <= row_no[:, None]).astype(jnp.int32), axis=1)
    row_owner = owners[request_of]
    row_slot = jnp.minimum(row_no - starts[request_of], most_rows - 1)
    flat_back = returned_rows.reshape(owner_count * most_rows, returned_rows.shape[2])
    delta_rows = jnp.take(flat_back, row_owner * most_rows + row_slot, axis=0).astype(jnp.float32)
    in_hot = jnp.zeros((tok_rows,), bool)
    frequent_share = jnp.zeros((tok_rows, head_cols), jnp.float32)
    is_mine = (request_of % core_count == core_index) & jnp.logical_not(in_hot)
    contrib = jnp.where(is_mine[:, None], delta_rows, 0.0)
    shared_rows = lax.psum_scatter(
        contrib.astype(jnp.bfloat16), "tensor", scatter_dimension=1, tiled=True
    ).astype(jnp.float32)
    return (base_output + adapter_scale * (shared_rows + frequent_share)).astype(jnp.bfloat16)


def solution(mesh):
    placed = (
        P(("groups", "adapter"), "tensor"),
        P(None, "tensor"),
        P(("groups", "adapter"), None, None),
        P(("groups", "adapter"), None, None),
        P(("groups", "adapter")),
        P(("groups", "adapter")),
    )
    return jax.shard_map(
        shards,
        mesh=mesh,
        in_specs=placed,
        out_specs=P(("groups", "adapter"), "tensor"),
        check_vma=False,
    )
```

profile of v0, /device:TPU:0, one launch (start us, length us, event | category | flops | bytes accessed | tf_op | source)
XLA Modules:
  0.0 490.2 jit_solution(10446390105890897399)
XLA Ops:
  6.5 0.7 all-gather.2.cloned.1.call-update
  7.3 0.8 reduce-window.8
  8.1 0.7 and_select_fusion
  8.8 0.8 select_reduce_fusion.1
  9.6 0.7 broadcast_in_dim.103
  10.3 7.3 %all-to-all-start = ((s32[8,1,73]{2,1,0:T(1,128)}), s32[8,1,73]{2,1,0:T(1,128)S(1)}, u32[]{:S(2)}, u32[]{:S(2)}) async-start(s32[8,1,73]{2,1,0:T(1,128)} %broadcast_in_dim.103), calls=%async_computation | async-start | bytes 8192 | tf_op jit(solution)/shard_map/all_to_all | solution.py:42
  17.8 7.6 %all-gather.2.cloned.1.call-done = bf16[256,8192]{1,0:T(8,128)(2,1)} async-done(((bf16[256,4096]{1,0:T(8,128)(2,1)}), bf16[256,8192]{1,0:T(8,128)(2,1)}) %all-gather.2.cloned.1.call-update) | async-done | bytes 4194320 | tf_op jit(solution)/shard_map/all_gather | solution.py:18
  25.3 23.8 %gather_fusion = bf16[584,8192]{1,0:T(8,128)(2,1)} fusion(bf16[256,8192]{1,0:T(8,128)(2,1)} %all-gather.2.cloned.1.call-done, s32[1024]{0:T(1024)S(1)} %pad_clamp_fusion.3), kind=kCustom, calls=%fused_computation | custom fusion | bytes 19138848 | tf_op jit(solution)/shard_map/jit(_take)/gather | solution.py:36
  49.2 11.0 %gather.31 = bf16[8,73,8192]{2,1,0:T(8,128)(2,1)} reshape(bf16[584,8192]{1,0:T(8,128)(2,1)} %gather_fusion) | data formatting | bytes 19136512 | tf_op jit(solution)/shard_map/jit(_take)/gather | solution.py:36
  60.2 10.2 %select_select_fusion = bf16[8,73,8192]{2,1,0:T(8,128)(2,1)} fusion(bf16[8,73,8192]{2,1,0:T(8,128)(2,1)} %gather.31, pred[8,73]{1,0:T(8,128)(4,1)S(1)} %get-tuple-element.37, pred[8,73]{1,0:T(8,128)(4,1)S(1)} %get-tuple-element.36), kind=kLoop, calls=%fused_computation.4 | loop fusion | flops 9568256 | bytes 19137680 | tf_op jit(solution)/shard_map/jit(_where)/select_n | solution.py:39
  70.4 5.9 %all-to-all-start.1 = ((bf16[8,73,8192]{2,1,0:T(8,128)(2,1)}), bf16[8,73,8192]{2,1,0:T(8,128)(2,1)}, u32[]{:S(2)}, u32[]{:S(2)}) async-start(bf16[8,73,8192]{2,1,0:T(8,128)(2,1)} %select_select_fusion), calls=%async_computation.1 | async-start | bytes 20971520 | tf_op jit(solution)/shard_map/all_to_all | solution.py:41
  76.3 3.2 copy.11
  79.6 1.0 sort.31
  81.4 1.9 ragged-dot-metadata
  83.3 1.0 sort.32
  84.3 220.5 %all-to-all-done.1 = bf16[8,73,8192]{2,1,0:T(8,128)(2,1)} async-done(((bf16[8,73,8192]{2,1,0:T(8,128)(2,1)}), bf16[8,73,8192]{2,1,0:T(8,128)(2,1)}, u32[]{:S(2)}, u32[]{:S(2)}) %all-to-all-start.1) | async-done | bytes 9568288 | tf_op jit(solution)/shard_map/all_to_all | solution.py:41
  304.9 9.5 %gather_fusion.1 = bf16[8,73,8192]{2,1,0:T(8,128)(2,1)} fusion(bf16[8,73,8192]{2,1,0:T(8,128)(2,1)} %all-to-all-done.1, s32[1024]{0:T(1024)S(1)} %pad_clamp_fusion.2), kind=kCustom, calls=%fused_computation.1 | custom fusion | bytes 19136544 | tf_op jit(solution)/shard_map/jit(_take)/gather | solution.py:47
  314.3 11.1 %gather.33 = bf16[584,8192]{1,0:T(8,128)(2,1)} reshape(bf16[8,73,8192]{2,1,0:T(8,128)(2,1)} %gather_fusion.1) | data formatting | bytes 19136512 | tf_op jit(solution)/shard_map/jit(_take)/gather | solution.py:47
  325.4 8.4 %broadcast_select_fusion = bf16[584,8192]{1,0:T(8,128)(2,1)} fusion(bf16[584,8192]{1,0:T(8,128)(2,1)} %gather.33, pred[584]{0:T(1024)(128)(4,1)S(1)} %broadcast_in_dim.106), kind=kLoop, calls=%fused_computation.5 | loop fusion | flops 4784128 | bytes 19137096 | tf_op jit(solution)/shard_map/jit(_take)/select_n | solution.py:47
  333.8 53.2 %ragged-dot-none.1 = f32[584,64]{1,0:T(8,128)} custom-call(s32[1]{0:T(128)} %get-tuple-element.9, s32[3]{0:T(128)} %get-tuple-element.10, s32[74]{0:T(128)} %get-tuple-element.11, s32[74]{0:T(128)} %get-tuple-element.12, s32[1]{0:T(128)} %get-tuple-element.9, bf16[584,8192]{1,0:T(8,128)(2,1)} %broadcast_select_fusion, bf16[2,8192,64]{2,1,0:T(8,128)(2,1)} %copy.11), custom_call_target="tpu_custom_call" | custom-call | flops 612368384 | bytes 11814920 | tf_op jit(solution)/shard_map/ragged_dot_general/ragged-dot-none
  387.0 1.6 convert_element_type.27
  388.7 38.0 %ragged-dot-none = f32[584,1024]{1,0:T(8,128)} custom-call(s32[1]{0:T(128)} %get-tuple-element.9, s32[3]{0:T(128)} %get-tuple-element.10, s32[74]{0:T(128)} %get-tuple-element.11, s32[74]{0:T(128)} %get-tuple-element.12, s32[1]{0:T(128)} %get-tuple-element.9, bf16[584,64]{1,0:T(8,128)(2,1)} %convert_element_type.27, bf16[2,64,1024]{2,1,0:T(8,128)(2,1)} %param.9), custom_call_target="tpu_custom_call" | custom-call | flops 76546048 | bytes 2728968 | tf_op jit(solution)/shard_map/ragged_dot_general/ragged-dot-none
  426.7 1.9 convert_element_type.28
  429.6 1.3 broadcast_select_fusion.1
  430.8 3.6 all-to-all-start.2
  435.9 4.4 compare_select_fusion.7
  440.4 4.3 compare_select_fusion.2
  444.8 21.3 %all-to-all-done.2 = bf16[8,73,1024]{2,1,0:T(8,128)(2,1)S(1)} async-done(((bf16[8,73,1024]{2,1,0:T(8,128)(2,1)}), bf16[8,73,1024]{2,1,0:T(8,128)(2,1)S(1)}, u32[]{:S(2)}, u32[]{:S(2)}) %all-to-all-start.2) | async-done | bytes 1196064 | tf_op jit(solution)/shard_map/all_to_all | solution.py:64
  466.4 1.2 gather_fusion.3
  467.6 1.0 select_convert_fusion
  468.6 7.2 %reduce-scatter.2.cloned.1.call-done = bf16[256,512]{1,0:T(8,128)(2,1)} async-done(((bf16[256,1024]{1,0:T(8,128)(2,1)}), bf16[256,512]{1,0:T(8,128)(2,1)}) %reduce-scatter.2.cloned.1.call-update) | async-done | bytes 262160 | tf_op jit(solution)/shard_map/reduce_scatter | solution.py:77
  475.8 7.6 %fusion = bf16[256,512]{1,0:T(8,128)(2,1)} fusion(bf16[256,8192]{1,0:T(8,128)(2,1)} %all-gather.2.cloned.1.call-done, bf16[8192,512]{1,0:T(8,128)(2,1)} %param.7, bf16[256,512]{1,0:T(8,128)(2,1)} %reduce-scatter.2.cloned.1.call-done), kind=kOutput, calls=%fused_computation.8 | convolution fusion | flops 2148007936 | bytes 13107200 | tf_op jit(solution)/shard_map/dot_general | solution.py:19
  (35 shorter events, 4.1 us)
Async XLA Ops:
  6.5 18.8 %all-gather.2.cloned.1.call-start = ((), (), s32[]{:S(2)}) async-start(), calls=%async_computation.4 | async-start | bytes 6291456 | tf_op jit(solution)/shard_map/all_gather | solution.py:18
  10.3 60.1 %all-to-all-start = ((s32[8,1,73]{2,1,0:T(1,128)}), s32[8,1,73]{2,1,0:T(1,128)S(1)}, u32[]{:S(2)}, u32[]{:S(2)}) async-start(s32[8,1,73]{2,1,0:T(1,128)} %broadcast_in_dim.103), calls=%async_computation | async-start | bytes 8192 | tf_op jit(solution)/shard_map/all_to_all | solution.py:42
  70.4 5.9 %copy-start = (bf16[2,8192,64]{1,2,0:T(8,128)(2,1)S(1)}, bf16[2,8192,64]{1,2,0:T(8,128)(2,1)}, u32[]{:S(2)}) copy-start(bf16[2,8192,64]{1,2,0:T(8,128)(2,1)} %param.8) | copy-start | bytes 6291460
  70.4 234.5 %all-to-all-start.1 = ((bf16[8,73,8192]{2,1,0:T(8,128)(2,1)}), bf16[8,73,8192]{2,1,0:T(8,128)(2,1)}, u32[]{:S(2)}, u32[]{:S(2)}) async-start(bf16[8,73,8192]{2,1,0:T(8,128)(2,1)} %select_select_fusion), calls=%async_computation.1 | async-start | bytes 20971520 | tf_op jit(solution)/shard_map/all_to_all | solution.py:41
  430.8 35.2 %all-to-all-start.2 = ((bf16[8,73,1024]{2,1,0:T(8,128)(2,1)}), bf16[8,73,1024]{2,1,0:T(8,128)(2,1)S(1)}, u32[]{:S(2)}, u32[]{:S(2)}) async-start(bf16[8,73,1024]{2,1,0:T(8,128)(2,1)} %broadcast_select_fusion.1), calls=%async_computation.2 | async-start | bytes 2621440 | tf_op jit(solution)/shard_map/all_to_all | solution.py:64
  434.5 41.3 %reduce-scatter.2.cloned.1.call-start = ((), (), s32[]{:S(2)}) async-start(), calls=%async_computation.5 | async-start | bytes 786432 | tf_op jit(solution)/shard_map/reduce_scatter | solution.py:77
Sparse Core Ops, SparseCore 0:
  8.9 16.3 all-gather.1
  468.8 6.9 reduce-scatter.1
where the time goes:
time: 494 us; the launch traced here: 490 us
  waiting for transfers between devices  257 us (52%)
  Pallas kernels  93.1 us (19%)
  local copies, waits for them, and re-layouts  63.6 us (13%)
  other arithmetic  38.3 us (8%)
  starting transfers between devices  16.8 us (3%)
  between operations  13.6 us (3%)
  matrix products  7.6 us (2%)
    all_to_all x1, waiting for transfers between devices, shards(): lax.all_to_all(send_rows, 'adapter', split_axis=0, concat_axis=0, tiled=T...  221 us
    another operation x2, Pallas kernels  91.3 us
    gather x2, local copies, waits for them, and re-layouts, shards(): jnp.take(gathered, row_index.reshape(-1), axis=0)  34.8 us
    all_to_all x1, waiting for transfers between devices, shards(): lax.all_to_all(adapter_delta, 'adapter', split_axis=0, concat_axis=0, til...  21.3 us
    gather x2, local copies, waits for them, and re-layouts, shards(): jnp.take(sent_rows, order, axis=0).reshape(block_list * token_count, width)  20.6 us
    select_n x1, other arithmetic, shards(): jnp.where(usable[:, :, None], picked, jnp.zeros((), gathered.dtype))  10.2 us
  transfers between devices with their start and end apart: 5, of which 4 were waited for; matrix products, arithmetic and copies ran while one was open for 13% of the time, Pallas kernels for 0%

commit v1 on v0

v1 whole, which is shorter than its diff:
```python
import jax
import jax.numpy as jnp
from jax import lax
from jax.sharding import PartitionSpec as P

adapter_scale = 2.0
bf16 = jnp.bfloat16
f32 = jnp.float32
swap_bit = 2
chunk_count = 4


def dot(left, right, contract):
    return lax.dot_general(left, right, ((contract[:1], contract[1:]), ((), ())), preferred_element_type=f32)


def shards(tokens, kv_weight, down_a, up_weight, adapter_ids, lengths):
    owners = lax.axis_size("adapter")
    me = lax.axis_index("adapter")
    core = lax.axis_index("tensor")
    adapt_dev, width, rank = down_a.shape
    both = adapt_dev * rank
    rows, half = tokens.shape
    heads = kv_weight.shape[1]
    req_dev = lengths.shape[0]
    most = 2 * rows // req_dev
    cold = -(-(rows - most) // (req_dev - 1))
    slots = min(rows, most + (owners // 2 - 1) * cold)
    slots = -(-slots // 16) * 16

    def flip(x, bit):
        return lax.ppermute(x, "adapter", [(j, j ^ bit) for j in range(owners)])

    def other_core(x):
        return lax.ppermute(x, "tensor", [(0, 1), (1, 0)])

    down_t = jnp.transpose(down_a, (0, 2, 1)).reshape(both, width)
    step = half // chunk_count
    pieces = {0: [lax.dynamic_slice(down_t, (0, core * half + c * step), (both, step)) for c in range(chunk_count)]}
    up_mine = lax.dynamic_slice(up_weight.reshape(both, -1), (0, core * heads), (both, heads))
    pieces[0][0] = jnp.concatenate([pieces[0][0], up_mine], axis=1)

    q = jnp.arange(req_dev, dtype=jnp.int32)
    upto = q[None, :] <= q[:, None]
    ends = jnp.sum(jnp.where(upto, lengths[None, :], 0), axis=1)
    starts = ends - lengths
    away_q = (((adapter_ids // adapt_dev) ^ me) & swap_bit) != 0
    away_len = jnp.where(away_q, lengths, 0)
    offset = jnp.sum(jnp.where(upto, away_len[None, :], 0), axis=1) - away_len
    r = jnp.arange(rows, dtype=jnp.int32)
    inside = (starts[None, :] <= r[:, None]) & (r[:, None] < ends[None, :])
    row_adapter = jnp.sum(jnp.where(inside, adapter_ids[None, :], 0), axis=1)
    place = jnp.sum(jnp.where(inside & away_q[None, :], (offset - starts + 1)[None, :] + r[:, None], 0), axis=1) - 1
    s = jnp.arange(slots, dtype=jnp.int32)
    hit = s[:, None] == place[None, :]
    pick = hit.astype(bf16)
    sent = dot(pick, tokens, (1, 0)).astype(bf16)
    sent_adapter = jnp.sum(jnp.where(hit, row_adapter[None, :], 0), axis=1)

    got_adapter = flip(sent_adapter, swap_bit)
    got = flip(sent, swap_bit)
    tokens_other = other_core(tokens)

    bits = [1 << b for b in range(owners.bit_length() - 1)]
    for bit in [b for b in bits if b > swap_bit] + [b for b in bits if b < swap_bit]:
        for m in list(pieces):
            pieces[m | bit] = [flip(c, bit) for c in pieces[m]]

    base = dot(tokens, lax.dynamic_slice(kv_weight, (core * half, 0), (half, heads)), (1, 0))
    base = base + dot(tokens_other, lax.dynamic_slice(kv_weight, ((1 - core) * half, 0), (half, heads)), (1, 0))

    def low_rank_part(x, which):
        total = jnp.zeros((x.shape[0], both), f32)
        for m, chunks in pieces.items():
            term = sum(dot(x[:, c * step : (c + 1) * step], chunks[c][:, :step], (1, 1)) for c in range(chunk_count))
            total = total + jnp.where((which // adapt_dev == (me ^ m))[:, None], term, 0.0)
        lane = jnp.arange(both, dtype=jnp.int32) // rank
        return jnp.where((which % adapt_dev)[:, None] == lane[None, :], total, 0.0)

    up_all = jnp.concatenate([chunks[0][:, step:] for chunks in pieces.values()], axis=0)

    def delta_of(low, which):
        spread = jnp.concatenate(
            [jnp.where((which // adapt_dev == (me ^ m))[:, None], low, jnp.zeros((), bf16)) for m in pieces], axis=1
        )
        return dot(spread, up_all, (1, 0)).astype(bf16)

    part_got = low_rank_part(got, got_adapter)
    part_own = low_rank_part(tokens, row_adapter)
    low_got = (part_got + other_core(part_got)).astype(bf16)
    low_own = (part_own + other_core(part_own)).astype(bf16)
    delta_got = delta_of(low_got, got_adapter)
    back = flip(delta_got, swap_bit)
    delta_own = delta_of(low_own, row_adapter)
    delta = delta_own.astype(f32) + dot(pick, back, (0, 0))
    return (base + adapter_scale * delta).astype(bf16)


def solution(mesh):
    placed = (
        P(("groups", "adapter"), "tensor"),
        P(None, "tensor"),
        P(("groups", "adapter"), None, None),
        P(("groups", "adapter"), None, None),
        P(("groups", "adapter")),
        P(("groups", "adapter")),
    )
    return jax.shard_map(
        shards,
        mesh=mesh,
        in_specs=placed,
        out_specs=P(("groups", "adapter"), "tensor"),
        check_vma=False,
    )
```

time: 494 us -> 106 us (0.21)
  waiting for transfers between devices: 257 us -> 50.4 us
  Pallas kernels: 93.1 us -> 0 us
  local copies, waits for them, and re-layouts: 63.6 us -> 2.36 us
  other arithmetic: 38.3 us -> 4.42 us
  matrix products: 7.6 us -> 27.1 us
  between operations: 13.6 us -> 0.52 us
    all_to_all x3 -> x0, waiting for transfers between devices: 242 us -> none  [the longest x1 221 us: shards(): lax.all_to_all(send_rows, 'adapter', split_axis=0, concat_axis=0, tiled=T...]
    another operation x2 -> x0, Pallas kernels: 91.3 us -> none
    gather x8 -> x0, local copies, waits for them, and re-layouts: 58.6 us -> none  [the longest x2 34.8 us: shards(): jnp.take(gathered, row_index.reshape(-1), axis=0)]
    ppermute x0 -> x18, waiting for transfers between devices: none -> 50.4 us  [the longest x15 48.9 us: flip(): return lax.ppermute(x, 'adapter', [(j, j ^ bit) for j in range(owners)])]
    select_n x9 -> x8, other arithmetic: 25 us -> 2.02 us  [the longest x2 1.22 us: low_rank_part(): return jnp.where((which % adapt_dev)[:, None] == lane[None, :], total, 0.0)]
    ppermute x0 -> x18, starting transfers between devices: none -> 20.8 us  [the longest x15 20.6 us: flip(): return lax.ppermute(x, 'adapter', [(j, j ^ bit) for j in range(owners)])]
    dot_general x1 -> x38, matrix products: 7.6 us -> 27.1 us  [dot(): lax.dot_general(left, right, ((contract[:1], contract[1:]), ((), ())), pr...]
    all_to_all x3 -> x0, starting transfers between devices: 16.8 us -> none  [the longest x1 7.25 us: shards(): lax.all_to_all(send_ids, 'adapter', split_axis=0, concat_axis=0, tiled=True)]
  transfers between devices with their start and end apart: 5 -> 18, of which waited for: 4 -> 12; matrix products, arithmetic and copies ran while one was open for 13% -> 30% of each run, Pallas kernels for 0% -> 0%
where the time goes in v1:
time: 106 us
  waiting for transfers between devices  50.4 us (48%)
  matrix products  27.1 us (26%)
  starting transfers between devices  20.8 us (20%)
  other arithmetic  4.42 us (4%)
  local copies, waits for them, and re-layouts  2.36 us (2%)
    ppermute x15, waiting for transfers between devices, flip(): return lax.ppermute(x, 'adapter', [(j, j ^ bit) for j in range(owners)])  48.9 us
    dot_general x38, matrix products, dot(): lax.dot_general(left, right, ((contract[:1], contract[1:]), ((), ())), pr...  27.1 us
    ppermute x15, starting transfers between devices, flip(): return lax.ppermute(x, 'adapter', [(j, j ^ bit) for j in range(owners)])  20.6 us
  transfers between devices with their start and end apart: 18, of which 12 were waited for; matrix products, arithmetic and copies ran while one was open for 30% of the time, Pallas kernels for 0%

profile of v1, /device:TPU:0, one launch (start us, length us, event | category | flops | bytes accessed | tf_op | source)
XLA Modules:
  0.0 105.7 jit_solution(10660037810448586050)
XLA Ops:
  0.0 1.4 %constant_dynamic-slice_fusion.1 = (bf16[128,1024]{1,0:T(8,128)(2,1)S(1)}, bf16[128,1024]{1,0:T(8,128)(2,1)S(1)}, bf16[128,1024]{1,0:T(8,128)(2,1)S(1)}, bf16[128,1024]{1,0:T(8,128)(2,1)S(1)}) fusion(bf16[128,8192]{1,0:T(8,128)(2,1)} %bitcast.41, s32[]{:T(128)S(6)} %select_n.194, s32[]{:T(128)S(6)} %select_n.193, s32[]{:T(128)S(6)} %select_n.192, ...), kind=kLoop, calls=%fused_computation.160 | loop fusion | bytes 2097168 | tf_op jit(solution)/shard_map/dynamic_slice | solution.py:39
  1.4 4.1 %collective-permute-start.4 = (bf16[128,1024]{1,0:T(8,128)(2,1)S(1)}, bf16[128,1024]{1,0:T(8,128)(2,1)}, u32[]{:S(2)}, u32[]{:S(2)}) collective-permute-start(bf16[128,1024]{1,0:T(8,128)(2,1)S(1)} %get-tuple-element.19), channel_id=1, source_target_pairs={{0,8},{2,10},{4,12},{6,14},{8,0},{10,2},{12,4},{14,6},{1,9},{3,11}... | collective-permute-start | bytes 786440 | tf_op jit(solution)/shard_map/ppermute | solution.py:32
  5.6 1.5 %collective-permute-start.8 = (bf16[128,1024]{1,0:T(8,128)(2,1)S(1)}, bf16[128,1024]{1,0:T(8,128)(2,1)}, u32[]{:S(2)}, u32[]{:S(2)}) collective-permute-start(bf16[128,1024]{1,0:T(8,128)(2,1)S(1)} %get-tuple-element.19), channel_id=1, source_target_pairs={{0,2},{2,0},{4,6},{6,4},{8,10},{10,8},{12,14},{14,12},{1,3},{3,1},... | collective-permute-start | bytes 786440 | tf_op jit(solution)/shard_map/ppermute | solution.py:32
  7.4 2.6 %collective-permute-start.2 = (bf16[128,1024]{1,0:T(8,128)(2,1)S(1)}, bf16[128,1024]{1,0:T(8,128)(2,1)}, u32[]{:S(2)}, u32[]{:S(2)}) collective-permute-start(bf16[128,1024]{1,0:T(8,128)(2,1)S(1)} %get-tuple-element.21), channel_id=1, source_target_pairs={{0,8},{2,10},{4,12},{6,14},{8,0},{10,2},{12,4},{14,6},{1,9},{3,11}... | collective-permute-start | bytes 786440 | tf_op jit(solution)/shard_map/ppermute | solution.py:32
  10.9 1.6 %collective-permute-start.14 = (s32[176]{0:T(256)}, s32[176]{0:T(256)}, u32[]{:S(2)}, u32[]{:S(2)}) collective-permute-start(s32[176]{0:T(256)} %select_reduce_fusion), channel_id=1, source_target_pairs={{0,4},{2,6},{4,0},{6,2},{8,12},{10,14},{12,8},{14,10},{1,5},{3,7},... | collective-permute-start | bytes 2120 | tf_op jit(solution)/shard_map/ppermute | solution.py:32
  13.1 1.7 %convolution_convert_fusion = bf16[176,4096]{1,0:T(8,128)(2,1)} fusion(bf16[256,4096]{1,0:T(8,128)(2,1)S(1)} %copy-done.1, s32[256]{0:T(256)S(1)} %broadcast_add_fusion), kind=kOutput, calls=%fused_computation | convolution fusion | flops 369864704 | bytes 3539968 | tf_op jit(solution)/shard_map/dot_general | solution.py:14
  16.5 1.2 %convolution_add_fusion.6 = f32[128,256]{1,0:T(8,128)S(1)} fusion(f32[128,256]{1,0:T(8,128)} %fusion.69, bf16[128,1024]{1,0:T(8,128)(2,1)S(1)} %get-tuple-element.21, bf16[256,4096]{1,0:T(8,128)(2,1)S(1)} %copy-done.1), kind=kOutput, calls=%fused_computation.23 | convolution fusion | flops 67141632 | bytes 1048576 | tf_op jit(solution)/shard_map/dot_general | solution.py:14
  18.1 4.3 %fusion.2 = f32[512,256]{1,0:T(8,128)} fusion(bf16[256,4096]{1,0:T(8,128)(2,1)S(1)} %copy-done.1, bf16[8192,512]{1,0:T(8,128)(2,1)} %param.7, s32[]{:T(128)S(6)} %select_n.185), kind=kOutput, calls=%fused_computation.3 | convolution fusion | flops 1073741824 | bytes 6815748 | tf_op jit(solution)/shard_map/dot_general | solution.py:14
  25.1 4.6 %collective-permute-done.4 = bf16[128,1024]{1,0:T(8,128)(2,1)} collective-permute-done((bf16[128,1024]{1,0:T(8,128)(2,1)S(1)}, bf16[128,1024]{1,0:T(8,128)(2,1)}, u32[]{:S(2)}, u32[]{:S(2)}) %collective-permute-start.4) | collective-permute-done | bytes 262176 | tf_op jit(solution)/shard_map/ppermute | solution.py:32
  29.6 1.8 %collective-permute-start.6 = (bf16[128,1024]{1,0:T(8,128)(2,1)S(1)}, bf16[128,1024]{1,0:T(8,128)(2,1)S(1)}, u32[]{:S(2)}, u32[]{:S(2)}) collective-permute-start(bf16[128,1024]{1,0:T(8,128)(2,1)S(1)} %get-tuple-element.21), channel_id=1, source_target_pairs={{0,2},{2,0},{4,6},{6,4},{8,10},{10,8},{12,14},{14,12},{1,3},{3,1},... | collective-permute-start | bytes 786440 | tf_op jit(solution)/shard_map/ppermute | solution.py:32
  31.5 1.3 %fusion.49 = f32[128,256]{1,0:T(8,128)S(1)} fusion(bf16[128,1024]{1,0:T(8,128)(2,1)} %collective-permute-done.4, bf16[256,4096]{1,0:T(8,128)(2,1)S(1)} %copy-done.1), kind=kOutput, calls=%fused_computation.61 | convolution fusion | flops 67108864 | bytes 917504 | tf_op jit(solution)/shard_map/dot_general | solution.py:14
  32.8 2.5 %collective-permute-done.3 = bf16[128,1024]{1,0:T(8,128)(2,1)} collective-permute-done((bf16[128,1024]{1,0:T(8,128)(2,1)S(1)}, bf16[128,1024]{1,0:T(8,128)(2,1)}, u32[]{:S(2)}, u32[]{:S(2)}) %collective-permute-start.3) | collective-permute-done | bytes 262176 | tf_op jit(solution)/shard_map/ppermute | solution.py:32
  35.3 1.3 %fusion.56 = f32[128,256]{1,0:T(8,128)S(1)} fusion(bf16[128,1024]{1,0:T(8,128)(2,1)} %collective-permute-done.3, bf16[256,4096]{1,0:T(8,128)(2,1)S(1)} %copy-done.1), kind=kOutput, calls=%fused_computation.68 | convolution fusion | flops 67108864 | bytes 917504 | tf_op jit(solution)/shard_map/dot_general | solution.py:14
  36.5 12.8 %collective-permute-done.2 = bf16[128,1024]{1,0:T(8,128)(2,1)} collective-permute-done((bf16[128,1024]{1,0:T(8,128)(2,1)S(1)}, bf16[128,1024]{1,0:T(8,128)(2,1)}, u32[]{:S(2)}, u32[]{:S(2)}) %collective-permute-start.2) | collective-permute-done | bytes 262176 | tf_op jit(solution)/shard_map/ppermute | solution.py:32
  49.3 1.8 %collective-permute-start.5 = (bf16[128,1536]{1,0:T(8,128)(2,1)}, bf16[128,1536]{1,0:T(8,128)(2,1)S(1)}, u32[]{:S(2)}, u32[]{:S(2)}) collective-permute-start(bf16[128,1536]{1,0:T(8,128)(2,1)} %pad_maximum_fusion.1), channel_id=1, source_target_pairs={{0,2},{2,0},{4,6},{6,4},{8,10},{10,8},{12,14},{14,12},{1,3},{3,1},... | collective-permute-start | bytes 1179656 | tf_op jit(solution)/shard_map/ppermute | solution.py:32
  51.1 1.3 %fusion.63 = f32[128,256]{1,0:T(8,128)S(1)} fusion(bf16[128,1024]{1,0:T(8,128)(2,1)} %collective-permute-done.2, bf16[256,4096]{1,0:T(8,128)(2,1)S(1)} %copy-done.1), kind=kOutput, calls=%fused_computation.75 | convolution fusion | flops 67108864 | bytes 917504 | tf_op jit(solution)/shard_map/dot_general | solution.py:14
  52.5 1.3 %fusion.47 = f32[128,256]{1,0:T(8,128)S(1)} fusion(bf16[128,1024]{1,0:T(8,128)(2,1)} %collective-permute-done.8, bf16[256,4096]{1,0:T(8,128)(2,1)S(1)} %copy-done.1), kind=kOutput, calls=%fused_computation.59 | convolution fusion | flops 67108864 | bytes 917504 | tf_op jit(solution)/shard_map/dot_general | solution.py:14
  54.8 2.0 %collective-permute-done.1 = bf16[128,1536]{1,0:T(8,128)(2,1)S(1)} collective-permute-done((bf16[128,1536]{1,0:T(8,128)(2,1)}, bf16[128,1536]{1,0:T(8,128)(2,1)S(1)}, u32[]{:S(2)}, u32[]{:S(2)}) %collective-permute-start.1) | collective-permute-done | bytes 393248 | tf_op jit(solution)/shard_map/ppermute | solution.py:32
  56.8 1.6 %collective-permute-start.11 = (bf16[128,1024]{1,0:T(8,128)(2,1)}, bf16[128,1024]{1,0:T(8,128)(2,1)S(1)}, u32[]{:S(2)}, u32[]{:S(2)}) collective-permute-start(bf16[128,1024]{1,0:T(8,128)(2,1)} %collective-permute-done.3), channel_id=1, source_target_pairs={{0,2},{2,0},{4,6},{6,4},{8,10},{10,8},{12,14},{14,12},{1,3},{3,1},... | collective-permute-start | bytes 786440 | tf_op jit(solution)/shard_map/ppermute | solution.py:32
  58.8 1.6 %collective-permute-start.10 = (bf16[128,1024]{1,0:T(8,128)(2,1)}, bf16[128,1024]{1,0:T(8,128)(2,1)S(1)}, u32[]{:S(2)}, u32[]{:S(2)}) collective-permute-start(bf16[128,1024]{1,0:T(8,128)(2,1)} %collective-permute-done.2), channel_id=1, source_target_pairs={{0,2},{2,0},{4,6},{6,4},{8,10},{10,8},{12,14},{14,12},{1,3},{3,1},... | collective-permute-start | bytes 786440 | tf_op jit(solution)/shard_map/ppermute | solution.py:32
  60.7 2.9 %collective-permute-done.12 = bf16[128,1024]{1,0:T(8,128)(2,1)S(1)} collective-permute-done((bf16[128,1024]{1,0:T(8,128)(2,1)}, bf16[128,1024]{1,0:T(8,128)(2,1)S(1)}, u32[]{:S(2)}, u32[]{:S(2)}) %collective-permute-start.12) | collective-permute-done | bytes 262176 | tf_op jit(solution)/shard_map/ppermute | solution.py:32
  63.6 2.4 %collective-permute-start.9 = (bf16[128,1536]{1,0:T(8,128)(2,1)S(1)}, bf16[128,1536]{1,0:T(8,128)(2,1)S(1)}, u32[]{:S(2)}, u32[]{:S(2)}) collective-permute-start(bf16[128,1536]{1,0:T(8,128)(2,1)S(1)} %collective-permute-done.1), channel_id=1, source_target_pairs={{0,2},{2,0},{4,6},{6,4},{8,10},{10,8},{12,14},{14,12},{1,3},{3,1},... | collective-permute-start | bytes 1179656 | tf_op jit(solution)/shard_map/ppermute | solution.py:32
  66.3 2.9 %collective-permute-done.11 = bf16[128,1024]{1,0:T(8,128)(2,1)S(1)} collective-permute-done((bf16[128,1024]{1,0:T(8,128)(2,1)}, bf16[128,1024]{1,0:T(8,128)(2,1)S(1)}, u32[]{:S(2)}, u32[]{:S(2)}) %collective-permute-start.11) | collective-permute-done | bytes 262176 | tf_op jit(solution)/shard_map/ppermute | solution.py:32
  69.5 5.3 %collective-permute-done.10 = bf16[128,1024]{1,0:T(8,128)(2,1)S(1)} collective-permute-done((bf16[128,1024]{1,0:T(8,128)(2,1)}, bf16[128,1024]{1,0:T(8,128)(2,1)S(1)}, u32[]{:S(2)}, u32[]{:S(2)}) %collective-permute-start.10) | collective-permute-done | bytes 262176 | tf_op jit(solution)/shard_map/ppermute | solution.py:32
  75.2 7.7 %collective-permute-done.9 = bf16[128,1536]{1,0:T(8,128)(2,1)S(1)} collective-permute-done((bf16[128,1536]{1,0:T(8,128)(2,1)S(1)}, bf16[128,1536]{1,0:T(8,128)(2,1)S(1)}, u32[]{:S(2)}, u32[]{:S(2)}) %collective-permute-start.9) | collective-permute-done | bytes 393248 | tf_op jit(solution)/shard_map/ppermute | solution.py:32
  84.6 3.2 %collective-permute-done.15 = bf16[176,4096]{1,0:T(8,128)(2,1)S(1)} collective-permute-done((bf16[176,4096]{1,0:T(8,128)(2,1)S(1)}, bf16[176,4096]{1,0:T(8,128)(2,1)S(1)}, u32[]{:S(2)}, u32[]{:S(2)}) %collective-permute-start.15) | collective-permute-done | bytes 1441824 | tf_op jit(solution)/shard_map/ppermute | solution.py:32
  87.8 1.2 %fusion.82 = f32[176,128]{1,0:T(8,128)S(1)} fusion(bf16[128,1024]{1,0:T(8,128)(2,1)} %collective-permute-done.4, bf16[176,4096]{1,0:T(8,128)(2,1)S(1)} %collective-permute-done.15), kind=kOutput, calls=%fused_computation.94 | convolution fusion | flops 46137344 | bytes 712704 | tf_op jit(solution)/shard_map/dot_general | solution.py:14
  89.0 1.2 %fusion.90 = f32[176,128]{1,0:T(8,128)S(1)} fusion(bf16[128,1024]{1,0:T(8,128)(2,1)} %collective-permute-done.3, bf16[176,4096]{1,0:T(8,128)(2,1)S(1)} %collective-permute-done.15), kind=kOutput, calls=%fused_computation.102 | convolution fusion | flops 46137344 | bytes 712704 | tf_op jit(solution)/shard_map/dot_general | solution.py:14
  90.3 1.2 %fusion.98 = f32[176,128]{1,0:T(8,128)S(1)} fusion(bf16[128,1024]{1,0:T(8,128)(2,1)} %collective-permute-done.2, bf16[176,4096]{1,0:T(8,128)(2,1)S(1)} %collective-permute-done.15), kind=kOutput, calls=%fused_computation.110 | convolution fusion | flops 46137344 | bytes 712704 | tf_op jit(solution)/shard_map/dot_general | solution.py:14
  91.5 1.2 %fusion.80 = f32[176,128]{1,0:T(8,128)S(1)} fusion(bf16[128,1024]{1,0:T(8,128)(2,1)} %collective-permute-done.8, bf16[176,4096]{1,0:T(8,128)(2,1)S(1)} %collective-permute-done.15), kind=kOutput, calls=%fused_computation.92 | convolution fusion | flops 46137344 | bytes 712704 | tf_op jit(solution)/shard_map/dot_general | solution.py:14
  98.2 1.3 %fusion.9 = f32[256,512]{0,1:T(8,128)S(1)} fusion(f32[512,256]{1,0:T(8,128)S(1)} %copy-done.10, bf16[256,4096]{1,0:T(8,128)(2,1)S(1)} %collective-permute-done, bf16[8192,512]{1,0:T(8,128)(2,1)S(1)} %bitcast.43, s32[]{:T(128)S(6)} %select_n.186), kind=kOutput, calls=%fused_computation.9 | convolution fusion | flops 1073872896 | bytes 7340036 | tf_op jit(solution)/shard_map/dot_general | solution.py:14
  99.6 5.0 %collective-permute-done.17 = bf16[176,512]{1,0:T(8,128)(2,1)S(1)} collective-permute-done((bf16[176,512]{1,0:T(8,128)(2,1)S(1)}, bf16[176,512]{1,0:T(8,128)(2,1)S(1)}, u32[]{:S(2)}, u32[]{:S(2)}) %collective-permute-start.17) | collective-permute-done | bytes 180256 | tf_op jit(solution)/shard_map/ppermute | solution.py:32
  (93 shorter events, 17.4 us)
Async XLA Ops:
  0.0 15.7 %copy-start = (bf16[2,64,1024]{2,1,0:T(8,128)(2,1)S(1)}, bf16[2,64,1024]{2,1,0:T(8,128)(2,1)}, u32[]{:S(2)}) copy-start(bf16[2,64,1024]{2,1,0:T(8,128)(2,1)} %param.9) | copy-start | bytes 786436
  0.0 10.0 %copy-start.9 = (s32[7]{0:T(128)S(1)}, s32[7]{0:T(128)}, u32[]{:S(2)}) copy-start(s32[7]{0:T(128)} %param.10) | copy-start | bytes 88
  0.0 10.0 %copy-start.6 = (s32[7]{0:T(128)S(1)}, s32[7]{0:T(128)}, u32[]{:S(2)}) copy-start(s32[7]{0:T(128)} %param.11) | copy-start | bytes 88
  0.0 13.1 %copy-start.1 = (bf16[256,4096]{1,0:T(8,128)(2,1)S(1)}, bf16[256,4096]{1,0:T(8,128)(2,1)}, u32[]{:S(2)}) copy-start(bf16[256,4096]{1,0:T(8,128)(2,1)} %param.6) | copy-start | bytes 6291460
  1.4 28.2 %collective-permute-start.4 = (bf16[128,1024]{1,0:T(8,128)(2,1)S(1)}, bf16[128,1024]{1,0:T(8,128)(2,1)}, u32[]{:S(2)}, u32[]{:S(2)}) collective-permute-start(bf16[128,1024]{1,0:T(8,128)(2,1)S(1)} %get-tuple-element.19), channel_id=1, source_target_pairs={{0,8},{2,10},{4,12},{6,14},{8,0},{10,2},{12,4},{14,6},{1,9},{3,11}... | collective-permute-start | bytes 786440 | tf_op jit(solution)/shard_map/ppermute | solution.py:32
  5.6 46.9 %collective-permute-start.8 = (bf16[128,1024]{1,0:T(8,128)(2,1)S(1)}, bf16[128,1024]{1,0:T(8,128)(2,1)}, u32[]{:S(2)}, u32[]{:S(2)}) collective-permute-start(bf16[128,1024]{1,0:T(8,128)(2,1)S(1)} %get-tuple-element.19), channel_id=1, source_target_pairs={{0,2},{2,0},{4,6},{6,4},{8,10},{10,8},{12,14},{14,12},{1,3},{3,1},... | collective-permute-start | bytes 786440 | tf_op jit(solution)/shard_map/ppermute | solution.py:32
  7.0 28.2 %collective-permute-start.3 = (bf16[128,1024]{1,0:T(8,128)(2,1)S(1)}, bf16[128,1024]{1,0:T(8,128)(2,1)}, u32[]{:S(2)}, u32[]{:S(2)}) collective-permute-start(bf16[128,1024]{1,0:T(8,128)(2,1)S(1)} %get-tuple-element.20), channel_id=1, source_target_pairs={{0,8},{2,10},{4,12},{6,14},{8,0},{10,2},{12,4},{14,6},{1,9},{3,11}... | collective-permute-start | bytes 786440 | tf_op jit(solution)/shard_map/ppermute | solution.py:32
  7.4 41.9 %collective-permute-start.2 = (bf16[128,1024]{1,0:T(8,128)(2,1)S(1)}, bf16[128,1024]{1,0:T(8,128)(2,1)}, u32[]{:S(2)}, u32[]{:S(2)}) collective-permute-start(bf16[128,1024]{1,0:T(8,128)(2,1)S(1)} %get-tuple-element.21), channel_id=1, source_target_pairs={{0,8},{2,10},{4,12},{6,14},{8,0},{10,2},{12,4},{14,6},{1,9},{3,11}... | collective-permute-start | bytes 786440 | tf_op jit(solution)/shard_map/ppermute | solution.py:32
  10.9 12.9 %collective-permute-start.14 = (s32[176]{0:T(256)}, s32[176]{0:T(256)}, u32[]{:S(2)}, u32[]{:S(2)}) collective-permute-start(s32[176]{0:T(256)} %select_reduce_fusion), channel_id=1, source_target_pairs={{0,4},{2,6},{4,0},{6,2},{8,12},{10,14},{12,8},{14,10},{1,5},{3,7},... | collective-permute-start | bytes 2120 | tf_op jit(solution)/shard_map/ppermute | solution.py:32
  22.4 1.0 copy-start.4
  23.9 29.9 %copy-start.2 = (bf16[176,4096]{1,0:T(8,128)(2,1)S(1)}, bf16[176,4096]{1,0:T(8,128)(2,1)}, u32[]{:S(2)}) copy-start(bf16[176,4096]{1,0:T(8,128)(2,1)} %convolution_convert_fusion) | copy-start | bytes 4325380
  23.9 29.9 %collective-permute-start.7 = (bf16[128,1024]{1,0:T(8,128)(2,1)S(1)}, bf16[128,1024]{1,0:T(8,128)(2,1)S(1)}, u32[]{:S(2)}, u32[]{:S(2)}) collective-permute-start(bf16[128,1024]{1,0:T(8,128)(2,1)S(1)} %get-tuple-element.20), channel_id=1, source_target_pairs={{0,2},{2,0},{4,6},{6,4},{8,10},{10,8},{12,14},{14,12},{1,3},{3,1},... | collective-permute-start | bytes 786440 | tf_op jit(solution)/shard_map/ppermute | solution.py:32
  29.6 24.5 %collective-permute-start.6 = (bf16[128,1024]{1,0:T(8,128)(2,1)S(1)}, bf16[128,1024]{1,0:T(8,128)(2,1)S(1)}, u32[]{:S(2)}, u32[]{:S(2)}) collective-permute-start(bf16[128,1024]{1,0:T(8,128)(2,1)S(1)} %get-tuple-element.21), channel_id=1, source_target_pairs={{0,2},{2,0},{4,6},{6,4},{8,10},{10,8},{12,14},{14,12},{1,3},{3,1},... | collective-permute-start | bytes 786440 | tf_op jit(solution)/shard_map/ppermute | solution.py:32
  32.7 25.7 %copy-start.3 = (f32[128,256]{1,0:T(8,128)S(1)}, f32[128,256]{1,0:T(8,128)}, u32[]{:S(2)}) copy-start(f32[128,256]{1,0:T(8,128)} %fusion.17) | copy-start | bytes 393220
  35.3 21.5 %collective-permute-start.1 = (bf16[128,1536]{1,0:T(8,128)(2,1)}, bf16[128,1536]{1,0:T(8,128)(2,1)S(1)}, u32[]{:S(2)}, u32[]{:S(2)}) collective-permute-start(bf16[128,1536]{1,0:T(8,128)(2,1)} %pad_maximum_fusion.1), channel_id=1, source_target_pairs={{0,8},{2,10},{4,12},{6,14},{8,0},{10,2},{12,4},{14,6},{1,9},{3,11}... | collective-permute-start | bytes 1179656 | tf_op jit(solution)/shard_map/ppermute | solution.py:32
  49.3 9.5 %collective-permute-start.5 = (bf16[128,1536]{1,0:T(8,128)(2,1)}, bf16[128,1536]{1,0:T(8,128)(2,1)S(1)}, u32[]{:S(2)}, u32[]{:S(2)}) collective-permute-start(bf16[128,1536]{1,0:T(8,128)(2,1)} %pad_maximum_fusion.1), channel_id=1, source_target_pairs={{0,2},{2,0},{4,6},{6,4},{8,10},{10,8},{12,14},{14,12},{1,3},{3,1},... | collective-permute-start | bytes 1179656 | tf_op jit(solution)/shard_map/ppermute | solution.py:32
  52.4 45.8 %collective-permute-start = (bf16[256,4096]{1,0:T(8,128)(2,1)S(1)}, bf16[256,4096]{1,0:T(8,128)(2,1)S(1)}, u32[]{:S(2)}, u32[]{:S(2)}) collective-permute-start(bf16[256,4096]{1,0:T(8,128)(2,1)S(1)} %copy-done.1), channel_id=1, source_target_pairs={{0,1},{1,0},{2,3},{3,2},{4,5},{5,4},{6,7},{7,6},{8,9},{9,8},{10,11... | collective-permute-start | bytes 6291464 | tf_op jit(solution)/shard_map/ppermute | solution.py:35
  53.8 34.0 %collective-permute-start.15 = (bf16[176,4096]{1,0:T(8,128)(2,1)S(1)}, bf16[176,4096]{1,0:T(8,128)(2,1)S(1)}, u32[]{:S(2)}, u32[]{:S(2)}) collective-permute-start(bf16[176,4096]{1,0:T(8,128)(2,1)S(1)} %copy-done.2), channel_id=1, source_target_pairs={{0,4},{2,6},{4,0},{6,2},{8,12},{10,14},{12,8},{14,10},{1,5},{3,7},... | collective-permute-start | bytes 4325384 | tf_op jit(solution)/shard_map/ppermute | solution.py:32
  54.2 9.4 %collective-permute-start.12 = (bf16[128,1024]{1,0:T(8,128)(2,1)}, bf16[128,1024]{1,0:T(8,128)(2,1)S(1)}, u32[]{:S(2)}, u32[]{:S(2)}) collective-permute-start(bf16[128,1024]{1,0:T(8,128)(2,1)} %collective-permute-done.4), channel_id=1, source_target_pairs={{0,2},{2,0},{4,6},{6,4},{8,10},{10,8},{12,14},{14,12},{1,3},{3,1},... | collective-permute-start | bytes 786440 | tf_op jit(solution)/shard_map/ppermute | solution.py:32
  56.8 12.4 %collective-permute-start.11 = (bf16[128,1024]{1,0:T(8,128)(2,1)}, bf16[128,1024]{1,0:T(8,128)(2,1)S(1)}, u32[]{:S(2)}, u32[]{:S(2)}) collective-permute-start(bf16[128,1024]{1,0:T(8,128)(2,1)} %collective-permute-done.3), channel_id=1, source_target_pairs={{0,2},{2,0},{4,6},{6,4},{8,10},{10,8},{12,14},{14,12},{1,3},{3,1},... | collective-permute-start | bytes 786440 | tf_op jit(solution)/shard_map/ppermute | solution.py:32
  58.8 16.1 %collective-permute-start.10 = (bf16[128,1024]{1,0:T(8,128)(2,1)}, bf16[128,1024]{1,0:T(8,128)(2,1)S(1)}, u32[]{:S(2)}, u32[]{:S(2)}) collective-permute-start(bf16[128,1024]{1,0:T(8,128)(2,1)} %collective-permute-done.2), channel_id=1, source_target_pairs={{0,2},{2,0},{4,6},{6,4},{8,10},{10,8},{12,14},{14,12},{1,3},{3,1},... | collective-permute-start | bytes 786440 | tf_op jit(solution)/shard_map/ppermute | solution.py:32
  60.4 22.5 %copy-start.7 = (s32[256]{0:T(256)S(1)}, s32[256]{0:T(256)}, u32[]{:S(2)}) copy-start(s32[256]{0:T(256)} %and_select_fusion.4) | copy-start | bytes 3076
  60.4 22.5 %copy-start.8 = (s32[128]{0:T(128)S(1)}, s32[128]{0:T(128)}, u32[]{:S(2)}) copy-start(s32[128]{0:T(128)} %and_select_fusion.3) | copy-start | bytes 1540
  63.6 19.2 %collective-permute-start.9 = (bf16[128,1536]{1,0:T(8,128)(2,1)S(1)}, bf16[128,1536]{1,0:T(8,128)(2,1)S(1)}, u32[]{:S(2)}, u32[]{:S(2)}) collective-permute-start(bf16[128,1536]{1,0:T(8,128)(2,1)S(1)} %collective-permute-done.1), channel_id=1, source_target_pairs={{0,2},{2,0},{4,6},{6,4},{8,10},{10,8},{12,14},{14,12},{1,3},{3,1},... | collective-permute-start | bytes 1179656 | tf_op jit(solution)/shard_map/ppermute | solution.py:32
  66.3 18.3 %copy-start.5 = (pred[256]{0:T(512)(128)(4,1)S(1)}, pred[256]{0:T(512)(128)(4,1)}, u32[]{:S(2)}) copy-start(pred[256]{0:T(512)(128)(4,1)} %copy-done.4) | copy-start | bytes 772
  83.2 1.4 %collective-permute-start.13 = (f32[256,128]{0,1:T(8,128)S(1)}, f32[256,128]{0,1:T(8,128)S(1)}, u32[]{:S(2)}, u32[]{:S(2)}) collective-permute-start(f32[256,128]{0,1:T(8,128)S(1)} %fusion.24), channel_id=1, source_target_pairs={{0,1},{1,0},{2,3},{3,2},{4,5},{5,4},{6,7},{7,6},{8,9},{9,8},{10,11... | collective-permute-start | bytes 393224 | tf_op jit(solution)/shard_map/ppermute | solution.py:35
  93.0 5.2 %slice-start = ((s8[8388608]{0:T(1024)(128)(4,1)}), s8[4194304]{0:T(1024)(128)(4,1)S(1)}, s32[]{:S(2)}) async-start(s8[8388608]{0:T(1024)(128)(4,1)} %bitcast.42), calls=%async_computation | async-start | bytes 8388608
  95.4 2.8 %slice-start.1 = ((s8[8388608]{0:T(1024)(128)(4,1)}), s8[4194304]{0:T(1024)(128)(4,1)S(1)}, s32[]{:S(2)}) async-start(s8[8388608]{0:T(1024)(128)(4,1)} %bitcast.42), calls=%async_computation.1 | async-start | bytes 8388608
  96.0 1.4 %collective-permute-start.16 = (f32[176,128]{1,0:T(8,128)S(1)}, f32[176,128]{1,0:T(8,128)S(1)}, u32[]{:S(2)}, u32[]{:S(2)}) collective-permute-start(f32[176,128]{1,0:T(8,128)S(1)} %fusion.33), channel_id=1, source_target_pairs={{0,1},{1,0},{2,3},{3,2},{4,5},{5,4},{6,7},{7,6},{8,9},{9,8},{10,11... | collective-permute-start | bytes 270344 | tf_op jit(solution)/shard_map/ppermute | solution.py:35
  96.4 1.8 %copy-start.10 = (f32[512,256]{1,0:T(8,128)S(1)}, f32[512,256]{1,0:T(8,128)}, u32[]{:S(2)}) copy-start(f32[512,256]{1,0:T(8,128)} %fusion.2) | copy-start | bytes 1572868
  97.9 6.7 %collective-permute-start.17 = (bf16[176,512]{1,0:T(8,128)(2,1)S(1)}, bf16[176,512]{1,0:T(8,128)(2,1)S(1)}, u32[]{:S(2)}, u32[]{:S(2)}) collective-permute-start(bf16[176,512]{1,0:T(8,128)(2,1)S(1)} %convolution_convert_fusion.2), channel_id=1, source_target_pairs={{0,4},{2,6},{4,0},{6,2},{8,12},{10,14},{12,8},{14,10},{1,5},{3,7},... | collective-permute-start | bytes 540680 | tf_op jit(solution)/shard_map/ppermute | solution.py:32

commit v2 on v1

v2 whole, which is shorter than its diff:
```python
import functools
import math

import jax
import jax.numpy as jnp
from jax import lax
from jax.experimental import pallas as pl
from jax.experimental.pallas import tpu as pltpu
from jax.sharding import PartitionSpec as P

adapter_scale = 2.0
bf16 = jnp.bfloat16
f32 = jnp.float32
i32 = jnp.int32
swap_bit = 2
chunk_parts = (10, 6)
vmem_limit = 48 * 1024 * 1024
smem = pl.BlockSpec(memory_space=pltpu.SMEM)


def dot(left, right, contract=(1, 0)):
    return lax.dot_general(left, right, ((contract[:1], contract[1:]), ((), ())), preferred_element_type=f32)


def requests(len_ref, id_ref, me, adapt_dev):
    first, slot = 0, 0
    for q in range(len_ref.shape[0]):
        length, adapter = len_ref[q], id_ref[q]
        away = jnp.where((((adapter // adapt_dev) ^ me) & swap_bit) != 0, length, 0)
        yield first, length, adapter, slot, away
        first, slot = first + length, slot + away


def row_places(reqs, shape, dim):
    r = lax.broadcasted_iota(i32, shape, dim)
    place = jnp.full(shape, -1, i32)
    for first, _, _, slot, away in reqs:
        place = jnp.where((r >= first) & (r < first + away), r - first + slot, place)
    return place


def pack_kernel(adapt_dev, me_ref, len_ref, id_ref, tok_ref, out_ref):
    slots, step = out_ref.shape
    rows = tok_ref.shape[0]
    reqs = list(requests(len_ref, id_ref, me_ref[0], adapt_dev))
    hit = lax.broadcasted_iota(i32, (slots, rows), 0) == row_places(reqs, (1, rows), 1)
    packed = dot(hit.astype(f32).astype(bf16), tok_ref[...])
    col = lax.broadcasted_iota(i32, (1, step), 1) + pl.program_id(0) * step
    adapter_of = jnp.zeros((1, step), i32)
    for _, _, adapter, slot, away in reqs:
        adapter_of = jnp.where((col >= slot) & (col < slot + away), adapter, adapter_of)
    last = lax.broadcasted_iota(i32, (slots, step), 0) == slots - 1
    out_ref[...] = jnp.where(last, adapter_of.astype(f32), packed).astype(bf16)


def cut_kernel(spans, at_ref, down_ref, up_ref, *out_refs):
    *part_refs, mine_ref = out_refs
    heads = up_ref.shape[1]
    for c, (start, size) in enumerate(spans):
        values = down_ref[:, start : start + size]
        part_refs[c][:, :size] = values
        behind = heads if c else 0
        mine_ref[:, start + behind : start + behind + size] = values
    size = spans[0][1]
    part_refs[0][:, size:] = up_ref[...]
    mine_ref[:, size : size + heads] = up_ref[...]


def own_adapters(reqs, rows, both):
    r = lax.broadcasted_iota(i32, (rows, both), 0)
    adapter_of = jnp.zeros((rows, both), i32)
    for first, length, adapter, _, _ in reqs:
        adapter_of = jnp.where((r >= first) & (r < first + length), adapter, adapter_of)
    return adapter_of


def got_adapters(head, both):
    slots, wide = head.shape
    slot = lax.broadcasted_iota(i32, (slots, wide), 0)
    named = jnp.sum(jnp.where(slot == slots - 1, head.astype(f32), 0.0), axis=0, keepdims=True)
    col = lax.broadcasted_iota(i32, (slots, wide), 1)
    across = jnp.sum(jnp.where(slot == col, named, 0.0), axis=1, keepdims=True)
    return jnp.broadcast_to(across, (slots, both)).astype(i32)


def low_kernel(adapt_dev, rank, plan, block, sets, count_x, with_sums, joined, *refs):
    me_ref, len_ref, id_ref, *refs = refs
    me = me_ref[0]
    head_ref = refs.pop(0) if "got" in sets else None
    x_refs = {}
    for name in sets:
        x_refs[name], refs = refs[:count_x], refs[count_x:]
    out_refs = [refs.pop()] * len(sets) if joined else [refs.pop(-len(sets) + k) for k in range(len(sets))]
    sum_refs = [refs.pop(-len(sets) + k) for k in range(len(sets))] if with_sums else None
    at = 0
    for k, name in enumerate(sets):
        count, both = x_refs[name][0].shape[0], out_refs[k].shape[1]
        if name == "own":
            which = own_adapters(list(requests(len_ref, id_ref, me, adapt_dev)), count, both)
        else:
            which = got_adapters(head_ref[...], both)
        total = sum_refs[k][...] if with_sums else jnp.zeros((count, both), f32)
        for m, ref_no, blocks in plan:
            term = None
            for start, col, size in blocks:
                for j in range(0, size, block):
                    more = dot(x_refs[name][(start + j) // block][...], refs[ref_no][:, col + j : col + j + block], (1, 1))
                    term = more if term is None else term + more
            total = total + jnp.where(which // adapt_dev == (me ^ m), term, 0.0)
        if joined:
            lane = lax.broadcasted_iota(i32, (count, both), 1)
            out_refs[k][at : at + count, :] = jnp.where(which % adapt_dev == lane // rank, total, 0.0)
            at += count
        else:
            out_refs[k][...] = total


def up_kernel(adapt_dev, marks, me_ref, len_ref, id_ref, head_ref, part_ref, other_ref, *refs):
    up_refs, (own_ref, got_ref) = refs[:-2], refs[-2:]
    rows, slots = own_ref.shape[0], got_ref.shape[0]
    both = part_ref.shape[1]
    me = me_ref[0]
    own_which = own_adapters(list(requests(len_ref, id_ref, me, adapt_dev)), rows, both)
    got_which = got_adapters(head_ref[...], both)
    for which, out_ref, at, count in ((got_which, got_ref, rows, slots), (own_which, own_ref, 0, rows)):
        low = (part_ref[at : at + count, :] + other_ref[at : at + count, :]).astype(bf16).astype(f32)
        total = None
        for m, up_ref in zip(marks, up_refs, strict=True):
            term = dot(jnp.where(which // adapt_dev == (me ^ m), low, 0.0).astype(bf16), up_ref[...])
            total = term if total is None else total + term
        out_ref[...] = total.astype(bf16)


def last_kernel(adapt_dev, me_ref, len_ref, id_ref, base_ref, own_ref, back_ref, out_ref):
    rows, slots = own_ref.shape[0], back_ref.shape[0]
    reqs = list(requests(len_ref, id_ref, me_ref[0], adapt_dev))
    hit = row_places(reqs, (rows, slots), 0) == lax.broadcasted_iota(i32, (rows, slots), 1)
    delta = own_ref[...].astype(f32) + dot(hit.astype(f32).astype(bf16), back_ref[...])
    out_ref[...] = (base_ref[...] + adapter_scale * delta).astype(bf16)


def whole(x):
    return pl.BlockSpec(x.shape, lambda *_: (0,) * x.ndim)


def columns(x, start, size):
    return pl.BlockSpec((x.shape[0], size), lambda *_: (0, start // size))


def after(x, *others):
    return lax.optimization_barrier((x, *others))[0]


def shards(tokens, kv_weight, down_a, up_weight, adapter_ids, lengths):
    owners = lax.axis_size("adapter")
    core = lax.axis_index("tensor")
    adapt_dev, width, rank = down_a.shape
    both = adapt_dev * rank
    rows, half = tokens.shape
    heads = kv_weight.shape[1]
    req_dev = lengths.shape[0]
    most = 2 * rows // req_dev
    cold = -(-(rows - most) // (req_dev - 1))
    slots = min(rows, most + (owners // 2 - 1) * cold) + 1
    slots = -(-slots // 8) * 8
    head_wide = -(-slots // 128) * 128
    me = lax.axis_index("adapter").astype(i32).reshape(1)
    scalars = (me, lengths, adapter_ids)
    params = pltpu.CompilerParams(vmem_limit_bytes=vmem_limit)

    def flip(x, bit):
        return lax.ppermute(x, "adapter", [(j, j ^ bit) for j in range(owners)])

    def other_core(x):
        return lax.ppermute(x, "tensor", [(0, 1), (1, 0)])

    sizes = [half * p // 16 for p in chunk_parts]
    spans = [(sum(sizes[:c]), size) for c, size in enumerate(sizes)]
    widths = [size + (heads if c == 0 else 0) for c, size in enumerate(sizes)] + [half + heads]
    *parts, mine = pl.pallas_call(
        functools.partial(cut_kernel, spans),
        grid_spec=pltpu.PrefetchScalarGridSpec(
            num_scalar_prefetch=1,
            grid=(1,),
            in_specs=[
                pl.BlockSpec((both, half), lambda _, at: (0, at[0])),
                pl.BlockSpec((both, heads), lambda _, at: (0, at[0])),
            ],
            out_specs=[pl.BlockSpec((both, w), lambda _, at: (0, 0)) for w in widths],
        ),
        out_shape=[jax.ShapeDtypeStruct((both, w), bf16) for w in widths],
        compiler_params=params,
        name="cut",
    )(
        core.astype(i32).reshape(1),
        jnp.transpose(down_a, (0, 2, 1)).reshape(both, width),
        up_weight.reshape(both, -1),
    )

    tokens_other = other_core(after(tokens, mine))

    sent = pl.pallas_call(
        functools.partial(pack_kernel, adapt_dev),
        grid=(4,),
        out_shape=jax.ShapeDtypeStruct((slots, half), bf16),
        in_specs=[smem] * 3 + [pl.BlockSpec((rows, half // 4), lambda g: (0, g))],
        out_specs=pl.BlockSpec((slots, half // 4), lambda g: (0, g)),
        compiler_params=params,
        name="pack",
    )(*scalars, after(tokens, tokens_other))
    got = flip(sent, swap_bit)

    bits = [1 << b for b in range(owners.bit_length() - 1)]
    single = [(mine, [(c, a + (heads if c else 0)) for c, (a, _) in enumerate(spans)])]
    split = [(part, [(c, 0)]) for c, part in enumerate(parts)]
    pieces = {0: single}
    for bit in [b for b in bits if b > swap_bit]:
        for m in list(pieces):
            pieces[m | bit] = [(flip(x, bit), places) for x, places in (split if m == 0 else pieces[m])]
    near = flip(after(mine, sent), 1)

    base_own = dot(tokens, lax.dynamic_slice(kv_weight, (core * half, 0), (half, heads)))
    base = base_own + dot(tokens_other, lax.dynamic_slice(kv_weight, ((1 - core) * half, 0), (half, heads)))

    row_arrays = {"own": tokens, "got": got}

    def add_low(sets, sums, group, joined=False):
        used = sorted({c for _, _, places in group for c, _ in places})
        lowest, above = spans[used[0]][0], sum(spans[used[-1]])
        block = math.gcd(half, *(edge for c in used for edge in spans[c]), lowest)
        at = range(lowest, above, block)
        plan = [
            (m, k, [(spans[c][0] - lowest, col, spans[c][1]) for c, col in places])
            for k, (m, _, places) in enumerate(group)
        ]
        xs = [row_arrays[name] for name in sets]
        tail = [x for _, x, _ in group] + list(sums or [])
        head = [got] if "got" in sets else []
        counts = [rows + slots] if joined else [x.shape[0] for x in xs]
        flops = sum(2 * x.shape[0] * both * size for x in xs for _, _, blocks in plan for _, _, size in blocks)
        return pl.pallas_call(
            functools.partial(low_kernel, adapt_dev, rank, plan, block, sets, len(at), bool(sums), joined),
            grid=(1,),
            out_shape=[jax.ShapeDtypeStruct((n, both), f32) for n in counts],
            in_specs=[smem] * 3
            + [columns(got, 0, head_wide) for _ in head]
            + [columns(x, a, block) for x in xs for a in at]
            + [whole(x) for x in tail],
            out_specs=[pl.BlockSpec((n, both), lambda *_: (0, 0)) for n in counts],
            compiler_params=params,
            cost_estimate=pl.CostEstimate(flops=4 * flops, bytes_accessed=flops // 64, transcendentals=0),
            name="low",
        )(*scalars, *head, *[x for x in xs for _ in at], *tail)

    pieces[1] = [(near, single[0][1])]
    far = [(m, x, places) for m, piece in pieces.items() if m & ~1 and not m & 1 for x, places in piece]
    far.sort(key=lambda item: item[2][0][0])
    batch = max(3, owners // 8)
    groups = [[(0, mine, single[0][1]), (1, near, single[0][1]), far[0]]]
    own = add_low(("own",), None, groups[0])[0]
    rest = []
    for k, (m, x, places) in enumerate(far):
        last = places[0][0] == len(spans) - 1
        across = flip(after(x, own, base) if last else after(x, base_own), 1)
        pieces.setdefault(m | 1, []).append((across, places))
        rest.extend([(m, x, places), (m | 1, across, places)][0 if k else 1 :])
    groups = groups + [rest[a : min(a + batch, len(rest) - 1)] for a in range(0, len(rest) - 1, batch)]
    sums = [own, add_low(("got",), None, groups[0])[0]]
    for group in groups[1:]:
        sums = add_low(("own", "got"), sums, group)
    sums = add_low(("own", "got"), sums, rest[-1:], True)[0]

    other = other_core(sums)
    ups = [piece[0][0] for piece in pieces.values()]
    delta_own, delta_got = pl.pallas_call(
        functools.partial(up_kernel, adapt_dev, list(pieces)),
        grid=(1,),
        out_shape=[jax.ShapeDtypeStruct((count, heads), bf16) for count in (rows, slots)],
        in_specs=[smem] * 3
        + [columns(got, 0, head_wide), whole(sums), whole(other)]
        + [columns(x, sizes[0], heads) for x in ups],
        out_specs=[pl.BlockSpec((count, heads), lambda *_: (0, 0)) for count in (rows, slots)],
        compiler_params=params,
        name="up",
    )(*scalars, got, sums, other, *ups)
    back = flip(delta_got, swap_bit)
    return pl.pallas_call(
        functools.partial(last_kernel, adapt_dev),
        grid=(1,),
        out_shape=jax.ShapeDtypeStruct((rows, heads), bf16),
        in_specs=[smem] * 3 + [whole(base), whole(delta_own), whole(back)],
        out_specs=pl.BlockSpec((rows, heads), lambda *_: (0, 0)),
        compiler_params=params,
        name="last",
    )(*scalars, base, delta_own, back)


def solution(mesh):
    placed = (
        P(("groups", "adapter"), "tensor"),
        P(None, "tensor"),
        P(("groups", "adapter"), None, None),
        P(("groups", "adapter"), None, None),
        P(("groups", "adapter")),
        P(("groups", "adapter")),
    )
    return jax.shard_map(
        shards,
        mesh=mesh,
        in_specs=placed,
        out_specs=P(("groups", "adapter"), "tensor"),
        check_vma=False,
    )
```

time: 106 us -> 96.1 us (0.907)
  matrix products: 27.1 us -> 7.49 us
  Pallas kernels: 0 us -> 18.2 us
  starting transfers between devices: 20.8 us -> 11.1 us
  waiting for transfers between devices: 50.4 us -> 56.2 us
  other arithmetic: 4.42 us -> 0 us
    dot_general x38 -> x2, matrix products: 27.1 us -> 7.49 us  [dot(): lax.dot_general(left, right, ((contract[:1], contract[1:]), ((), ())), pr...]
    pallas_call x0 -> x8, Pallas kernels: none -> 18.2 us  [the longest x4 10.2 us: add_low(): pl.pallas_call(functools.partial(low_kernel, adapt_dev, rank, plan, block...]
    ppermute x15 -> x7, starting transfers between devices: 20.6 us -> 10.6 us  [flip(): return lax.ppermute(x, 'adapter', [(j, j ^ bit) for j in range(owners)])]
    ppermute x3 -> x2, waiting for transfers between devices: 1.53 us -> 5.38 us  [other_core(): return lax.ppermute(x, 'tensor', [(0, 1), (1, 0)])]
    unnamed x26 -> x10, local copies, waits for them, and re-layouts: 0.06 us -> 2.7 us
    select_n x8 -> x0, other arithmetic: 2.02 us -> none  [the longest x2 1.22 us: low_rank_part(): return jnp.where((which % adapt_dev)[:, None] == lane[None, :], total, 0.0)]
    ppermute x15 -> x7, waiting for transfers between devices: 48.9 us -> 50.9 us  [flip(): return lax.ppermute(x, 'adapter', [(j, j ^ bit) for j in range(owners)])]
    dynamic_slice x2 -> x0, local copies, waits for them, and re-layouts: 1.43 us -> none  [the longest x1 1.42 us: shards(): lax.dynamic_slice(down_t, (0, core * half + c * step), (both, step))]
  transfers between devices with their start and end apart: 18 -> 9, of which waited for: 12 -> 7; matrix products, arithmetic and copies ran while one was open for 30% -> 8% of each run, Pallas kernels for 0% -> 9%
where the time goes in v2:
time: 96.1 us; the launch traced here: 95.9 us
  waiting for transfers between devices  56.2 us (58%)
  Pallas kernels  18.2 us (19%)
  starting transfers between devices  11.1 us (12%)
  matrix products  7.49 us (8%)
  local copies, waits for them, and re-layouts  2.7 us (3%)
    ppermute x7, waiting for transfers between devices, flip(): return lax.ppermute(x, 'adapter', [(j, j ^ bit) for j in range(owners)])  50.9 us
    ppermute x7, starting transfers between devices, flip(): return lax.ppermute(x, 'adapter', [(j, j ^ bit) for j in range(owners)])  10.6 us
    pallas_call x4, Pallas kernels, add_low(): pl.pallas_call(functools.partial(low_kernel, adapt_dev, rank, plan, block...  10.2 us
    dot_general x2, matrix products, dot(): lax.dot_general(left, right, ((contract[:1], contract[1:]), ((), ())), pr...  7.49 us
    ppermute x2, waiting for transfers between devices, other_core(): return lax.ppermute(x, 'tensor', [(0, 1), (1, 0)])  5.38 us
    pallas_call x1, Pallas kernels, shards(): pl.pallas_call(functools.partial(pack_kernel, adapt_dev), grid=(4,), out_...  3.06 us
    unnamed x10, local copies, waits for them, and re-layouts  2.7 us
  transfers between devices with their start and end apart: 9, of which 7 were waited for; matrix products, arithmetic and copies ran while one was open for 8% of the time, Pallas kernels for 9%

profile of v2, /device:TPU:0, one launch (start us, length us, event | category | flops | bytes accessed | tf_op | source)
XLA Modules:
  0.0 95.9 jit_solution(2804864007505981277)
XLA Ops:
  0.0 1.7 %copy-done.1 = bf16[2,8192,64]{1,2,0:T(8,128)(2,1)S(1)} copy-done((bf16[2,8192,64]{1,2,0:T(8,128)(2,1)S(1)}, bf16[2,8192,64]{1,2,0:T(8,128)(2,1)}, u32[]{:S(2)}) %copy-start.1) | copy-done | bytes 2097176
  1.7 0.9 copy-done.2
  2.7 1.5 %cut.1 = (bf16[128,3072]{1,0:T(8,128)(2,1)}, bf16[128,1536]{1,0:T(8,128)(2,1)}, bf16[128,4608]{1,0:T(8,128)(2,1)}) custom-call(s32[1]{0:T(128)} %bitcast.2.at_ref, bf16[128,8192]{1,0:T(8,128)(2,1)S(1)} %bitcast.10, bf16[128,1024]{1,0:T(8,128)(2,1)S(1)} %bitcast.11), custom_call_target="tpu_custom_call" | custom-call | tf_op jit(solution)/shard_map/cut/pallas_call | solution.py:180
  4.2 0.0 copy-done
  4.2 0.5 collective-permute-start
  4.7 3.9 %collective-permute-done = bf16[256,4096]{1,0:T(8,128)(2,1)} collective-permute-done((bf16[256,4096]{1,0:T(8,128)(2,1)S(1)}, bf16[256,4096]{1,0:T(8,128)(2,1)}, u32[]{:S(2)}, u32[]{:S(2)}) %collective-permute-start) | collective-permute-done | bytes 2097184 | tf_op jit(solution)/shard_map/ppermute | solution.py:175
  8.6 0.0 copy-done.4
  8.6 3.1 %pack.1 = bf16[168,4096]{1,0:T(8,128)(2,1)} custom-call(s32[1]{0:T(128)} %bitcast.me_ref.refs_0_, s32[7]{0:T(128)S(1)} %copy-done.3, s32[7]{0:T(128)S(1)} %copy-done.4, bf16[256,4096]{1,0:T(8,128)(2,1)S(1)} %copy-done), custom_call_target="tpu_custom_call" | custom-call | tf_op jit(solution)/shard_map/pack/pallas_call | solution.py:202
  11.6 2.9 %collective-permute-start.3 = (bf16[128,4608]{1,0:T(8,128)(2,1)}, bf16[128,4608]{1,0:T(8,128)(2,1)}, u32[]{:S(2)}, u32[]{:S(2)}) collective-permute-start(bf16[128,4608]{1,0:T(8,128)(2,1)} %get-tuple-element.21.refs_11_.refs_12_.refs_0_), channel_id=1, source_target_pairs={{0,2},{2,0},{4,6},{6,4},{8,10},{10,8},{12,14},{14,12},{1,3},{3,1},... | collective-permute-start | bytes 3538952 | tf_op jit(solution)/shard_map/ppermute | solution.py:172
  14.5 2.6 %collective-permute-start.4 = (bf16[128,3072]{1,0:T(8,128)(2,1)}, bf16[128,3072]{1,0:T(8,128)(2,1)}, u32[]{:S(2)}, u32[]{:S(2)}) collective-permute-start(bf16[128,3072]{1,0:T(8,128)(2,1)} %get-tuple-element.22), channel_id=1, source_target_pairs={{0,8},{2,10},{4,12},{6,14},{8,0},{10,2},{12,4},{14,6},{1,9},{3,11}... | collective-permute-start | bytes 2359304 | tf_op jit(solution)/shard_map/ppermute | solution.py:172
  17.1 1.6 %collective-permute-start.1 = (bf16[168,4096]{1,0:T(8,128)(2,1)}, bf16[168,4096]{1,0:T(8,128)(2,1)S(1)}, u32[]{:S(2)}, u32[]{:S(2)}) collective-permute-start(bf16[168,4096]{1,0:T(8,128)(2,1)} %pack.1), channel_id=1, source_target_pairs={{0,4},{2,6},{4,0},{6,2},{8,12},{10,14},{12,8},{14,10},{1,5},{3,7},... | collective-permute-start | bytes 4128776 | tf_op jit(solution)/shard_map/ppermute | solution.py:172
  18.7 0.3 collective-permute-start.2
  19.0 3.4 %fusion.4 = f32[256,512]{1,0:T(8,128)S(1)} fusion(bf16[256,4096]{1,0:T(8,128)(2,1)S(1)} %copy-done, bf16[8192,512]{1,0:T(8,128)(2,1)} %param.7, s32[]{:T(128)S(6)} %select_n.6), kind=kOutput, calls=%fused_computation.4 | convolution fusion | flops 1073741824 | bytes 6815748 | tf_op jit(solution)/shard_map/dot_general | solution.py:22
  22.5 30.6 %collective-permute-done.4.refs_13_.refs_14_.refs_1_ = bf16[128,3072]{1,0:T(8,128)(2,1)} collective-permute-done((bf16[128,3072]{1,0:T(8,128)(2,1)}, bf16[128,3072]{1,0:T(8,128)(2,1)}, u32[]{:S(2)}, u32[]{:S(2)}) %collective-permute-start.4) | collective-permute-done | bytes 786464 | tf_op jit(solution)/shard_map/ppermute | solution.py:172
  53.1 0.2 collective-permute-start.6
  53.3 4.1 %fusion.7.base_ref = f32[256,512]{1,0:T(8,128)S(1)} fusion(f32[256,512]{1,0:T(8,128)S(1)} %fusion.4, bf16[256,4096]{1,0:T(8,128)(2,1)} %collective-permute-done, bf16[8192,512]{1,0:T(8,128)(2,1)} %param.7, s32[]{:T(128)S(6)} %select_n.7), kind=kOutput, calls=%fused_computation.5 | convolution fusion | flops 1073872896 | bytes 7340036 | tf_op jit(solution)/shard_map/dot_general | solution.py:22
  57.4 0.0 collective-permute-done.3.refs_12_.refs_13_.refs_2_
  57.4 3.5 %low.4.refs_22_ = f32[256,128]{1,0:T(8,128)S(1)} custom-call(s32[1]{0:T(128)} %bitcast.me_ref.refs_0_, s32[7]{0:T(128)S(1)} %copy-done.3, s32[7]{0:T(128)S(1)} %copy-done.4, bf16[256,4096]{1,0:T(8,128)(2,1)S(1)} %copy-done, bf16[256,4096]{1,0:T(8,128)(2,1)S(1)} %copy-done, bf16[256,4096]{1,0:T(8,128)(2,1)S(1)} %copy-done, bf16[256,4096]{1,0:T(8,128)(2,1)S(1)} %copy-done, ...), custom_call_target="tpu_custom_call" | custom-call | flops 2818572288 | bytes 11010048 | tf_op jit(solution)/shard_map/low/pallas_call | solution.py:241
  60.9 11.3 %collective-permute-done.2.refs_21_ = bf16[128,1536]{1,0:T(8,128)(2,1)} collective-permute-done((bf16[128,1536]{1,0:T(8,128)(2,1)}, bf16[128,1536]{1,0:T(8,128)(2,1)}, u32[]{:S(2)}, u32[]{:S(2)}) %collective-permute-start.2) | collective-permute-done | bytes 393248 | tf_op jit(solution)/shard_map/ppermute | solution.py:172
  72.2 0.5 collective-permute-start.5
  72.7 0.4 collective-permute-done.1.refs_3_.refs_4_.refs_5_.refs_6_.refs_7_.refs_8_.refs_9_.refs_10_.refs_11_.refs_12_.refs_13_.refs_14_.refs_15_.refs_16_.refs_17_.refs_18_.refs_19_.head_ref
  73.1 3.0 %low.5.refs_23_ = f32[168,128]{1,0:T(8,128)S(1)} custom-call(s32[1]{0:T(128)} %bitcast.me_ref.refs_0_, s32[7]{0:T(128)S(1)} %copy-done.3, s32[7]{0:T(128)S(1)} %copy-done.4, ...), custom_call_target="tpu_custom_call" | custom-call | flops 1849688064 | bytes 7225344 | tf_op jit(solution)/shard_map/low/pallas_call | solution.py:241
  76.1 0.0 collective-permute-done.6.refs_20_.refs_3_
  76.2 2.4 %low.6 = (f32[256,128]{1,0:T(8,128)S(1)}, f32[168,128]{1,0:T(8,128)S(1)}) custom-call(s32[1]{0:T(128)} %bitcast.me_ref.refs_0_, s32[7]{0:T(128)S(1)} %copy-done.3, s32[7]{0:T(128)S(1)} %copy-done.4, ...), custom_call_target="tpu_custom_call" | custom-call | flops 1778384896 | bytes 6946816 | tf_op jit(solution)/shard_map/low/pallas_call | solution.py:241
  78.6 3.8 %collective-permute-done.5.refs_10_ = bf16[128,1536]{1,0:T(8,128)(2,1)S(1)} collective-permute-done((bf16[128,1536]{1,0:T(8,128)(2,1)}, bf16[128,1536]{1,0:T(8,128)(2,1)S(1)}, u32[]{:S(2)}, u32[]{:S(2)}) %collective-permute-start.5) | collective-permute-done | bytes 393248 | tf_op jit(solution)/shard_map/ppermute | solution.py:172
  82.4 1.2 %low.7.part_ref = f32[424,128]{1,0:T(8,128)S(1)} custom-call(s32[1]{0:T(128)} %bitcast.me_ref.refs_0_, s32[7]{0:T(128)S(1)} %copy-done.3, s32[7]{0:T(128)S(1)} %copy-done.4, ...), custom_call_target="tpu_custom_call" | custom-call | flops 666894336 | bytes 2605056 | tf_op jit(solution)/shard_map/low/pallas_call | solution.py:241
  83.6 0.1 collective-permute-start.7
  83.7 1.5 %collective-permute-done.7.other_ref = f32[424,128]{1,0:T(8,128)S(1)} collective-permute-done((f32[424,128]{1,0:T(8,128)S(1)}, f32[424,128]{1,0:T(8,128)S(1)}, u32[]{:S(2)}, u32[]{:S(2)}) %collective-permute-start.7) | collective-permute-done | bytes 217120 | tf_op jit(solution)/shard_map/ppermute | solution.py:175
  85.2 1.9 %up.1 = (bf16[256,512]{1,0:T(8,128)(2,1)S(1)}, bf16[168,512]{1,0:T(8,128)(2,1)S(1)}) custom-call(s32[1]{0:T(128)} %bitcast.me_ref.refs_0_, s32[7]{0:T(128)S(1)} %copy-done.3, s32[7]{0:T(128)S(1)} %copy-done.4, ...), custom_call_target="tpu_custom_call" | custom-call | tf_op jit(solution)/shard_map/up/pallas_call | solution.py:275
  87.1 2.5 %collective-permute-start.8 = (bf16[168,512]{1,0:T(8,128)(2,1)S(1)}, bf16[168,512]{1,0:T(8,128)(2,1)S(1)}, u32[]{:S(2)}, u32[]{:S(2)}) collective-permute-start(bf16[168,512]{1,0:T(8,128)(2,1)S(1)} %get-tuple-element.28), channel_id=1, source_target_pairs={{0,4},{2,6},{4,0},{6,2},{8,12},{10,14},{12,8},{14,10},{1,5},{3,7},... | collective-permute-start | bytes 516104 | tf_op jit(solution)/shard_map/ppermute | solution.py:172
  89.6 4.7 %collective-permute-done.8.back_ref = bf16[168,512]{1,0:T(8,128)(2,1)S(1)} collective-permute-done((bf16[168,512]{1,0:T(8,128)(2,1)S(1)}, bf16[168,512]{1,0:T(8,128)(2,1)S(1)}, u32[]{:S(2)}, u32[]{:S(2)}) %collective-permute-start.8) | collective-permute-done | bytes 172064 | tf_op jit(solution)/shard_map/ppermute | solution.py:172
  94.2 1.6 %last.1 = bf16[256,512]{1,0:T(8,128)(2,1)} custom-call(s32[1]{0:T(128)} %bitcast.me_ref.refs_0_, s32[7]{0:T(128)S(1)} %copy-done.3, s32[7]{0:T(128)S(1)} %copy-done.4, f32[256,512]{1,0:T(8,128)S(1)} %fusion.7.base_ref, bf16[256,512]{1,0:T(8,128)(2,1)S(1)} %get-tuple-element.27.own_ref, bf16[168,512]{1,0:T(8,128)(2,1)S(1)} %collective-permute-done.8.back_ref), custom_call_target="tpu_custom_call" | custom-call | tf_op jit(solution)/shard_map/last/pallas_call | solution.py:287
  (6 shorter events, 0.0 us)
Async XLA Ops:
  0.0 4.2 %copy-start = (bf16[256,4096]{1,0:T(8,128)(2,1)S(1)}, bf16[256,4096]{1,0:T(8,128)(2,1)}, u32[]{:S(2)}) copy-start(bf16[256,4096]{1,0:T(8,128)(2,1)} %refs_6_.5) | copy-start | bytes 6291460
  0.0 1.7 %copy-start.1 = (bf16[2,8192,64]{1,2,0:T(8,128)(2,1)S(1)}, bf16[2,8192,64]{1,2,0:T(8,128)(2,1)}, u32[]{:S(2)}) copy-start(bf16[2,8192,64]{1,2,0:T(8,128)(2,1)} %param.8) | copy-start | bytes 6291460
  1.7 0.9 copy-start.2
  2.7 5.9 %copy-start.3 = (s32[7]{0:T(128)S(1)}, s32[7]{0:T(128)}, u32[]{:S(2)}) copy-start(s32[7]{0:T(128)} %len_ref.5) | copy-start | bytes 88
  2.7 5.9 %copy-start.4 = (s32[7]{0:T(128)S(1)}, s32[7]{0:T(128)}, u32[]{:S(2)}) copy-start(s32[7]{0:T(128)} %id_ref.5) | copy-start | bytes 88
  4.2 4.4 %collective-permute-start = (bf16[256,4096]{1,0:T(8,128)(2,1)S(1)}, bf16[256,4096]{1,0:T(8,128)(2,1)}, u32[]{:S(2)}, u32[]{:S(2)}) collective-permute-start(bf16[256,4096]{1,0:T(8,128)(2,1)S(1)} %copy-done), channel_id=1, source_target_pairs={{0,1},{1,0},{2,3},{3,2},{4,5},{5,4},{6,7},{7,6},{8,9},{9,8},{10,11... | collective-permute-start | bytes 6291464 | tf_op jit(solution)/shard_map/ppermute | solution.py:175
  11.6 45.7 %collective-permute-start.3 = (bf16[128,4608]{1,0:T(8,128)(2,1)}, bf16[128,4608]{1,0:T(8,128)(2,1)}, u32[]{:S(2)}, u32[]{:S(2)}) collective-permute-start(bf16[128,4608]{1,0:T(8,128)(2,1)} %get-tuple-element.21.refs_11_.refs_12_.refs_0_), channel_id=1, source_target_pairs={{0,2},{2,0},{4,6},{6,4},{8,10},{10,8},{12,14},{14,12},{1,3},{3,1},... | collective-permute-start | bytes 3538952 | tf_op jit(solution)/shard_map/ppermute | solution.py:172
  14.5 38.6 %collective-permute-start.4 = (bf16[128,3072]{1,0:T(8,128)(2,1)}, bf16[128,3072]{1,0:T(8,128)(2,1)}, u32[]{:S(2)}, u32[]{:S(2)}) collective-permute-start(bf16[128,3072]{1,0:T(8,128)(2,1)} %get-tuple-element.22), channel_id=1, source_target_pairs={{0,8},{2,10},{4,12},{6,14},{8,0},{10,2},{12,4},{14,6},{1,9},{3,11}... | collective-permute-start | bytes 2359304 | tf_op jit(solution)/shard_map/ppermute | solution.py:172
  17.1 56.0 %collective-permute-start.1 = (bf16[168,4096]{1,0:T(8,128)(2,1)}, bf16[168,4096]{1,0:T(8,128)(2,1)S(1)}, u32[]{:S(2)}, u32[]{:S(2)}) collective-permute-start(bf16[168,4096]{1,0:T(8,128)(2,1)} %pack.1), channel_id=1, source_target_pairs={{0,4},{2,6},{4,0},{6,2},{8,12},{10,14},{12,8},{14,10},{1,5},{3,7},... | collective-permute-start | bytes 4128776 | tf_op jit(solution)/shard_map/ppermute | solution.py:172
  18.7 53.5 %collective-permute-start.2 = (bf16[128,1536]{1,0:T(8,128)(2,1)}, bf16[128,1536]{1,0:T(8,128)(2,1)}, u32[]{:S(2)}, u32[]{:S(2)}) collective-permute-start(bf16[128,1536]{1,0:T(8,128)(2,1)} %get-tuple-element.20), channel_id=1, source_target_pairs={{0,8},{2,10},{4,12},{6,14},{8,0},{10,2},{12,4},{14,6},{1,9},{3,11}... | collective-permute-start | bytes 1179656 | tf_op jit(solution)/shard_map/ppermute | solution.py:172
  53.1 23.1 %collective-permute-start.6 = (bf16[128,3072]{1,0:T(8,128)(2,1)}, bf16[128,3072]{1,0:T(8,128)(2,1)S(1)}, u32[]{:S(2)}, u32[]{:S(2)}) collective-permute-start(bf16[128,3072]{1,0:T(8,128)(2,1)} %collective-permute-done.4.refs_13_.refs_14_.refs_1_), channel_id=1, source_target_pairs={{0,2},{2,0},{4,6},{6,4},{8,10},{10,8},{12,14},{14,12},{1,3},{3,1},... | collective-permute-start | bytes 2359304 | tf_op jit(solution)/shard_map/ppermute | solution.py:172
  72.2 10.2 %collective-permute-start.5 = (bf16[128,1536]{1,0:T(8,128)(2,1)}, bf16[128,1536]{1,0:T(8,128)(2,1)S(1)}, u32[]{:S(2)}, u32[]{:S(2)}) collective-permute-start(bf16[128,1536]{1,0:T(8,128)(2,1)} %collective-permute-done.2.refs_21_), channel_id=1, source_target_pairs={{0,2},{2,0},{4,6},{6,4},{8,10},{10,8},{12,14},{14,12},{1,3},{3,1},... | collective-permute-start | bytes 1179656 | tf_op jit(solution)/shard_map/ppermute | solution.py:172
  83.6 1.5 %collective-permute-start.7 = (f32[424,128]{1,0:T(8,128)S(1)}, f32[424,128]{1,0:T(8,128)S(1)}, u32[]{:S(2)}, u32[]{:S(2)}) collective-permute-start(f32[424,128]{1,0:T(8,128)S(1)} %low.7.part_ref), channel_id=1, source_target_pairs={{0,1},{1,0},{2,3},{3,2},{4,5},{5,4},{6,7},{7,6},{8,9},{9,8},{10,11... | collective-permute-start | bytes 651272 | tf_op jit(solution)/shard_map/ppermute | solution.py:175
  87.1 7.2 %collective-permute-start.8 = (bf16[168,512]{1,0:T(8,128)(2,1)S(1)}, bf16[168,512]{1,0:T(8,128)(2,1)S(1)}, u32[]{:S(2)}, u32[]{:S(2)}) collective-permute-start(bf16[168,512]{1,0:T(8,128)(2,1)S(1)} %get-tuple-element.28), channel_id=1, source_target_pairs={{0,4},{2,6},{4,0},{6,2},{8,12},{10,14},{12,8},{14,10},{1,5},{3,7},... | collective-permute-start | bytes 516104 | tf_op jit(solution)/shard_map/ppermute | solution.py:172

commit v3 on v2

v3 whole, which is shorter than its diff:
```python
import functools
import math

import jax
import jax.numpy as jnp
from jax import lax
from jax.experimental import pallas as pl
from jax.experimental.pallas import tpu as pltpu
from jax.sharding import PartitionSpec as P

adapter_scale = 2.0
bf16 = jnp.bfloat16
f32 = jnp.float32
i32 = jnp.int32
swap_bit = 2
chunk_parts = (7, 5, 4)
up_chunk = 0
halves = 2
vmem_limit = 48 * 1024 * 1024
smem = pl.BlockSpec(memory_space=pltpu.SMEM)


def dot(left, right, contract=(1, 0)):
    return lax.dot_general(left, right, ((contract[:1], contract[1:]), ((), ())), preferred_element_type=f32)


def requests(len_ref, id_ref, me, adapt_dev):
    first, slot = 0, 0
    for q in range(len_ref.shape[0]):
        length, adapter = len_ref[q], id_ref[q]
        away = jnp.where((((adapter // adapt_dev) ^ me) & swap_bit) != 0, length, 0)
        yield first, length, adapter, slot, away
        first, slot = first + length, slot + away


def row_places(reqs, shape, dim):
    r = lax.broadcasted_iota(i32, shape, dim)
    place = jnp.full(shape, -1, i32)
    for first, _, _, slot, away in reqs:
        place = jnp.where((r >= first) & (r < first + away), r - first + slot, place)
    return place


def start_kernel(adapt_dev, spans, with_up, len_ref, id_ref, tok_ref, down_ref, up_ref, *refs):
    sent_refs, (*part_refs, mine_ref, sems) = refs[:halves], refs[halves:]
    half = sum(size for _, size in spans)
    heads = mine_ref.shape[1] - half
    core = lax.axis_index("tensor")

    def features(start, size):
        return down_ref.at[:, pl.ds(pl.multiple_of(core * half + start, 128), size)]

    up = up_ref.at[:, pl.ds(pl.multiple_of(core * heads, 128), heads)]
    moves = []
    for c, (start, size) in enumerate(spans):
        ahead = heads if c == with_up else 0
        moves.append((features(start, size), part_refs[c].at[:, pl.ds(ahead, size)]))
    moves.append((up, part_refs[with_up].at[:, pl.ds(0, heads)]))
    moves.append((up, mine_ref.at[:, pl.ds(0, heads)]))
    moves.append((features(0, half), mine_ref.at[:, pl.ds(heads, half)]))
    copies = [pltpu.make_async_copy(source, target, sems.at[k]) for k, (source, target) in enumerate(moves)]

    @pl.when(pl.program_id(0) == 0)
    def _():
        for copy in copies:
            copy.start()

    slots, step = sent_refs[0].shape
    rows = tok_ref.shape[0]
    reqs = list(requests(len_ref, id_ref, lax.axis_index("adapter"), adapt_dev))
    hit = lax.broadcasted_iota(i32, (slots, rows), 0) == row_places(reqs, (1, rows), 1)
    packed = dot(hit.astype(f32).astype(bf16), tok_ref[...])
    col = lax.broadcasted_iota(i32, (1, step), 1) + pl.program_id(0) * step
    adapter_of = jnp.zeros((1, step), i32)
    for _, _, adapter, slot, away in reqs:
        adapter_of = jnp.where((col >= slot) & (col < slot + away), adapter, adapter_of)
    last = lax.broadcasted_iota(i32, (slots, step), 0) == slots - 1
    packed = jnp.where(last, adapter_of.astype(f32), packed).astype(bf16)
    for part, sent_ref in enumerate(sent_refs):

        @pl.when(pl.program_id(0) == part)
        def _():
            sent_ref[...] = packed

    @pl.when(pl.program_id(0) == halves - 1)
    def _():
        for copy in copies:
            copy.wait()


def own_adapters(reqs, rows, both):
    r = lax.broadcasted_iota(i32, (rows, both), 0)
    adapter_of = jnp.zeros((rows, both), i32)
    for first, length, adapter, _, _ in reqs:
        adapter_of = jnp.where((r >= first) & (r < first + length), adapter, adapter_of)
    return adapter_of


def got_adapters(head, both):
    slots, wide = head.shape
    slot = lax.broadcasted_iota(i32, (slots, wide), 0)
    named = jnp.sum(jnp.where(slot == slots - 1, head.astype(f32), 0.0), axis=0, keepdims=True)
    col = lax.broadcasted_iota(i32, (slots, wide), 1)
    across = jnp.sum(jnp.where(slot == col, named, 0.0), axis=1, keepdims=True)
    return jnp.broadcast_to(across, (slots, both)).astype(i32)


def which_adapters(adapt_dev, me_ref, len_ref, id_ref, head_refs, shape):
    if head_refs:
        return got_adapters(head_refs[0][...], shape[1])
    return own_adapters(list(requests(len_ref, id_ref, me_ref[0], adapt_dev)), *shape)


def low_kernel(adapt_dev, rank, plan, block, heads_in, x_count, first, final, me_ref, len_ref, id_ref, *refs):
    head_refs, refs = refs[:heads_in], refs[heads_in:]
    x_refs, refs, out_ref = refs[:x_count], refs[x_count:-1], refs[-1]
    which = which_adapters(adapt_dev, me_ref, len_ref, id_ref, head_refs, out_ref.shape)
    me = me_ref[0]
    total = jnp.zeros(out_ref.shape, f32) if first else refs[-1][...]
    for m, ref_no, blocks in plan:
        term = None
        for start, col, size in blocks:
            for j in range(0, size, block):
                down = refs[ref_no][:, col + j : col + j + block]
                more = dot(x_refs[(start + j) // block][...], down, (1, 1))
                term = more if term is None else term + more
        total = total + jnp.where(which // adapt_dev == (me ^ m), term, 0.0)
    if final:
        lane = lax.broadcasted_iota(i32, out_ref.shape, 1)
        total = jnp.where(which % adapt_dev == lane // rank, total, 0.0)
    out_ref[...] = total


def up_kernel(adapt_dev, marks, heads_in, me_ref, len_ref, id_ref, *refs):
    head_refs, refs = refs[:heads_in], refs[heads_in:]
    part_ref, other_ref, *refs, out_ref = refs
    which = which_adapters(adapt_dev, me_ref, len_ref, id_ref, head_refs, part_ref.shape)
    low = (part_ref[...] + other_ref[...]).astype(bf16).astype(f32)
    total = None
    for m, up_ref in zip(marks, refs):
        term = dot(jnp.where(which // adapt_dev == (me_ref[0] ^ m), low, 0.0).astype(bf16), up_ref[...])
        total = term if total is None else total + term
    delta = total.astype(bf16)
    if heads_in:
        out_ref[...] = delta
    else:
        out_ref[...] = refs[-1][...] + adapter_scale * delta.astype(f32)


def last_kernel(adapt_dev, me_ref, len_ref, id_ref, sum_ref, back_ref, out_ref):
    rows, slots = sum_ref.shape[0], back_ref.shape[0]
    reqs = list(requests(len_ref, id_ref, me_ref[0], adapt_dev))
    hit = row_places(reqs, (rows, slots), 0) == lax.broadcasted_iota(i32, (rows, slots), 1)
    delta = dot(hit.astype(f32).astype(bf16), back_ref[...])
    out_ref[...] = (sum_ref[...] + adapter_scale * delta).astype(bf16)


def whole(x):
    return pl.BlockSpec(x.shape, lambda *_: (0,) * x.ndim)


def columns(x, start, size):
    return pl.BlockSpec((x.shape[0], size), lambda *_: (0, start // size))


def after(x, *others):
    return lax.optimization_barrier((x, *others))[0]


def shards(tokens, kv_weight, down_a, up_weight, adapter_ids, lengths):
    owners = lax.axis_size("adapter")
    core = lax.axis_index("tensor")
    adapt_dev, width, rank = down_a.shape
    both = adapt_dev * rank
    rows, half = tokens.shape
    heads = kv_weight.shape[1]
    req_dev = lengths.shape[0]
    most = 2 * rows // req_dev
    cold = -(-(rows - most) // (req_dev - 1))
    slots = min(rows, most + (owners // 2 - 1) * cold) + 1
    slots = -(-slots // 8) * 8
    head_wide = -(-slots // 128) * 128
    me = lax.axis_index("adapter").astype(i32).reshape(1)
    scalars = (me, lengths, adapter_ids)
    params = pltpu.CompilerParams(vmem_limit_bytes=vmem_limit)

    def flip(x, bit):
        return lax.ppermute(x, "adapter", [(j, j ^ bit) for j in range(owners)])

    def other_core(x):
        return lax.ppermute(x, "tensor", [(0, 1), (1, 0)])

    sizes = [half * p // 16 for p in chunk_parts]
    spans = [(sum(sizes[:c]), size) for c, size in enumerate(sizes)]
    widths = [size + (heads if c == up_chunk else 0) for c, size in enumerate(sizes)] + [half + heads]
    sent_shapes = [jax.ShapeDtypeStruct((slots, half // halves), bf16)] * halves
    *outs, mine = pl.pallas_call(
        functools.partial(start_kernel, adapt_dev, spans, up_chunk),
        grid=(halves,),
        out_shape=sent_shapes + [jax.ShapeDtypeStruct((both, w), bf16) for w in widths],
        in_specs=[smem] * 2
        + [pl.BlockSpec((rows, half // halves), lambda g: (0, g))]
        + [pl.BlockSpec(memory_space=pl.ANY)] * 2,
        out_specs=[pl.BlockSpec((slots, half // halves), lambda *_: (0, 0))] * halves
        + [pl.BlockSpec((both, w), lambda *_: (0, 0)) for w in widths],
        scratch_shapes=[pltpu.SemaphoreType.DMA((len(spans) + 3,))],
        compiler_params=params,
        name="start",
    )(lengths, adapter_ids, tokens, jnp.transpose(down_a, (0, 2, 1)).reshape(both, width), up_weight.reshape(both, -1))
    sent, parts = outs[:halves], outs[halves:]
    tokens_other = other_core(after(tokens, sent[0]))
    got = [flip(after(x, tokens_other), swap_bit) for x in sent]

    bits = [1 << b for b in range(owners.bit_length() - 1)]
    whole_places = [(c, heads + a) for c, (a, _) in enumerate(spans)]
    split = [(part, [(c, heads if c == up_chunk else 0)]) for c, part in enumerate(parts)]
    pieces = {0: [(mine, whole_places)]}
    for bit in [b for b in bits if b > swap_bit]:
        for m in list(pieces):
            came = []
            for c, (x, places) in enumerate(split if m == 0 else pieces[m]):
                came.append((flip(after(x, came[0][0]) if c == 2 else x, bit), places))
            pieces[m | bit] = came
    near = flip(mine, 1)

    base_own = dot(tokens, lax.dynamic_slice(kv_weight, (core * half, 0), (half, heads)))
    base = base_own + dot(tokens_other, lax.dynamic_slice(kv_weight, ((1 - core) * half, 0), (half, heads)))

    def add_low(arrays, heads_in, sums, group, final=False):
        used = sorted({c for _, _, places in group for c, _ in places})
        lowest, above = spans[used[0]][0], sum(spans[used[-1]])
        block = math.gcd(half // halves, *(edge for c in used for edge in spans[c]), lowest)
        at = range(lowest, above, block)
        plan = [
            (m, k, [(spans[c][0] - lowest, col, spans[c][1]) for c, col in places])
            for k, (m, _, places) in enumerate(group)
        ]
        xs = [arrays[a * len(arrays) // half] for a in at]
        x_specs = [columns(x, a % x.shape[1], block) for x, a in zip(xs, at, strict=True)]
        tail = [x for _, x, _ in group] + ([] if sums is None else [sums])
        n = arrays[0].shape[0]
        flops = sum(2 * n * both * size for _, _, blocks in plan for _, _, size in blocks)
        return pl.pallas_call(
            functools.partial(
                low_kernel, adapt_dev, rank, plan, block, len(heads_in), len(xs), sums is None, final
            ),
            grid=(1,),
            out_shape=jax.ShapeDtypeStruct((n, both), f32),
            in_specs=[smem] * 3 + [columns(x, 0, head_wide) for x in heads_in] + x_specs + [whole(x) for x in tail],
            out_specs=pl.BlockSpec((n, both), lambda *_: (0, 0)),
            compiler_params=params,
            cost_estimate=pl.CostEstimate(flops=4 * flops, bytes_accessed=flops // 64, transcendentals=0),
            name="low",
        )(*scalars, *heads_in, *xs, *tail)

    pieces[1] = [(near, whole_places)]
    far = [(m, x, places) for m, piece in pieces.items() if m & ~1 and not m & 1 for x, places in piece]
    far.sort(key=lambda item: item[2][0][0])
    items = [(0, mine, whole_places), (1, near, whole_places), far[0]]
    own = add_low([tokens], [], None, items)
    done = len(items)
    for k, (m, x, places) in enumerate(far):
        last = places[0][0] == len(spans) - 1
        if False:
            own, done = add_low([tokens], [], own, items[3:5]), 5
        across = flip(after(x, own, base) if last else after(x, own if k else base_own), 1)
        pieces.setdefault(m | 1, []).append((across, places))
        items.extend([(m, x, places), (m | 1, across, places)][0 if k else 1 :])

    def low_rank(arrays, heads_in, sums, todo, batch, final):
        rest = len(todo) - final
        for a in range(0, rest, batch):
            sums = add_low(arrays, heads_in, sums, todo[a : min(a + batch, rest)])
        part = add_low(arrays, heads_in, sums, todo[rest:], True)
        return part, other_core(part)

    ups = [next(x for x, places in piece if (up_chunk, heads) == places[-1] or len(places) > 1) for piece in pieces.values()]

    def up(heads_in, lows, extra, kind):
        n = lows[0].shape[0]
        return pl.pallas_call(
            functools.partial(up_kernel, adapt_dev, list(pieces), len(heads_in)),
            grid=(1,),
            out_shape=jax.ShapeDtypeStruct((n, heads), kind),
            in_specs=[smem] * 3
            + [columns(x, 0, head_wide) for x in heads_in]
            + [whole(x) for x in lows]
            + [columns(x, 0, heads) for x in ups]
            + [whole(x) for x in extra],
            out_specs=pl.BlockSpec((n, heads), lambda *_: (0, 0)),
            compiler_params=params,
            name="up",
        )(*scalars, *heads_in, *lows, *ups, *extra)

    low_got = low_rank(got, got[:1], None, items, max(6, owners // 8), 2)
    delta_got = up(got[:1], low_got, [], bf16)
    back = flip(delta_got, swap_bit)
    low_own = low_rank([tokens], [], after(own, delta_got), items[done:], max(5, owners // 8), 5)
    total = up([], low_own, [base], f32)
    return pl.pallas_call(
        functools.partial(last_kernel, adapt_dev),
        grid=(1,),
        out_shape=jax.ShapeDtypeStruct((rows, heads), bf16),
        in_specs=[smem] * 3 + [whole(total), whole(back)],
        out_specs=pl.BlockSpec((rows, heads), lambda *_: (0, 0)),
        compiler_params=params,
        name="last",
    )(*scalars, total, back)


def solution(mesh):
    placed = (
        P(("groups", "adapter"), "tensor"),
        P(None, "tensor"),
        P(("groups", "adapter"), None, None),
        P(("groups", "adapter"), None, None),
        P(("groups", "adapter")),
        P(("groups", "adapter")),
    )
    return jax.shard_map(
        shards,
        mesh=mesh,
        in_specs=placed,
        out_specs=P(("groups", "adapter"), "tensor"),
        check_vma=False,
    )
```

time: 96.1 us -> 90.1 us (0.938)
  waiting for transfers between devices: 56.2 us -> 47 us
  matrix products: 7.49 us -> 8.94 us
  local copies, waits for them, and re-layouts: 2.7 us -> 3.82 us
    ppermute x7 -> x10, waiting for transfers between devices: 50.9 us -> 44.4 us  [flip(): return lax.ppermute(x, 'adapter', [(j, j ^ bit) for j in range(owners)])]
    ppermute x2 -> x3, waiting for transfers between devices: 5.38 us -> 2.61 us  [other_core(): return lax.ppermute(x, 'tensor', [(0, 1), (1, 0)])]
    dot_general x2, matrix products: 7.49 us -> 8.94 us  [dot(): lax.dot_general(left, right, ((contract[:1], contract[1:]), ((), ())), pr...]
    unnamed x10 -> x16, local copies, waits for them, and re-layouts: 2.7 us -> 3.82 us
    ppermute x7 -> x10, starting transfers between devices: 10.6 us -> 10.7 us  [flip(): return lax.ppermute(x, 'adapter', [(j, j ^ bit) for j in range(owners)])]
  transfers between devices with their start and end apart: 9 -> 13, of which waited for: 7 -> 7; matrix products, arithmetic and copies ran while one was open for 8% -> 10% of each run, Pallas kernels for 9% -> 12%
where the time goes in v3:
time: 90.1 us; the launch traced here: 89.8 us
  waiting for transfers between devices  47 us (52%)
  Pallas kernels  18.7 us (21%)
  starting transfers between devices  11.2 us (12%)
  matrix products  8.94 us (10%)
  local copies, waits for them, and re-layouts  3.82 us (4%)
    ppermute x10, waiting for transfers between devices, flip(): return lax.ppermute(x, 'adapter', [(j, j ^ bit) for j in range(owners)])  44.4 us
    ppermute x10, starting transfers between devices, flip(): return lax.ppermute(x, 'adapter', [(j, j ^ bit) for j in range(owners)])  10.7 us
    pallas_call x4, Pallas kernels, add_low(): pl.pallas_call(functools.partial(low_kernel, adapt_dev, rank, plan, block...  10.1 us
    dot_general x2, matrix products, dot(): lax.dot_general(left, right, ((contract[:1], contract[1:]), ((), ())), pr...  8.94 us
    pallas_call x1, Pallas kernels, shards(): pl.pallas_call(functools.partial(start_kernel, adapt_dev, spans, up_chunk...  4.08 us
    unnamed x16, local copies, waits for them, and re-layouts  3.82 us
    pallas_call x2, Pallas kernels, up(): pl.pallas_call(functools.partial(up_kernel, adapt_dev, list(pieces), len(...  2.87 us
    ppermute x3, waiting for transfers between devices, other_core(): return lax.ppermute(x, 'tensor', [(0, 1), (1, 0)])  2.61 us
  transfers between devices with their start and end apart: 13, of which 7 were waited for; matrix products, arithmetic and copies ran while one was open for 10% of the time, Pallas kernels for 12%

profile of v3, /device:TPU:0, one launch (start us, length us, event | category | flops | bytes accessed | tf_op | source)
XLA Modules:
  0.0 89.8 jit_solution(36379036865753643)
XLA Ops:
  0.0 0.9 %copy-done = bf16[2,64,1024]{2,1,0:T(8,128)(2,1)S(1)} copy-done((bf16[2,64,1024]{2,1,0:T(8,128)(2,1)S(1)}, bf16[2,64,1024]{2,1,0:T(8,128)(2,1)}, u32[]{:S(2)}) %copy-start) | copy-done | bytes 262168
  1.0 0.7 copy-done.1
  1.6 0.7 copy-done.3
  2.3 4.1 %start.1 = (bf16[168,2048]{1,0:T(8,128)(2,1)}, bf16[168,2048]{1,0:T(8,128)(2,1)S(1)}, bf16[128,2304]{1,0:T(8,128)(2,1)}, bf16[128,1280]{1,0:T(8,128)(2,1)}, bf16...) custom-call(s32[7]{0:T(128)S(1)} %copy-done.1, s32[7]{0:T(128)S(1)} %copy-done.3, bf16[256,4096]{1,0:T(8,128)(2,1)} %refs_15_.3, ...), custom_call_target="tpu_custom_call" | custom-call | tf_op jit(solution)/shard_map/start/pallas_call | solution.py:197
  6.4 0.8 copy-done.5
  7.2 0.7 copy-done.6
  7.9 0.5 collective-permute-start.6
  8.4 2.5 %collective-permute-start.3 = (bf16[128,4608]{1,0:T(8,128)(2,1)S(1)}, bf16[128,4608]{1,0:T(8,128)(2,1)}, u32[]{:S(2)}, u32[]{:S(2)}) collective-permute-start(bf16[128,4608]{1,0:T(8,128)(2,1)S(1)} %get-tuple-element.22.refs_16_.refs_17_.refs_3_.refs_2_), channel_id=1, source_target_pairs={{0,2},{2,0},{4,6},{6,4},{8,10},{10,8},{12,14},{14,12},{1,3},{3,1},... | collective-permute-start | bytes 3538952 | tf_op jit(solution)/shard_map/ppermute | solution.py:188
  10.8 2.6 %collective-permute-start = (bf16[128,2304]{1,0:T(8,128)(2,1)}, bf16[128,2304]{1,0:T(8,128)(2,1)S(1)}, u32[]{:S(2)}, u32[]{:S(2)}) collective-permute-start(bf16[128,2304]{1,0:T(8,128)(2,1)} %get-tuple-element.19), channel_id=1, source_target_pairs={{0,8},{2,10},{4,12},{6,14},{8,0},{10,2},{12,4},{14,6},{1,9},{3,11}... | collective-permute-start | bytes 1769480 | tf_op jit(solution)/shard_map/ppermute | solution.py:188
  13.4 0.3 collective-permute-start.2
  13.8 1.7 %collective-permute-start.8 = (bf16[168,2048]{1,0:T(8,128)(2,1)}, bf16[168,2048]{1,0:T(8,128)(2,1)S(1)}, u32[]{:S(2)}, u32[]{:S(2)}) collective-permute-start(bf16[168,2048]{1,0:T(8,128)(2,1)} %get-tuple-element.29), channel_id=1, source_target_pairs={{0,4},{2,6},{4,0},{6,2},{8,12},{10,14},{12,8},{14,10},{1,5},{3,7},... | collective-permute-start | bytes 2064392 | tf_op jit(solution)/shard_map/ppermute | solution.py:188
  15.4 0.4 collective-permute-start.9
  15.8 4.9 %fusion.4 = f32[256,512]{1,0:T(8,128)} fusion(bf16[256,4096]{1,0:T(8,128)(2,1)} %refs_15_.3, bf16[8192,512]{1,0:T(8,128)(2,1)} %param.7, s32[]{:T(128)S(6)} %select_n.6), kind=kOutput, calls=%fused_computation.4 | convolution fusion | flops 1073741824 | bytes 6815748 | tf_op jit(solution)/shard_map/dot_general | solution.py:24
  20.7 27.2 %collective-permute-done.refs_18_.refs_19_.refs_4_.refs_3_ = bf16[128,2304]{1,0:T(8,128)(2,1)S(1)} collective-permute-done((bf16[128,2304]{1,0:T(8,128)(2,1)}, bf16[128,2304]{1,0:T(8,128)(2,1)S(1)}, u32[]{:S(2)}, u32[]{:S(2)}) %collective-permute-start) | collective-permute-done | bytes 589856 | tf_op jit(solution)/shard_map/ppermute | solution.py:188
  47.9 0.2 collective-permute-start.1
  48.1 3.6 %low.4.refs_21_ = f32[256,128]{1,0:T(8,128)S(1)} custom-call(s32[1]{0:T(128)} %bitcast.me_ref, s32[7]{0:T(128)S(1)} %copy-done.2, s32[7]{0:T(128)S(1)} %copy-done.4, bf16[256,4096]{1,0:T(8,128)(2,1)} %refs_15_.3, bf16[256,4096]{1,0:T(8,128)(2,1)} %refs_15_.3, bf16[256,4096]{1,0:T(8,128)(2,1)} %refs_15_.3, bf16[256,4096]{1,0:T(8,128)(2,1)} %refs_15_.3, ...), custom_call_target="tpu_custom_call" | custom-call | flops 2617245696 | bytes 10223616 | tf_op jit(solution)/shard_map/low/pallas_call | solution.py:243
  51.7 3.2 %collective-permute-done.2.refs_21_.refs_17_ = bf16[128,1280]{1,0:T(8,128)(2,1)S(1)} collective-permute-done((bf16[128,1280]{1,0:T(8,128)(2,1)}, bf16[128,1280]{1,0:T(8,128)(2,1)S(1)}, u32[]{:S(2)}, u32[]{:S(2)}) %collective-permute-start.2) | collective-permute-done | bytes 327712 | tf_op jit(solution)/shard_map/ppermute | solution.py:188
  54.9 0.2 collective-permute-start.4
  55.1 4.1 %fusion.7.refs_6_ = f32[256,512]{1,0:T(8,128)S(1)} fusion(f32[256,512]{1,0:T(8,128)S(1)} %copy-done.7, bf16[256,4096]{1,0:T(8,128)(2,1)} %collective-permute-done.6, bf16[8192,512]{1,0:T(8,128)(2,1)} %param.7, s32[]{:T(128)S(6)} %select_n.7), kind=kOutput, calls=%fused_computation.5 | convolution fusion | flops 1073872896 | bytes 7340036 | tf_op jit(solution)/shard_map/dot_general | solution.py:24
  59.1 9.8 %collective-permute-done.5.refs_2_.refs_19_ = bf16[128,1024]{1,0:T(8,128)(2,1)S(1)} collective-permute-done((bf16[128,1024]{1,0:T(8,128)(2,1)}, bf16[128,1024]{1,0:T(8,128)(2,1)S(1)}, u32[]{:S(2)}, u32[]{:S(2)}) %collective-permute-start.5) | collective-permute-done | bytes 262176 | tf_op jit(solution)/shard_map/ppermute | solution.py:188
  68.9 0.5 collective-permute-start.7
  69.5 0.8 collective-permute-done.9.refs_9_.refs_10_.refs_11_.refs_12_.refs_13_.refs_14_.refs_15_.refs_16_.refs_1_
  70.3 2.9 %low.5.refs_4_ = f32[168,128]{1,0:T(8,128)S(1)} custom-call(s32[1]{0:T(128)} %bitcast.me_ref, s32[7]{0:T(128)S(1)} %copy-done.2, s32[7]{0:T(128)S(1)} %copy-done.4, bf16[168,2048]{1,0:T(8,128)(2,1)S(1)} %collective-permute-done.8.refs_0_.refs_1_.refs_2_.refs_3_.refs_4_.refs_5_.refs_6_.refs_7_.refs_8_, ...), custom_call_target="tpu_custom_call" | custom-call | flops 2466250752 | bytes 9633792 | tf_op jit(solution)/shard_map/low/pallas_call | solution.py:243
  73.2 3.4 %collective-permute-done.7.refs_3_.refs_20_ = bf16[128,1024]{1,0:T(8,128)(2,1)S(1)} collective-permute-done((bf16[128,1024]{1,0:T(8,128)(2,1)S(1)}, bf16[128,1024]{1,0:T(8,128)(2,1)S(1)}, u32[]{:S(2)}, u32[]{:S(2)}) %collective-permute-start.7) | collective-permute-done | bytes 262176 | tf_op jit(solution)/shard_map/ppermute | solution.py:188
  76.5 0.9 low.6.refs_1_
  77.5 1.3 %collective-permute-done.10.refs_2_ = f32[168,128]{1,0:T(8,128)S(1)} collective-permute-done((f32[168,128]{1,0:T(8,128)S(1)}, f32[168,128]{1,0:T(8,128)S(1)}, u32[]{:S(2)}, u32[]{:S(2)}) %collective-permute-start.10) | collective-permute-done | bytes 86048 | tf_op jit(solution)/shard_map/ppermute | solution.py:191
  78.8 1.4 %up.2 = bf16[168,512]{1,0:T(8,128)(2,1)S(1)} custom-call(s32[1]{0:T(128)} %bitcast.me_ref, s32[7]{0:T(128)S(1)} %copy-done.2, s32[7]{0:T(128)S(1)} %copy-done.4, bf16[168,2048]{1,0:T(8,128)(2,1)S(1)} %collective-permute-done.8.refs_0_.refs_1_.refs_2_.refs_3_.refs_4_.refs_5_.refs_6_.refs_7_.refs_8_, f32[168,128]{1,0:T(8,128)S(1)} %low.6.refs_1_, ...), custom_call_target="tpu_custom_call" | custom-call | tf_op jit(solution)/shard_map/up/pallas_call | solution.py:281
  80.2 2.3 %collective-permute-start.12 = (bf16[168,512]{1,0:T(8,128)(2,1)S(1)}, bf16[168,512]{1,0:T(8,128)(2,1)S(1)}, u32[]{:S(2)}, u32[]{:S(2)}) collective-permute-start(bf16[168,512]{1,0:T(8,128)(2,1)S(1)} %up.2), channel_id=1, source_target_pairs={{0,4},{2,6},{4,0},{6,2},{8,12},{10,14},{12,8},{14,10},{1,5},{3,7},... | collective-permute-start | bytes 516104 | tf_op jit(solution)/shard_map/ppermute | solution.py:188
  82.5 2.7 %low.7.refs_0_ = f32[256,128]{1,0:T(8,128)S(1)} custom-call(s32[1]{0:T(128)} %bitcast.me_ref, s32[7]{0:T(128)S(1)} %copy-done.2, s32[7]{0:T(128)S(1)} %copy-done.4, bf16[256,4096]{1,0:T(8,128)(2,1)} %refs_15_.3, bf16[256,4096]{1,0:T(8,128)(2,1)} %refs_15_.3, bf16[256,4096]{1,0:T(8,128)(2,1)} %refs_15_.3, bf16[256,4096]{1,0:T(8,128)(2,1)} %refs_15_.3, ...), custom_call_target="tpu_custom_call" | custom-call | flops 1677721600 | bytes 6553600 | tf_op jit(solution)/shard_map/low/pallas_call | solution.py:243
  85.3 1.3 %collective-permute-done.11.refs_1_ = f32[256,128]{1,0:T(8,128)S(1)} collective-permute-done((f32[256,128]{1,0:T(8,128)S(1)}, f32[256,128]{1,0:T(8,128)S(1)}, u32[]{:S(2)}, u32[]{:S(2)}) %collective-permute-start.11) | collective-permute-done | bytes 131104 | tf_op jit(solution)/shard_map/ppermute | solution.py:191
  86.7 1.5 %up.3.sum_ref = f32[256,512]{1,0:T(8,128)S(1)} custom-call(s32[1]{0:T(128)} %bitcast.me_ref, s32[7]{0:T(128)S(1)} %copy-done.2, s32[7]{0:T(128)S(1)} %copy-done.4, f32[256,128]{1,0:T(8,128)S(1)} %low.7.refs_0_, f32[256,128]{1,0:T(8,128)S(1)} %collective-permute-done.11.refs_1_, bf16[128,4608]{1,0:T(8,128)(2,1)S(1)} %get-tuple-element.22.refs_16_.refs_17_.refs_3_.refs_2_, ...), custom_call_target="tpu_custom_call" | custom-call | tf_op jit(solution)/shard_map/up/pallas_call | solution.py:281
  88.2 1.6 %last.1 = bf16[256,512]{1,0:T(8,128)(2,1)} custom-call(s32[1]{0:T(128)} %bitcast.me_ref, s32[7]{0:T(128)S(1)} %copy-done.2, s32[7]{0:T(128)S(1)} %copy-done.4, f32[256,512]{1,0:T(8,128)S(1)} %up.3.sum_ref, bf16[168,512]{1,0:T(8,128)(2,1)S(1)} %collective-permute-done.12.back_ref), custom_call_target="tpu_custom_call" | custom-call | tf_op jit(solution)/shard_map/last/pallas_call | solution.py:300
  (20 shorter events, 0.2 us)
Async XLA Ops:
  0.0 0.9 %copy-start = (bf16[2,64,1024]{2,1,0:T(8,128)(2,1)S(1)}, bf16[2,64,1024]{2,1,0:T(8,128)(2,1)}, u32[]{:S(2)}) copy-start(bf16[2,64,1024]{2,1,0:T(8,128)(2,1)} %param.9) | copy-start | bytes 786436
  1.0 0.7 copy-start.1
  1.6 0.7 copy-start.3
  6.3 0.9 copy-start.5
  7.2 0.7 copy-start.6
  7.9 5.9 %collective-permute-start.6 = (bf16[256,4096]{1,0:T(8,128)(2,1)}, bf16[256,4096]{1,0:T(8,128)(2,1)}, u32[]{:S(2)}, u32[]{:S(2)}) collective-permute-start(bf16[256,4096]{1,0:T(8,128)(2,1)} %refs_15_.3), channel_id=1, source_target_pairs={{0,1},{1,0},{2,3},{3,2},{4,5},{5,4},{6,7},{7,6},{8,9},{9,8},{10,11... | collective-permute-start | bytes 6291464 | tf_op jit(solution)/shard_map/ppermute | solution.py:191
  8.4 39.5 %collective-permute-start.3 = (bf16[128,4608]{1,0:T(8,128)(2,1)S(1)}, bf16[128,4608]{1,0:T(8,128)(2,1)}, u32[]{:S(2)}, u32[]{:S(2)}) collective-permute-start(bf16[128,4608]{1,0:T(8,128)(2,1)S(1)} %get-tuple-element.22.refs_16_.refs_17_.refs_3_.refs_2_), channel_id=1, source_target_pairs={{0,2},{2,0},{4,6},{6,4},{8,10},{10,8},{12,14},{14,12},{1,3},{3,1},... | collective-permute-start | bytes 3538952 | tf_op jit(solution)/shard_map/ppermute | solution.py:188
  10.8 37.0 %collective-permute-start = (bf16[128,2304]{1,0:T(8,128)(2,1)}, bf16[128,2304]{1,0:T(8,128)(2,1)S(1)}, u32[]{:S(2)}, u32[]{:S(2)}) collective-permute-start(bf16[128,2304]{1,0:T(8,128)(2,1)} %get-tuple-element.19), channel_id=1, source_target_pairs={{0,8},{2,10},{4,12},{6,14},{8,0},{10,2},{12,4},{14,6},{1,9},{3,11}... | collective-permute-start | bytes 1769480 | tf_op jit(solution)/shard_map/ppermute | solution.py:188
  13.4 41.5 %collective-permute-start.2 = (bf16[128,1280]{1,0:T(8,128)(2,1)}, bf16[128,1280]{1,0:T(8,128)(2,1)S(1)}, u32[]{:S(2)}, u32[]{:S(2)}) collective-permute-start(bf16[128,1280]{1,0:T(8,128)(2,1)} %get-tuple-element.21), channel_id=1, source_target_pairs={{0,8},{2,10},{4,12},{6,14},{8,0},{10,2},{12,4},{14,6},{1,9},{3,11}... | collective-permute-start | bytes 983048 | tf_op jit(solution)/shard_map/ppermute | solution.py:188
  13.8 34.3 %copy-start.2 = (s32[7]{0:T(128)S(1)}, s32[7]{0:T(128)}, u32[]{:S(2)}) copy-start(s32[7]{0:T(128)} %len_ref.15) | copy-start | bytes 88
  13.8 34.3 %copy-start.4 = (s32[7]{0:T(128)S(1)}, s32[7]{0:T(128)}, u32[]{:S(2)}) copy-start(s32[7]{0:T(128)} %id_ref.15) | copy-start | bytes 88
  13.8 55.7 %collective-permute-start.8 = (bf16[168,2048]{1,0:T(8,128)(2,1)}, bf16[168,2048]{1,0:T(8,128)(2,1)S(1)}, u32[]{:S(2)}, u32[]{:S(2)}) collective-permute-start(bf16[168,2048]{1,0:T(8,128)(2,1)} %get-tuple-element.29), channel_id=1, source_target_pairs={{0,4},{2,6},{4,0},{6,2},{8,12},{10,14},{12,8},{14,10},{1,5},{3,7},... | collective-permute-start | bytes 2064392 | tf_op jit(solution)/shard_map/ppermute | solution.py:188
  15.4 54.9 %collective-permute-start.9 = (bf16[168,2048]{1,0:T(8,128)(2,1)}, bf16[168,2048]{1,0:T(8,128)(2,1)S(1)}, u32[]{:S(2)}, u32[]{:S(2)}) collective-permute-start(bf16[168,2048]{1,0:T(8,128)(2,1)} %copy-done.5), channel_id=1, source_target_pairs={{0,4},{2,6},{4,0},{6,2},{8,12},{10,14},{12,8},{14,10},{1,5},{3,7},... | collective-permute-start | bytes 2064392 | tf_op jit(solution)/shard_map/ppermute | solution.py:188
  47.9 21.0 %collective-permute-start.5 = (bf16[128,1024]{1,0:T(8,128)(2,1)}, bf16[128,1024]{1,0:T(8,128)(2,1)S(1)}, u32[]{:S(2)}, u32[]{:S(2)}) collective-permute-start(bf16[128,1024]{1,0:T(8,128)(2,1)} %copy-done.6), channel_id=1, source_target_pairs={{0,8},{2,10},{4,12},{6,14},{8,0},{10,2},{12,4},{14,6},{1,9},{3,11}... | collective-permute-start | bytes 786440 | tf_op jit(solution)/shard_map/ppermute | solution.py:188
  47.9 21.6 %collective-permute-start.1 = (bf16[128,2304]{1,0:T(8,128)(2,1)S(1)}, bf16[128,2304]{1,0:T(8,128)(2,1)S(1)}, u32[]{:S(2)}, u32[]{:S(2)}) collective-permute-start(bf16[128,2304]{1,0:T(8,128)(2,1)S(1)} %collective-permute-done.refs_18_.refs_19_.refs_4_.refs_3_), channel_id=1, source_target_pairs={{0,2},{2,0},{4,6},{6,4},{8,10},{10,8},{12,14},{14,12},{1,3},{3,1},... | collective-permute-start | bytes 1769480 | tf_op jit(solution)/shard_map/ppermute | solution.py:188
  48.1 7.0 %copy-start.7 = (f32[256,512]{1,0:T(8,128)S(1)}, f32[256,512]{1,0:T(8,128)}, u32[]{:S(2)}) copy-start(f32[256,512]{1,0:T(8,128)} %fusion.4) | copy-start | bytes 1572868
  54.9 14.5 %collective-permute-start.4 = (bf16[128,1280]{1,0:T(8,128)(2,1)S(1)}, bf16[128,1280]{1,0:T(8,128)(2,1)S(1)}, u32[]{:S(2)}, u32[]{:S(2)}) collective-permute-start(bf16[128,1280]{1,0:T(8,128)(2,1)S(1)} %collective-permute-done.2.refs_21_.refs_17_), channel_id=1, source_target_pairs={{0,2},{2,0},{4,6},{6,4},{8,10},{10,8},{12,14},{14,12},{1,3},{3,1},... | collective-permute-start | bytes 983048 | tf_op jit(solution)/shard_map/ppermute | solution.py:188
  68.9 7.6 %collective-permute-start.7 = (bf16[128,1024]{1,0:T(8,128)(2,1)S(1)}, bf16[128,1024]{1,0:T(8,128)(2,1)S(1)}, u32[]{:S(2)}, u32[]{:S(2)}) collective-permute-start(bf16[128,1024]{1,0:T(8,128)(2,1)S(1)} %collective-permute-done.5.refs_2_.refs_19_), channel_id=1, source_target_pairs={{0,2},{2,0},{4,6},{6,4},{8,10},{10,8},{12,14},{14,12},{1,3},{3,1},... | collective-permute-start | bytes 786440 | tf_op jit(solution)/shard_map/ppermute | solution.py:188
  77.4 1.3 %collective-permute-start.10 = (f32[168,128]{1,0:T(8,128)S(1)}, f32[168,128]{1,0:T(8,128)S(1)}, u32[]{:S(2)}, u32[]{:S(2)}) collective-permute-start(f32[168,128]{1,0:T(8,128)S(1)} %low.6.refs_1_), channel_id=1, source_target_pairs={{0,1},{1,0},{2,3},{3,2},{4,5},{5,4},{6,7},{7,6},{8,9},{9,8},{10,11... | collective-permute-start | bytes 258056 | tf_op jit(solution)/shard_map/ppermute | solution.py:191
  80.2 8.0 %collective-permute-start.12 = (bf16[168,512]{1,0:T(8,128)(2,1)S(1)}, bf16[168,512]{1,0:T(8,128)(2,1)S(1)}, u32[]{:S(2)}, u32[]{:S(2)}) collective-permute-start(bf16[168,512]{1,0:T(8,128)(2,1)S(1)} %up.2), channel_id=1, source_target_pairs={{0,4},{2,6},{4,0},{6,2},{8,12},{10,14},{12,8},{14,10},{1,5},{3,7},... | collective-permute-start | bytes 516104 | tf_op jit(solution)/shard_map/ppermute | solution.py:188
  85.3 1.4 %collective-permute-start.11 = (f32[256,128]{1,0:T(8,128)S(1)}, f32[256,128]{1,0:T(8,128)S(1)}, u32[]{:S(2)}, u32[]{:S(2)}) collective-permute-start(f32[256,128]{1,0:T(8,128)S(1)} %low.7.refs_0_), channel_id=1, source_target_pairs={{0,1},{1,0},{2,3},{3,2},{4,5},{5,4},{6,7},{7,6},{8,9},{9,8},{10,11... | collective-permute-start | bytes 393224 | tf_op jit(solution)/shard_map/ppermute | solution.py:191

commit v4 on v3

--- a/solution.py
+++ b/solution.py
@@ -204,7 +204,7 @@
         out_specs=[pl.BlockSpec((slots, half // halves), lambda *_: (0, 0))] * halves
         + [pl.BlockSpec((both, w), lambda *_: (0, 0)) for w in widths],
         scratch_shapes=[pltpu.SemaphoreType.DMA((len(spans) + 3,))],
-        compiler_params=params,
+        compiler_params=pltpu.CompilerParams(vmem_limit_bytes=60 * 1024 * 1024),
         name="start",
     )(lengths, adapter_ids, tokens, jnp.transpose(down_a, (0, 2, 1)).reshape(both, width), up_weight.reshape(both, -1))
     sent, parts = outs[:halves], outs[halves:]

time: 90.1 us -> 87.5 us (0.971)
  local copies, waits for them, and re-layouts: 3.82 us -> 1.29 us
    unnamed x16 -> x12, local copies, waits for them, and re-layouts: 3.82 us -> 1.29 us
    pallas_call x1, Pallas kernels: 4.08 us -> 5.19 us  [shards(): pl.pallas_call(functools.partial(start_kernel, adapt_dev, spans, up_chunk...]
  transfers between devices with their start and end apart: 13 -> 13, of which waited for: 7 -> 7; matrix products, arithmetic and copies ran while one was open for 10% -> 9% of each run, Pallas kernels for 12% -> 11%
where the time goes in v4:
time: 87.5 us; the launch traced here: 87.2 us
  waiting for transfers between devices  46.6 us (53%)
  Pallas kernels  19.1 us (22%)
  starting transfers between devices  11.8 us (13%)
  matrix products  8.28 us (9%)
  local copies, waits for them, and re-layouts  1.29 us (1%)
    ppermute x10, waiting for transfers between devices, flip(): return lax.ppermute(x, 'adapter', [(j, j ^ bit) for j in range(owners)])  44 us
    ppermute x10, starting transfers between devices, flip(): return lax.ppermute(x, 'adapter', [(j, j ^ bit) for j in range(owners)])  11.1 us
    pallas_call x4, Pallas kernels, add_low(): pl.pallas_call(functools.partial(low_kernel, adapt_dev, rank, plan, block...  9.35 us
    dot_general x2, matrix products, dot(): lax.dot_general(left, right, ((contract[:1], contract[1:]), ((), ())), pr...  8.28 us
    pallas_call x1, Pallas kernels, shards(): pl.pallas_call(functools.partial(start_kernel, adapt_dev, spans, up_chunk...  5.19 us
    pallas_call x2, Pallas kernels, up(): pl.pallas_call(functools.partial(up_kernel, adapt_dev, list(pieces), len(...  2.97 us
    ppermute x3, waiting for transfers between devices, other_core(): return lax.ppermute(x, 'tensor', [(0, 1), (1, 0)])  2.61 us
  transfers between devices with their start and end apart: 13, of which 7 were waited for; matrix products, arithmetic and copies ran while one was open for 9% of the time, Pallas kernels for 11%

profile of v4, /device:TPU:0, one launch (start us, length us, event | category | flops | bytes accessed | tf_op | source)
XLA Modules:
  0.0 87.2 jit_solution(10497838928664270573)
XLA Ops:
  0.0 5.2 %start.1 = (bf16[168,2048]{1,0:T(8,128)(2,1)}, bf16[168,2048]{1,0:T(8,128)(2,1)}, bf16[128,2304]{1,0:T(8,128)(2,1)}, bf16[128,1280]{1,0:T(8,128)(2,1)}, bf16[128...) custom-call(s32[7]{0:T(128)} %len_ref.15, s32[7]{0:T(128)} %id_ref.15, bf16[256,4096]{1,0:T(8,128)(2,1)} %refs_15_.3, ...), custom_call_target="tpu_custom_call" | custom-call | tf_op jit(solution)/shard_map/start/pallas_call | solution.py:197
  5.2 0.5 collective-permute-start.6
  5.7 2.6 %collective-permute-start.3 = (bf16[128,4608]{1,0:T(8,128)(2,1)}, bf16[128,4608]{1,0:T(8,128)(2,1)}, u32[]{:S(2)}, u32[]{:S(2)}) collective-permute-start(bf16[128,4608]{1,0:T(8,128)(2,1)} %get-tuple-element.22.refs_16_.refs_17_.refs_3_.refs_2_), channel_id=1, source_target_pairs={{0,2},{2,0},{4,6},{6,4},{8,10},{10,8},{12,14},{14,12},{1,3},{3,1},... | collective-permute-start | bytes 3538952 | tf_op jit(solution)/shard_map/ppermute | solution.py:188
  8.3 2.6 %collective-permute-start = (bf16[128,2304]{1,0:T(8,128)(2,1)}, bf16[128,2304]{1,0:T(8,128)(2,1)}, u32[]{:S(2)}, u32[]{:S(2)}) collective-permute-start(bf16[128,2304]{1,0:T(8,128)(2,1)} %get-tuple-element.19), channel_id=1, source_target_pairs={{0,8},{2,10},{4,12},{6,14},{8,0},{10,2},{12,4},{14,6},{1,9},{3,11}... | collective-permute-start | bytes 1769480 | tf_op jit(solution)/shard_map/ppermute | solution.py:188
  10.9 0.3 collective-permute-start.2
  11.2 0.0 collective-permute-done.6
  11.2 1.6 %collective-permute-start.8 = (bf16[168,2048]{1,0:T(8,128)(2,1)}, bf16[168,2048]{1,0:T(8,128)(2,1)S(1)}, u32[]{:S(2)}, u32[]{:S(2)}) collective-permute-start(bf16[168,2048]{1,0:T(8,128)(2,1)} %get-tuple-element.29), channel_id=1, source_target_pairs={{0,4},{2,6},{4,0},{6,2},{8,12},{10,14},{12,8},{14,10},{1,5},{3,7},... | collective-permute-start | bytes 2064392 | tf_op jit(solution)/shard_map/ppermute | solution.py:188
  12.8 0.4 collective-permute-start.9
  13.3 4.2 %fusion.4 = f32[256,512]{1,0:T(8,128)} fusion(bf16[256,4096]{1,0:T(8,128)(2,1)S(1)} %copy-done, bf16[8192,512]{1,0:T(8,128)(2,1)} %param.7, s32[]{:T(128)S(6)} %select_n.6), kind=kOutput, calls=%fused_computation.4 | convolution fusion | flops 1073741824 | bytes 6815748 | tf_op jit(solution)/shard_map/dot_general | solution.py:24
  17.5 28.0 %collective-permute-done.refs_18_.refs_19_.refs_4_.refs_3_ = bf16[128,2304]{1,0:T(8,128)(2,1)} collective-permute-done((bf16[128,2304]{1,0:T(8,128)(2,1)}, bf16[128,2304]{1,0:T(8,128)(2,1)}, u32[]{:S(2)}, u32[]{:S(2)}) %collective-permute-start) | collective-permute-done | bytes 589856 | tf_op jit(solution)/shard_map/ppermute | solution.py:188
  45.5 0.2 collective-permute-start.1
  45.6 1.3 %copy-done.1 = bf16[128,4608]{1,0:T(8,128)(2,1)S(1)} copy-done((bf16[128,4608]{1,0:T(8,128)(2,1)S(1)}, bf16[128,4608]{1,0:T(8,128)(2,1)}, u32[]{:S(2)}) %copy-start.1) | copy-done | bytes 1179672
  46.9 3.1 %low.4.refs_21_ = f32[256,128]{1,0:T(8,128)S(1)} custom-call(s32[1]{0:T(128)} %bitcast.me_ref, s32[7]{0:T(128)S(1)} %copy-done.3, s32[7]{0:T(128)S(1)} %copy-done.4, bf16[256,4096]{1,0:T(8,128)(2,1)S(1)} %copy-done, bf16[256,4096]{1,0:T(8,128)(2,1)S(1)} %copy-done, bf16[256,4096]{1,0:T(8,128)(2,1)S(1)} %copy-done, bf16[256,4096]{1,0:T(8,128)(2,1)S(1)} %copy-done, ...), custom_call_target="tpu_custom_call" | custom-call | flops 2617245696 | bytes 10223616 | tf_op jit(solution)/shard_map/low/pallas_call | solution.py:243
  50.1 2.4 %collective-permute-done.2.refs_21_.refs_17_ = bf16[128,1280]{1,0:T(8,128)(2,1)} collective-permute-done((bf16[128,1280]{1,0:T(8,128)(2,1)}, bf16[128,1280]{1,0:T(8,128)(2,1)}, u32[]{:S(2)}, u32[]{:S(2)}) %collective-permute-start.2) | collective-permute-done | bytes 327712 | tf_op jit(solution)/shard_map/ppermute | solution.py:188
  52.5 0.2 collective-permute-start.4
  52.6 4.1 %fusion.7.refs_6_ = f32[256,512]{1,0:T(8,128)S(1)} fusion(f32[256,512]{1,0:T(8,128)S(1)} %copy-done.5, bf16[256,4096]{1,0:T(8,128)(2,1)} %collective-permute-done.6, bf16[8192,512]{1,0:T(8,128)(2,1)} %param.7, s32[]{:T(128)S(6)} %select_n.7), kind=kOutput, calls=%fused_computation.5 | convolution fusion | flops 1073872896 | bytes 7340036 | tf_op jit(solution)/shard_map/dot_general | solution.py:24
  56.7 9.6 %collective-permute-done.5.refs_2_.refs_19_ = bf16[128,1024]{1,0:T(8,128)(2,1)S(1)} collective-permute-done((bf16[128,1024]{1,0:T(8,128)(2,1)}, bf16[128,1024]{1,0:T(8,128)(2,1)S(1)}, u32[]{:S(2)}, u32[]{:S(2)}) %collective-permute-start.5) | collective-permute-done | bytes 262176 | tf_op jit(solution)/shard_map/ppermute | solution.py:188
  66.3 0.5 collective-permute-start.7
  66.8 0.0 collective-permute-done.1.refs_20_.refs_6_.refs_16_.refs_5_
  66.8 0.6 collective-permute-done.9.refs_9_.refs_10_.refs_11_.refs_12_.refs_13_.refs_14_.refs_15_.refs_16_.refs_1_
  67.5 3.0 %low.5.refs_4_ = f32[168,128]{1,0:T(8,128)S(1)} custom-call(s32[1]{0:T(128)} %bitcast.me_ref, s32[7]{0:T(128)S(1)} %copy-done.3, s32[7]{0:T(128)S(1)} %copy-done.4, bf16[168,2048]{1,0:T(8,128)(2,1)S(1)} %collective-permute-done.8.refs_0_.refs_1_.refs_2_.refs_3_.refs_4_.refs_5_.refs_6_.refs_7_.refs_8_, ...), custom_call_target="tpu_custom_call" | custom-call | flops 2466250752 | bytes 9633792 | tf_op jit(solution)/shard_map/low/pallas_call | solution.py:243
  70.5 3.4 %collective-permute-done.7.refs_3_.refs_20_ = bf16[128,1024]{1,0:T(8,128)(2,1)S(1)} collective-permute-done((bf16[128,1024]{1,0:T(8,128)(2,1)S(1)}, bf16[128,1024]{1,0:T(8,128)(2,1)S(1)}, u32[]{:S(2)}, u32[]{:S(2)}) %collective-permute-start.7) | collective-permute-done | bytes 262176 | tf_op jit(solution)/shard_map/ppermute | solution.py:188
  73.8 0.9 %low.6.refs_1_ = f32[168,128]{1,0:T(8,128)S(1)} custom-call(s32[1]{0:T(128)} %bitcast.me_ref, s32[7]{0:T(128)S(1)} %copy-done.3, s32[7]{0:T(128)S(1)} %copy-done.4, bf16[168,2048]{1,0:T(8,128)(2,1)S(1)} %collective-permute-done.8.refs_0_.refs_1_.refs_2_.refs_3_.refs_4_.refs_5_.refs_6_.refs_7_.refs_8_, ...), custom_call_target="tpu_custom_call" | custom-call | flops 352321536 | bytes 1376256 | tf_op jit(solution)/shard_map/low/pallas_call | solution.py:243
  74.7 0.1 collective-permute-start.10
  74.8 1.3 %collective-permute-done.10.refs_2_ = f32[168,128]{1,0:T(8,128)S(1)} collective-permute-done((f32[168,128]{1,0:T(8,128)S(1)}, f32[168,128]{1,0:T(8,128)S(1)}, u32[]{:S(2)}, u32[]{:S(2)}) %collective-permute-start.10) | collective-permute-done | bytes 86048 | tf_op jit(solution)/shard_map/ppermute | solution.py:191
  76.1 1.4 %up.2 = bf16[168,512]{1,0:T(8,128)(2,1)S(1)} custom-call(s32[1]{0:T(128)} %bitcast.me_ref, s32[7]{0:T(128)S(1)} %copy-done.3, s32[7]{0:T(128)S(1)} %copy-done.4, bf16[168,2048]{1,0:T(8,128)(2,1)S(1)} %collective-permute-done.8.refs_0_.refs_1_.refs_2_.refs_3_.refs_4_.refs_5_.refs_6_.refs_7_.refs_8_, f32[168,128]{1,0:T(8,128)S(1)} %low.6.refs_1_, ...), custom_call_target="tpu_custom_call" | custom-call | tf_op jit(solution)/shard_map/up/pallas_call | solution.py:281
  77.5 2.7 %collective-permute-start.12 = (bf16[168,512]{1,0:T(8,128)(2,1)S(1)}, bf16[168,512]{1,0:T(8,128)(2,1)S(1)}, u32[]{:S(2)}, u32[]{:S(2)}) collective-permute-start(bf16[168,512]{1,0:T(8,128)(2,1)S(1)} %up.2), channel_id=1, source_target_pairs={{0,4},{2,6},{4,0},{6,2},{8,12},{10,14},{12,8},{14,10},{1,5},{3,7},... | collective-permute-start | bytes 516104 | tf_op jit(solution)/shard_map/ppermute | solution.py:188
  80.3 2.3 %low.7.refs_0_ = f32[256,128]{1,0:T(8,128)S(1)} custom-call(s32[1]{0:T(128)} %bitcast.me_ref, s32[7]{0:T(128)S(1)} %copy-done.3, s32[7]{0:T(128)S(1)} %copy-done.4, bf16[256,4096]{1,0:T(8,128)(2,1)S(1)} %copy-done, bf16[256,4096]{1,0:T(8,128)(2,1)S(1)} %copy-done, bf16[256,4096]{1,0:T(8,128)(2,1)S(1)} %copy-done, bf16[256,4096]{1,0:T(8,128)(2,1)S(1)} %copy-done, ...), custom_call_target="tpu_custom_call" | custom-call | flops 1677721600 | bytes 6553600 | tf_op jit(solution)/shard_map/low/pallas_call | solution.py:243
  82.6 0.1 collective-permute-start.11
  82.7 1.3 %collective-permute-done.11.refs_1_ = f32[256,128]{1,0:T(8,128)S(1)} collective-permute-done((f32[256,128]{1,0:T(8,128)S(1)}, f32[256,128]{1,0:T(8,128)S(1)}, u32[]{:S(2)}, u32[]{:S(2)}) %collective-permute-start.11) | collective-permute-done | bytes 131104 | tf_op jit(solution)/shard_map/ppermute | solution.py:191
  84.0 1.6 %up.3.sum_ref = f32[256,512]{1,0:T(8,128)S(1)} custom-call(s32[1]{0:T(128)} %bitcast.me_ref, s32[7]{0:T(128)S(1)} %copy-done.3, s32[7]{0:T(128)S(1)} %copy-done.4, f32[256,128]{1,0:T(8,128)S(1)} %low.7.refs_0_, f32[256,128]{1,0:T(8,128)S(1)} %collective-permute-done.11.refs_1_, bf16[128,4608]{1,0:T(8,128)(2,1)S(1)} %copy-done.2, ...), custom_call_target="tpu_custom_call" | custom-call | tf_op jit(solution)/shard_map/up/pallas_call | solution.py:281
  85.6 1.6 %last.1 = bf16[256,512]{1,0:T(8,128)(2,1)} custom-call(s32[1]{0:T(128)} %bitcast.me_ref, s32[7]{0:T(128)S(1)} %copy-done.3, s32[7]{0:T(128)S(1)} %copy-done.4, f32[256,512]{1,0:T(8,128)S(1)} %up.3.sum_ref, bf16[168,512]{1,0:T(8,128)(2,1)S(1)} %collective-permute-done.12.back_ref), custom_call_target="tpu_custom_call" | custom-call | tf_op jit(solution)/shard_map/last/pallas_call | solution.py:300
  (16 shorter events, 0.0 us)
Async XLA Ops:
  0.0 5.2 %copy-start = (bf16[256,4096]{1,0:T(8,128)(2,1)S(1)}, bf16[256,4096]{1,0:T(8,128)(2,1)}, u32[]{:S(2)}) copy-start(bf16[256,4096]{1,0:T(8,128)(2,1)} %refs_15_.3) | copy-start | bytes 6291460
  5.2 6.0 %collective-permute-start.6 = (bf16[256,4096]{1,0:T(8,128)(2,1)S(1)}, bf16[256,4096]{1,0:T(8,128)(2,1)}, u32[]{:S(2)}, u32[]{:S(2)}) collective-permute-start(bf16[256,4096]{1,0:T(8,128)(2,1)S(1)} %copy-done), channel_id=1, source_target_pairs={{0,1},{1,0},{2,3},{3,2},{4,5},{5,4},{6,7},{7,6},{8,9},{9,8},{10,11... | collective-permute-start | bytes 6291464 | tf_op jit(solution)/shard_map/ppermute | solution.py:191
  5.7 39.7 %collective-permute-start.3 = (bf16[128,4608]{1,0:T(8,128)(2,1)}, bf16[128,4608]{1,0:T(8,128)(2,1)}, u32[]{:S(2)}, u32[]{:S(2)}) collective-permute-start(bf16[128,4608]{1,0:T(8,128)(2,1)} %get-tuple-element.22.refs_16_.refs_17_.refs_3_.refs_2_), channel_id=1, source_target_pairs={{0,2},{2,0},{4,6},{6,4},{8,10},{10,8},{12,14},{14,12},{1,3},{3,1},... | collective-permute-start | bytes 3538952 | tf_op jit(solution)/shard_map/ppermute | solution.py:188
  8.3 37.1 %collective-permute-start = (bf16[128,2304]{1,0:T(8,128)(2,1)}, bf16[128,2304]{1,0:T(8,128)(2,1)}, u32[]{:S(2)}, u32[]{:S(2)}) collective-permute-start(bf16[128,2304]{1,0:T(8,128)(2,1)} %get-tuple-element.19), channel_id=1, source_target_pairs={{0,8},{2,10},{4,12},{6,14},{8,0},{10,2},{12,4},{14,6},{1,9},{3,11}... | collective-permute-start | bytes 1769480 | tf_op jit(solution)/shard_map/ppermute | solution.py:188
  10.9 41.6 %collective-permute-start.2 = (bf16[128,1280]{1,0:T(8,128)(2,1)}, bf16[128,1280]{1,0:T(8,128)(2,1)}, u32[]{:S(2)}, u32[]{:S(2)}) collective-permute-start(bf16[128,1280]{1,0:T(8,128)(2,1)} %get-tuple-element.21), channel_id=1, source_target_pairs={{0,8},{2,10},{4,12},{6,14},{8,0},{10,2},{12,4},{14,6},{1,9},{3,11}... | collective-permute-start | bytes 983048 | tf_op jit(solution)/shard_map/ppermute | solution.py:188
  11.2 34.4 %copy-start.3 = (s32[7]{0:T(128)S(1)}, s32[7]{0:T(128)}, u32[]{:S(2)}) copy-start(s32[7]{0:T(128)} %len_ref.15) | copy-start | bytes 88
  11.2 34.4 %copy-start.4 = (s32[7]{0:T(128)S(1)}, s32[7]{0:T(128)}, u32[]{:S(2)}) copy-start(s32[7]{0:T(128)} %id_ref.15) | copy-start | bytes 88
  11.2 55.6 %collective-permute-start.8 = (bf16[168,2048]{1,0:T(8,128)(2,1)}, bf16[168,2048]{1,0:T(8,128)(2,1)S(1)}, u32[]{:S(2)}, u32[]{:S(2)}) collective-permute-start(bf16[168,2048]{1,0:T(8,128)(2,1)} %get-tuple-element.29), channel_id=1, source_target_pairs={{0,4},{2,6},{4,0},{6,2},{8,12},{10,14},{12,8},{14,10},{1,5},{3,7},... | collective-permute-start | bytes 2064392 | tf_op jit(solution)/shard_map/ppermute | solution.py:188
  12.8 54.6 %collective-permute-start.9 = (bf16[168,2048]{1,0:T(8,128)(2,1)}, bf16[168,2048]{1,0:T(8,128)(2,1)S(1)}, u32[]{:S(2)}, u32[]{:S(2)}) collective-permute-start(bf16[168,2048]{1,0:T(8,128)(2,1)} %get-tuple-element.31), channel_id=1, source_target_pairs={{0,4},{2,6},{4,0},{6,2},{8,12},{10,14},{12,8},{14,10},{1,5},{3,7},... | collective-permute-start | bytes 2064392 | tf_op jit(solution)/shard_map/ppermute | solution.py:188
  45.5 20.8 %collective-permute-start.5 = (bf16[128,1024]{1,0:T(8,128)(2,1)}, bf16[128,1024]{1,0:T(8,128)(2,1)S(1)}, u32[]{:S(2)}, u32[]{:S(2)}) collective-permute-start(bf16[128,1024]{1,0:T(8,128)(2,1)} %get-tuple-element.25), channel_id=1, source_target_pairs={{0,8},{2,10},{4,12},{6,14},{8,0},{10,2},{12,4},{14,6},{1,9},{3,11}... | collective-permute-start | bytes 786440 | tf_op jit(solution)/shard_map/ppermute | solution.py:188
  45.5 21.4 %collective-permute-start.1 = (bf16[128,2304]{1,0:T(8,128)(2,1)}, bf16[128,2304]{1,0:T(8,128)(2,1)S(1)}, u32[]{:S(2)}, u32[]{:S(2)}) collective-permute-start(bf16[128,2304]{1,0:T(8,128)(2,1)} %collective-permute-done.refs_18_.refs_19_.refs_4_.refs_3_), channel_id=1, source_target_pairs={{0,2},{2,0},{4,6},{6,4},{8,10},{10,8},{12,14},{14,12},{1,3},{3,1},... | collective-permute-start | bytes 1769480 | tf_op jit(solution)/shard_map/ppermute | solution.py:188
  45.6 1.3 %copy-start.1 = (bf16[128,4608]{1,0:T(8,128)(2,1)S(1)}, bf16[128,4608]{1,0:T(8,128)(2,1)}, u32[]{:S(2)}) copy-start(bf16[128,4608]{1,0:T(8,128)(2,1)} %get-tuple-element.22.refs_16_.refs_17_.refs_3_.refs_2_) | copy-start | bytes 3538948
  46.9 5.7 %copy-start.5 = (f32[256,512]{1,0:T(8,128)S(1)}, f32[256,512]{1,0:T(8,128)}, u32[]{:S(2)}) copy-start(f32[256,512]{1,0:T(8,128)} %fusion.4) | copy-start | bytes 1572868
  52.5 14.4 %collective-permute-start.4 = (bf16[128,1280]{1,0:T(8,128)(2,1)}, bf16[128,1280]{1,0:T(8,128)(2,1)S(1)}, u32[]{:S(2)}, u32[]{:S(2)}) collective-permute-start(bf16[128,1280]{1,0:T(8,128)(2,1)} %collective-permute-done.2.refs_21_.refs_17_), channel_id=1, source_target_pairs={{0,2},{2,0},{4,6},{6,4},{8,10},{10,8},{12,14},{14,12},{1,3},{3,1},... | collective-permute-start | bytes 983048 | tf_op jit(solution)/shard_map/ppermute | solution.py:188
  66.3 7.5 %collective-permute-start.7 = (bf16[128,1024]{1,0:T(8,128)(2,1)S(1)}, bf16[128,1024]{1,0:T(8,128)(2,1)S(1)}, u32[]{:S(2)}, u32[]{:S(2)}) collective-permute-start(bf16[128,1024]{1,0:T(8,128)(2,1)S(1)} %collective-permute-done.5.refs_2_.refs_19_), channel_id=1, source_target_pairs={{0,2},{2,0},{4,6},{6,4},{8,10},{10,8},{12,14},{14,12},{1,3},{3,1},... | collective-permute-start | bytes 786440 | tf_op jit(solution)/shard_map/ppermute | solution.py:188
  70.5 5.6 %copy-start.2 = (bf16[128,4608]{1,0:T(8,128)(2,1)S(1)}, bf16[128,4608]{1,0:T(8,128)(2,1)}, u32[]{:S(2)}) copy-start(bf16[128,4608]{1,0:T(8,128)(2,1)} %get-tuple-element.22.refs_16_.refs_17_.refs_3_.refs_2_) | copy-start | bytes 3538948
  74.7 1.3 %collective-permute-start.10 = (f32[168,128]{1,0:T(8,128)S(1)}, f32[168,128]{1,0:T(8,128)S(1)}, u32[]{:S(2)}, u32[]{:S(2)}) collective-permute-start(f32[168,128]{1,0:T(8,128)S(1)} %low.6.refs_1_), channel_id=1, source_target_pairs={{0,1},{1,0},{2,3},{3,2},{4,5},{5,4},{6,7},{7,6},{8,9},{9,8},{10,11... | collective-permute-start | bytes 258056 | tf_op jit(solution)/shard_map/ppermute | solution.py:191
  77.5 8.0 %collective-permute-start.12 = (bf16[168,512]{1,0:T(8,128)(2,1)S(1)}, bf16[168,512]{1,0:T(8,128)(2,1)S(1)}, u32[]{:S(2)}, u32[]{:S(2)}) collective-permute-start(bf16[168,512]{1,0:T(8,128)(2,1)S(1)} %up.2), channel_id=1, source_target_pairs={{0,4},{2,6},{4,0},{6,2},{8,12},{10,14},{12,8},{14,10},{1,5},{3,7},... | collective-permute-start | bytes 516104 | tf_op jit(solution)/shard_map/ppermute | solution.py:188
  82.6 1.4 %collective-permute-start.11 = (f32[256,128]{1,0:T(8,128)S(1)}, f32[256,128]{1,0:T(8,128)S(1)}, u32[]{:S(2)}, u32[]{:S(2)}) collective-permute-start(f32[256,128]{1,0:T(8,128)S(1)} %low.7.refs_0_), channel_id=1, source_target_pairs={{0,1},{1,0},{2,3},{3,2},{4,5},{5,4},{6,7},{7,6},{8,9},{9,8},{10,11... | collective-permute-start | bytes 393224 | tf_op jit(solution)/shard_map/ppermute | solution.py:191

commit v5 on v4

--- a/solution.py
+++ b/solution.py
@@ -13,8 +13,7 @@
 f32 = jnp.float32
 i32 = jnp.int32
 swap_bit = 2
-chunk_parts = (7, 5, 4)
-up_chunk = 0
+chunk_parts = (6, 6, 4)
 halves = 2
 vmem_limit = 48 * 1024 * 1024
 smem = pl.BlockSpec(memory_space=pltpu.SMEM)
@@ -41,51 +40,43 @@
     return place
 
 
-def start_kernel(adapt_dev, spans, with_up, len_ref, id_ref, tok_ref, down_ref, up_ref, *refs):
-    sent_refs, (*part_refs, mine_ref, sems) = refs[:halves], refs[halves:]
-    half = sum(size for _, size in spans)
-    heads = mine_ref.shape[1] - half
+def cut_kernel(cuts, down_ref, up_ref, *refs):
+    *out_refs, stage_ref, sems = refs
+    cores = lax.axis_size("tensor")
+    heads, half = up_ref.shape[1] // cores, down_ref.shape[1] // cores
     core = lax.axis_index("tensor")
-
-    def features(start, size):
-        return down_ref.at[:, pl.ds(pl.multiple_of(core * half + start, 128), size)]
-
+    features = down_ref.at[:, pl.ds(pl.multiple_of(core * half, 128), half)]
     up = up_ref.at[:, pl.ds(pl.multiple_of(core * heads, 128), heads)]
-    moves = []
-    for c, (start, size) in enumerate(spans):
-        ahead = heads if c == with_up else 0
-        moves.append((features(start, size), part_refs[c].at[:, pl.ds(ahead, size)]))
-    moves.append((up, part_refs[with_up].at[:, pl.ds(0, heads)]))
-    moves.append((up, mine_ref.at[:, pl.ds(0, heads)]))
-    moves.append((features(0, half), mine_ref.at[:, pl.ds(heads, half)]))
+    moves = [(features, stage_ref.at[:, pl.ds(heads, half)]), (up, stage_ref.at[:, pl.ds(0, heads)])]
+    for (start, size), out_ref in zip(cuts, out_refs):
+        moves.append((stage_ref.at[:, pl.ds(start, size)], out_ref))
     copies = [pltpu.make_async_copy(source, target, sems.at[k]) for k, (source, target) in enumerate(moves)]
-
-    @pl.when(pl.program_id(0) == 0)
-    def _():
-        for copy in copies:
-            copy.start()
-
+    for copy in copies[:2]:
+        copy.start()
+    for copy in copies[:2]:
+        copy.wait()
+    for copy in copies[2:]:
+        copy.start()
+    for copy in copies[2:]:
+        copy.wait()
+
+
+def pack_kernel(adapt_dev, me_ref, len_ref, id_ref, tok_ref, *sent_refs):
     slots, step = sent_refs[0].shape
     rows = tok_ref.shape[0]
-    reqs = list(requests(len_ref, id_ref, lax.axis_index("adapter"), adapt_dev))
+    reqs = list(requests(len_ref, id_ref, me_ref[0], adapt_dev))
     hit = lax.broadcasted_iota(i32, (slots, rows), 0) == row_places(reqs, (1, rows), 1)
-    packed = dot(hit.astype(f32).astype(bf16), tok_ref[...])
-    col = lax.broadcasted_iota(i32, (1, step), 1) + pl.program_id(0) * step
-    adapter_of = jnp.zeros((1, step), i32)
-    for _, _, adapter, slot, away in reqs:
-        adapter_of = jnp.where((col >= slot) & (col < slot + away), adapter, adapter_of)
+    pick = hit.astype(f32).astype(bf16)
     last = lax.broadcasted_iota(i32, (slots, step), 0) == slots - 1
-    packed = jnp.where(last, adapter_of.astype(f32), packed).astype(bf16)
     for part, sent_ref in enumerate(sent_refs):
-
-        @pl.when(pl.program_id(0) == part)
-        def _():
-            sent_ref[...] = packed
-
-    @pl.when(pl.program_id(0) == halves - 1)
-    def _():
-        for copy in copies:
-            copy.wait()
+        packed = dot(pick, tok_ref[:, part * step : (part + 1) * step])
+        if part * step < slots:
+            col = lax.broadcasted_iota(i32, (1, step), 1) + part * step
+            adapter_of = jnp.zeros((1, step), i32)
+            for _, _, adapter, slot, away in reqs:
+                adapter_of = jnp.where((col >= slot) & (col < slot + away), adapter, adapter_of)
+            packed = jnp.where(last, adapter_of.astype(f32), packed)
+        sent_ref[...] = packed.astype(bf16)
 
 
 def own_adapters(reqs, rows, both):
@@ -111,19 +102,17 @@
     return own_adapters(list(requests(len_ref, id_ref, me_ref[0], adapt_dev)), *shape)
 
 
-def low_kernel(adapt_dev, rank, plan, block, heads_in, x_count, first, final, me_ref, len_ref, id_ref, *refs):
+def low_kernel(adapt_dev, rank, plan, heads_in, x_count, first, final, me_ref, len_ref, id_ref, *refs):
     head_refs, refs = refs[:heads_in], refs[heads_in:]
     x_refs, refs, out_ref = refs[:x_count], refs[x_count:-1], refs[-1]
     which = which_adapters(adapt_dev, me_ref, len_ref, id_ref, head_refs, out_ref.shape)
     me = me_ref[0]
     total = jnp.zeros(out_ref.shape, f32) if first else refs[-1][...]
-    for m, ref_no, blocks in plan:
+    for m, pairs in plan:
         term = None
-        for start, col, size in blocks:
-            for j in range(0, size, block):
-                down = refs[ref_no][:, col + j : col + j + block]
-                more = dot(x_refs[(start + j) // block][...], down, (1, 1))
-                term = more if term is None else term + more
+        for x_no, ref_no in pairs:
+            more = dot(x_refs[x_no][...], refs[ref_no][...], (1, 1))
+            term = more if term is None else term + more
         total = total + jnp.where(which // adapt_dev == (me ^ m), term, 0.0)
     if final:
         lane = lax.broadcasted_iota(i32, out_ref.shape, 1)
@@ -192,28 +181,32 @@
 
     sizes = [half * p // 16 for p in chunk_parts]
     spans = [(sum(sizes[:c]), size) for c, size in enumerate(sizes)]
-    widths = [size + (heads if c == up_chunk else 0) for c, size in enumerate(sizes)] + [half + heads]
-    sent_shapes = [jax.ShapeDtypeStruct((slots, half // halves), bf16)] * halves
-    *outs, mine = pl.pallas_call(
-        functools.partial(start_kernel, adapt_dev, spans, up_chunk),
-        grid=(halves,),
-        out_shape=sent_shapes + [jax.ShapeDtypeStruct((both, w), bf16) for w in widths],
-        in_specs=[smem] * 2
-        + [pl.BlockSpec((rows, half // halves), lambda g: (0, g))]
-        + [pl.BlockSpec(memory_space=pl.ANY)] * 2,
-        out_specs=[pl.BlockSpec((slots, half // halves), lambda *_: (0, 0))] * halves
-        + [pl.BlockSpec((both, w), lambda *_: (0, 0)) for w in widths],
-        scratch_shapes=[pltpu.SemaphoreType.DMA((len(spans) + 3,))],
+    cuts = [(a + (heads if c else 0), size + (0 if c else heads)) for c, (a, size) in enumerate(spans)]
+    cuts.append((0, heads + half))
+    *parts, mine = pl.pallas_call(
+        functools.partial(cut_kernel, cuts),
+        out_shape=[jax.ShapeDtypeStruct((both, w), bf16) for _, w in cuts],
+        in_specs=[pl.BlockSpec(memory_space=pl.ANY)] * 2,
+        out_specs=[pl.BlockSpec(memory_space=pl.ANY)] * len(cuts),
+        scratch_shapes=[pltpu.VMEM((both, heads + half), bf16), pltpu.SemaphoreType.DMA((2 + len(cuts),))],
         compiler_params=pltpu.CompilerParams(vmem_limit_bytes=60 * 1024 * 1024),
-        name="start",
-    )(lengths, adapter_ids, tokens, jnp.transpose(down_a, (0, 2, 1)).reshape(both, width), up_weight.reshape(both, -1))
-    sent, parts = outs[:halves], outs[halves:]
-    tokens_other = other_core(after(tokens, sent[0]))
+        name="cut",
+    )(jnp.transpose(down_a, (0, 2, 1)).reshape(both, width), up_weight.reshape(both, -1))
+    tokens_other = other_core(after(tokens, mine))
+    sent = pl.pallas_call(
+        functools.partial(pack_kernel, adapt_dev),
+        grid=(1,),
+        out_shape=[jax.ShapeDtypeStruct((slots, half // halves), bf16)] * halves,
+        in_specs=[smem] * 3 + [whole(tokens)],
+        out_specs=[pl.BlockSpec((slots, half // halves), lambda *_: (0, 0))] * halves,
+        compiler_params=pltpu.CompilerParams(vmem_limit_bytes=60 * 1024 * 1024),
+        name="pack",
+    )(*scalars, after(tokens, mine))
     got = [flip(after(x, tokens_other), swap_bit) for x in sent]
 
     bits = [1 << b for b in range(owners.bit_length() - 1)]
     whole_places = [(c, heads + a) for c, (a, _) in enumerate(spans)]
-    split = [(part, [(c, heads if c == up_chunk else 0)]) for c, part in enumerate(parts)]
+    split = [(part, [(c, 0 if c else heads)]) for c, part in enumerate(parts)]
     pieces = {0: [(mine, whole_places)]}
     for bit in [b for b in bits if b > swap_bit]:
         for m in list(pieces):
@@ -223,30 +216,38 @@
             pieces[m | bit] = came
     near = flip(mine, 1)
 
-    base_own = dot(tokens, lax.dynamic_slice(kv_weight, (core * half, 0), (half, heads)))
+    base_own = dot(after(tokens, *sent), lax.dynamic_slice(kv_weight, (core * half, 0), (half, heads)))
     base = base_own + dot(tokens_other, lax.dynamic_slice(kv_weight, ((1 - core) * half, 0), (half, heads)))
 
-    def add_low(arrays, heads_in, sums, group, final=False):
-        used = sorted({c for _, _, places in group for c, _ in places})
-        lowest, above = spans[used[0]][0], sum(spans[used[-1]])
-        block = math.gcd(half // halves, *(edge for c in used for edge in spans[c]), lowest)
-        at = range(lowest, above, block)
-        plan = [
-            (m, k, [(spans[c][0] - lowest, col, spans[c][1]) for c, col in places])
-            for k, (m, _, places) in enumerate(group)
-        ]
+    def add_low(arrays, heads_in, sums, group, final=False, within=(0, half)):
+        takes = []
+        for m, x, places in group:
+            for c, col in places:
+                start, size = spans[c]
+                low, high = max(start, within[0]), min(start + size, within[1])
+                if low < high:
+                    takes.append((m, x, low, high, col - start))
+        block = math.gcd(half // halves, *(n for _, _, low, high, shift in takes for n in (low, high, shift)))
+        at = sorted({a for _, _, low, high, _ in takes for a in range(low, high, block)})
+        plan, tail, specs = [], [], []
+        for m, x, low, high, shift in takes:
+            pairs = []
+            for a in range(low, high, block):
+                pairs.append((at.index(a), len(tail)))
+                tail.append(x)
+                specs.append(columns(x, a + shift, block))
+            plan.append((m, pairs))
         xs = [arrays[a * len(arrays) // half] for a in at]
         x_specs = [columns(x, a % x.shape[1], block) for x, a in zip(xs, at, strict=True)]
-        tail = [x for _, x, _ in group] + ([] if sums is None else [sums])
+        if sums is not None:
+            tail, specs = tail + [sums], specs + [whole(sums)]
         n = arrays[0].shape[0]
-        flops = sum(2 * n * both * size for _, _, blocks in plan for _, _, size in blocks)
+        flops = sum(2 * n * both * block * len(pairs) for _, pairs in plan)
         return pl.pallas_call(
-            functools.partial(
-                low_kernel, adapt_dev, rank, plan, block, len(heads_in), len(xs), sums is None, final
-            ),
+            functools.partial(low_kernel, adapt_dev, rank, plan, len(heads_in), len(xs), sums is None, final),
             grid=(1,),
             out_shape=jax.ShapeDtypeStruct((n, both), f32),
-            in_specs=[smem] * 3 + [columns(x, 0, head_wide) for x in heads_in] + x_specs + [whole(x) for x in tail],
+            in_specs=[smem] * 3 + [columns(x, 0, head_wide) for x in heads_in] + x_specs + specs,
             out_specs=pl.BlockSpec((n, both), lambda *_: (0, 0)),
             compiler_params=params,
             cost_estimate=pl.CostEstimate(flops=4 * flops, bytes_accessed=flops // 64, transcendentals=0),
@@ -261,20 +262,21 @@
     done = len(items)
     for k, (m, x, places) in enumerate(far):
         last = places[0][0] == len(spans) - 1
-        if False:
-            own, done = add_low([tokens], [], own, items[3:5]), 5
         across = flip(after(x, own, base) if last else after(x, own if k else base_own), 1)
         pieces.setdefault(m | 1, []).append((across, places))
         items.extend([(m, x, places), (m | 1, across, places)][0 if k else 1 :])
 
     def low_rank(arrays, heads_in, sums, todo, batch, final):
         rest = len(todo) - final
-        for a in range(0, rest, batch):
-            sums = add_low(arrays, heads_in, sums, todo[a : min(a + batch, rest)])
+        cut = half // len(arrays)
+        for k in range(len(arrays)):
+            for a in range(0, rest, batch):
+                group = todo[a : min(a + batch, rest)]
+                sums = add_low(arrays, heads_in, sums, group, within=(k * cut, (k + 1) * cut))
         part = add_low(arrays, heads_in, sums, todo[rest:], True)
         return part, other_core(part)
 
-    ups = [next(x for x, places in piece if (up_chunk, heads) == places[-1] or len(places) > 1) for piece in pieces.values()]
+    ups = [piece[0][0] for piece in pieces.values()]
 
     def up(heads_in, lows, extra, kind):
         n = lows[0].shape[0]

time: 87.5 us -> 83.8 us (0.958)
  waiting for transfers between devices: 46.6 us -> 41.3 us
  starting transfers between devices: 11.8 us -> 13.9 us
  local copies, waits for them, and re-layouts: 1.29 us -> 0.02 us
  Pallas kernels: 19.1 us -> 20.3 us
    ppermute x10, waiting for transfers between devices: 44 us -> 38.7 us  [flip(): return lax.ppermute(x, 'adapter', [(j, j ^ bit) for j in range(owners)])]
    ppermute x10, starting transfers between devices: 11.1 us -> 13.2 us  [flip(): return lax.ppermute(x, 'adapter', [(j, j ^ bit) for j in range(owners)])]
    pallas_call x5 -> x7, Pallas kernels: 14.5 us -> 15.9 us  [the longest x5 10.1 us: add_low(): pl.pallas_call(functools.partial(low_kernel, adapt_dev, rank, plan, len(h...]
    unnamed x12 -> x10, local copies, waits for them, and re-layouts: 1.29 us -> 0.02 us
  transfers between devices with their start and end apart: 13 -> 13, of which waited for: 7 -> 7; matrix products, arithmetic and copies ran while one was open for 9% -> 9% of each run, Pallas kernels for 11% -> 16%
where the time goes in v5:
time: 83.8 us; the launch traced here: 83.5 us
  waiting for transfers between devices  41.3 us (49%)
  Pallas kernels  20.3 us (24%)
  starting transfers between devices  13.9 us (17%)
  matrix products  7.8 us (9%)
    ppermute x10, waiting for transfers between devices, flip(): return lax.ppermute(x, 'adapter', [(j, j ^ bit) for j in range(owners)])  38.7 us
    ppermute x10, starting transfers between devices, flip(): return lax.ppermute(x, 'adapter', [(j, j ^ bit) for j in range(owners)])  13.2 us
    pallas_call x5, Pallas kernels, add_low(): pl.pallas_call(functools.partial(low_kernel, adapt_dev, rank, plan, len(h...  10.1 us
    dot_general x2, matrix products, dot(): lax.dot_general(left, right, ((contract[:1], contract[1:]), ((), ())), pr...  7.8 us
    pallas_call x1, Pallas kernels, shards(): pl.pallas_call(functools.partial(pack_kernel, adapt_dev), grid=(1,), out_...  3.07 us
    pallas_call x2, Pallas kernels, up(): pl.pallas_call(functools.partial(up_kernel, adapt_dev, list(pieces), len(...  2.85 us
    pallas_call x1, Pallas kernels, shards(): pl.pallas_call(functools.partial(cut_kernel, cuts), out_shape=[jax.ShapeD...  2.69 us
    ppermute x3, waiting for transfers between devices, other_core(): return lax.ppermute(x, 'tensor', [(0, 1), (1, 0)])  2.61 us
  transfers between devices with their start and end apart: 13, of which 7 were waited for; matrix products, arithmetic and copies ran while one was open for 9% of the time, Pallas kernels for 16%

profile of v5, /device:TPU:0, one launch (start us, length us, event | category | flops | bytes accessed | tf_op | source)
XLA Modules:
  0.0 83.5 jit_solution(7052236947475476561)
XLA Ops:
  0.0 2.7 %cut.1 = (bf16[128,2048]{1,0:T(8,128)(2,1)}, bf16[128,1536]{1,0:T(8,128)(2,1)}, bf16[128,1024]{1,0:T(8,128)(2,1)}, bf16[128,4608]{1,0:T(8,128)(2,1)}) custom-call(bf16[128,8192]{1,0:T(8,128)(2,1)} %bitcast.7, bf16[128,1024]{1,0:T(8,128)(2,1)} %bitcast.8), custom_call_target="tpu_custom_call" | custom-call | tf_op jit(solution)/shard_map/cut/pallas_call | solution.py:186
  2.7 0.5 collective-permute-start.6
  3.2 2.6 %collective-permute-start.3 = (bf16[128,4608]{1,0:T(8,128)(2,1)}, bf16[128,4608]{1,0:T(8,128)(2,1)S(1)}, u32[]{:S(2)}, u32[]{:S(2)}) collective-permute-start(bf16[128,4608]{1,0:T(8,128)(2,1)} %get-tuple-element.21.refs_8_.refs_9_.refs_10_.refs_11_.refs_12_.refs_13_.refs_14_.refs_15_.refs_5_.refs_6_.refs_7_.r, ...), channel_id=1, source_target_pairs={{0,2},{2,0},{4,6},{6,4},{8,10},{10,8},{12,14},{14,12},{1,3},{3,1},... | collective-permute-start | bytes 3538952 | tf_op jit(solution)/shard_map/ppermute | solution.py:177
  5.8 2.6 %collective-permute-start = (bf16[128,2048]{1,0:T(8,128)(2,1)}, bf16[128,2048]{1,0:T(8,128)(2,1)}, u32[]{:S(2)}, u32[]{:S(2)}) collective-permute-start(bf16[128,2048]{1,0:T(8,128)(2,1)} %get-tuple-element.20), channel_id=1, source_target_pairs={{0,8},{2,10},{4,12},{6,14},{8,0},{10,2},{12,4},{14,6},{1,9},{3,11}... | collective-permute-start | bytes 1572872 | tf_op jit(solution)/shard_map/ppermute | solution.py:177
  8.4 0.3 collective-permute-start.2
  8.7 3.1 %pack.1 = (bf16[168,2048]{1,0:T(8,128)(2,1)}, bf16[168,2048]{1,0:T(8,128)(2,1)}) custom-call(s32[1]{0:T(128)} %bitcast.me_ref, s32[7]{0:T(128)} %len_ref.17, s32[7]{0:T(128)} %id_ref.17, bf16[256,4096]{1,0:T(8,128)(2,1)} %refs_7_.3), custom_call_target="tpu_custom_call" | custom-call | tf_op jit(solution)/shard_map/pack/pallas_call | solution.py:196
  11.8 1.6 %collective-permute-start.8 = (bf16[168,2048]{1,0:T(8,128)(2,1)}, bf16[168,2048]{1,0:T(8,128)(2,1)S(1)}, u32[]{:S(2)}, u32[]{:S(2)}) collective-permute-start(bf16[168,2048]{1,0:T(8,128)(2,1)} %get-tuple-element.32), channel_id=1, source_target_pairs={{0,4},{2,6},{4,0},{6,2},{8,12},{10,14},{12,8},{14,10},{1,5},{3,7},... | collective-permute-start | bytes 2064392 | tf_op jit(solution)/shard_map/ppermute | solution.py:177
  13.4 4.9 %fusion.2 = f32[256,512]{1,0:T(8,128)} fusion(bf16[256,4096]{1,0:T(8,128)(2,1)} %refs_7_.3, bf16[8192,512]{1,0:T(8,128)(2,1)} %param.7, s32[]{:T(128)S(6)} %select_n.6), kind=kOutput, calls=%fused_computation.2 | convolution fusion | flops 1073741824 | bytes 6815748 | tf_op jit(solution)/shard_map/dot_general | solution.py:23
  18.3 23.1 %collective-permute-done.refs_24_.refs_25_.refs_26_.refs_13_.refs_14_.refs_15_.refs_4_.refs_3_ = bf16[128,2048]{1,0:T(8,128)(2,1)} collective-permute-done((bf16[128,2048]{1,0:T(8,128)(2,1)}, bf16[128,2048]{1,0:T(8,128)(2,1)}, u32[]{:S(2)}, u32[]{:S(2)}) %collective-permute-start) | collective-permute-done | bytes 524320 | tf_op jit(solution)/shard_map/ppermute | solution.py:177
  41.4 0.0 collective-permute-start.5
  41.4 0.2 collective-permute-start.1
  41.7 3.7 %collective-permute-start.9 = (bf16[168,2048]{1,0:T(8,128)(2,1)}, bf16[168,2048]{1,0:T(8,128)(2,1)S(1)}, u32[]{:S(2)}, u32[]{:S(2)}) collective-permute-start(bf16[168,2048]{1,0:T(8,128)(2,1)} %get-tuple-element.33), channel_id=1, source_target_pairs={{0,4},{2,6},{4,0},{6,2},{8,12},{10,14},{12,8},{14,10},{1,5},{3,7},... | collective-permute-start | bytes 2064392 | tf_op jit(solution)/shard_map/ppermute | solution.py:177
  45.3 3.2 %low.5.refs_21_ = f32[256,128]{1,0:T(8,128)S(1)} custom-call(s32[1]{0:T(128)} %bitcast.me_ref, s32[7]{0:T(128)S(1)} %copy-done.1, s32[7]{0:T(128)S(1)} %copy-done.2, bf16[256,4096]{1,0:T(8,128)(2,1)} %refs_7_.3, bf16[256,4096]{1,0:T(8,128)(2,1)} %refs_7_.3, bf16[256,4096]{1,0:T(8,128)(2,1)} %refs_7_.3, bf16[256,4096]{1,0:T(8,128)(2,1)} %refs_7_.3, ...), custom_call_target="tpu_custom_call" | custom-call | flops 2550136832 | bytes 9961472 | tf_op jit(solution)/shard_map/low/pallas_call | solution.py:246
  48.5 6.9 %collective-permute-done.2.refs_19_.refs_13_.refs_14_.refs_11_.refs_12_ = bf16[128,1536]{1,0:T(8,128)(2,1)S(1)} collective-permute-done((bf16[128,1536]{1,0:T(8,128)(2,1)}, bf16[128,1536]{1,0:T(8,128)(2,1)S(1)}, u32[]{:S(2)}, u32[]{:S(2)}) %collective-permute-start.2) | collective-permute-done | bytes 393248 | tf_op jit(solution)/shard_map/ppermute | solution.py:177
  55.5 0.2 collective-permute-start.4
  55.6 2.9 %fusion.4.refs_6_ = f32[256,512]{1,0:T(8,128)S(1)} fusion(f32[256,512]{1,0:T(8,128)} %fusion.2, bf16[256,4096]{1,0:T(8,128)(2,1)} %collective-permute-done.6, bf16[8192,512]{1,0:T(8,128)(2,1)S(1)} %bitcast.10, s32[]{:T(128)S(6)} %select_n.7), kind=kOutput, calls=%fused_computation.4 | convolution fusion | flops 1073872896 | bytes 7340036 | tf_op jit(solution)/shard_map/dot_general | solution.py:23
  58.6 1.8 %collective-permute-done.5.refs_2_.refs_17_.refs_18_ = bf16[128,1024]{1,0:T(8,128)(2,1)S(1)} collective-permute-done((bf16[128,1024]{1,0:T(8,128)(2,1)}, bf16[128,1024]{1,0:T(8,128)(2,1)S(1)}, u32[]{:S(2)}, u32[]{:S(2)}) %collective-permute-start.5) | collective-permute-done | bytes 262176 | tf_op jit(solution)/shard_map/ppermute | solution.py:177
  60.3 0.5 collective-permute-start.7
  60.8 6.7 %collective-permute-done.4.refs_20_.refs_15_.refs_16_.refs_14_ = bf16[128,1536]{1,0:T(8,128)(2,1)S(1)} collective-permute-done((bf16[128,1536]{1,0:T(8,128)(2,1)S(1)}, bf16[128,1536]{1,0:T(8,128)(2,1)S(1)}, u32[]{:S(2)}, u32[]{:S(2)}) %collective-permute-start.4) | collective-permute-done | bytes 393248 | tf_op jit(solution)/shard_map/ppermute | solution.py:177
  67.5 2.0 %low.6.refs_17_ = f32[168,128]{1,0:T(8,128)S(1)} custom-call(s32[1]{0:T(128)} %bitcast.me_ref, s32[7]{0:T(128)S(1)} %copy-done.1, s32[7]{0:T(128)S(1)} %copy-done.2, bf16[168,2048]{1,0:T(8,128)(2,1)S(1)} %collective-permute-done.8.refs_0_.refs_1_.refs_2_.refs_3_.refs_4_, bf16[168,2048]{1,0:T(8,128)(2,1)S(1)} %collective-permute-done.8.refs_0_.refs_1_.refs_2_.refs_3_.refs_4_, ...), custom_call_target="tpu_custom_call" | custom-call | flops 1409286144 | bytes 5505024 | tf_op jit(solution)/shard_map/low/pallas_call | solution.py:246
  69.6 0.2 collective-permute-done.9.refs_1_.refs_2_.refs_3_.refs_4_
  69.8 1.3 %low.7.refs_4_ = f32[168,128]{1,0:T(8,128)S(1)} custom-call(s32[1]{0:T(128)} %bitcast.me_ref, s32[7]{0:T(128)S(1)} %copy-done.1, s32[7]{0:T(128)S(1)} %copy-done.2, bf16[168,2048]{1,0:T(8,128)(2,1)S(1)} %collective-permute-done.8.refs_0_.refs_1_.refs_2_.refs_3_.refs_4_, bf16[168,2048]{1,0:T(8,128)(2,1)S(1)} %collective-permute-done.9.refs_1_.refs_2_.refs_3_.refs_4_, ...), custom_call_target="tpu_custom_call" | custom-call | flops 1056964608 | bytes 4128768 | tf_op jit(solution)/shard_map/low/pallas_call | solution.py:246
  71.1 0.9 %low.8.refs_1_ = f32[168,128]{1,0:T(8,128)S(1)} custom-call(s32[1]{0:T(128)} %bitcast.me_ref, s32[7]{0:T(128)S(1)} %copy-done.1, s32[7]{0:T(128)S(1)} %copy-done.2, bf16[168,2048]{1,0:T(8,128)(2,1)S(1)} %collective-permute-done.8.refs_0_.refs_1_.refs_2_.refs_3_.refs_4_, bf16[168,2048]{1,0:T(8,128)(2,1)S(1)} %collective-permute-done.9.refs_1_.refs_2_.refs_3_.refs_4_, ...), custom_call_target="tpu_custom_call" | custom-call | flops 352321536 | bytes 1376256 | tf_op jit(solution)/shard_map/low/pallas_call | solution.py:246
  72.0 0.1 collective-permute-start.10
  72.1 1.3 %collective-permute-done.10.refs_2_ = f32[168,128]{1,0:T(8,128)S(1)} collective-permute-done((f32[168,128]{1,0:T(8,128)S(1)}, f32[168,128]{1,0:T(8,128)S(1)}, u32[]{:S(2)}, u32[]{:S(2)}) %collective-permute-start.10) | collective-permute-done | bytes 86048 | tf_op jit(solution)/shard_map/ppermute | solution.py:180
  73.3 1.4 %up.2 = bf16[168,512]{1,0:T(8,128)(2,1)S(1)} custom-call(s32[1]{0:T(128)} %bitcast.me_ref, s32[7]{0:T(128)S(1)} %copy-done.1, s32[7]{0:T(128)S(1)} %copy-done.2, bf16[168,2048]{1,0:T(8,128)(2,1)S(1)} %collective-permute-done.8.refs_0_.refs_1_.refs_2_.refs_3_.refs_4_, f32[168,128]{1,0:T(8,128)S(1)} %low.8.refs_1_, ...), custom_call_target="tpu_custom_call" | custom-call | tf_op jit(solution)/shard_map/up/pallas_call | solution.py:283
  74.7 1.5 %collective-permute-start.12 = (bf16[168,512]{1,0:T(8,128)(2,1)S(1)}, bf16[168,512]{1,0:T(8,128)(2,1)S(1)}, u32[]{:S(2)}, u32[]{:S(2)}) collective-permute-start(bf16[168,512]{1,0:T(8,128)(2,1)S(1)} %up.2), channel_id=1, source_target_pairs={{0,4},{2,6},{4,0},{6,2},{8,12},{10,14},{12,8},{14,10},{1,5},{3,7},... | collective-permute-start | bytes 516104 | tf_op jit(solution)/shard_map/ppermute | solution.py:177
  76.2 2.7 %low.9.refs_0_ = f32[256,128]{1,0:T(8,128)S(1)} custom-call(s32[1]{0:T(128)} %bitcast.me_ref, s32[7]{0:T(128)S(1)} %copy-done.1, s32[7]{0:T(128)S(1)} %copy-done.2, bf16[256,4096]{1,0:T(8,128)(2,1)} %refs_7_.3, bf16[256,4096]{1,0:T(8,128)(2,1)} %refs_7_.3, bf16[256,4096]{1,0:T(8,128)(2,1)} %refs_7_.3, bf16[256,4096]{1,0:T(8,128)(2,1)} %refs_7_.3, ...), custom_call_target="tpu_custom_call" | custom-call | flops 1744830464 | bytes 6815744 | tf_op jit(solution)/shard_map/low/pallas_call | solution.py:246
  78.9 0.1 collective-permute-start.11
  79.0 1.3 %collective-permute-done.11.refs_1_ = f32[256,128]{1,0:T(8,128)S(1)} collective-permute-done((f32[256,128]{1,0:T(8,128)S(1)}, f32[256,128]{1,0:T(8,128)S(1)}, u32[]{:S(2)}, u32[]{:S(2)}) %collective-permute-start.11) | collective-permute-done | bytes 131104 | tf_op jit(solution)/shard_map/ppermute | solution.py:180
  80.4 1.5 %up.3.sum_ref = f32[256,512]{1,0:T(8,128)S(1)} custom-call(s32[1]{0:T(128)} %bitcast.me_ref, s32[7]{0:T(128)S(1)} %copy-done.1, s32[7]{0:T(128)S(1)} %copy-done.2, f32[256,128]{1,0:T(8,128)S(1)} %low.9.refs_0_, f32[256,128]{1,0:T(8,128)S(1)} %collective-permute-done.11.refs_1_, bf16[128,4608]{1,0:T(8,128)(2,1)S(1)} %copy-done, ...), custom_call_target="tpu_custom_call" | custom-call | tf_op jit(solution)/shard_map/up/pallas_call | solution.py:283
  81.9 1.6 %last.1 = bf16[256,512]{1,0:T(8,128)(2,1)} custom-call(s32[1]{0:T(128)} %bitcast.me_ref, s32[7]{0:T(128)S(1)} %copy-done.1, s32[7]{0:T(128)S(1)} %copy-done.2, f32[256,512]{1,0:T(8,128)S(1)} %up.3.sum_ref, bf16[168,512]{1,0:T(8,128)(2,1)S(1)} %collective-permute-done.12.back_ref), custom_call_target="tpu_custom_call" | custom-call | tf_op jit(solution)/shard_map/last/pallas_call | solution.py:302
  (17 shorter events, 0.0 us)
Async XLA Ops:
  2.7 9.1 %collective-permute-start.6 = (bf16[256,4096]{1,0:T(8,128)(2,1)}, bf16[256,4096]{1,0:T(8,128)(2,1)}, u32[]{:S(2)}, u32[]{:S(2)}) collective-permute-start(bf16[256,4096]{1,0:T(8,128)(2,1)} %refs_7_.3), channel_id=1, source_target_pairs={{0,1},{1,0},{2,3},{3,2},{4,5},{5,4},{6,7},{7,6},{8,9},{9,8},{10,11... | collective-permute-start | bytes 6291464 | tf_op jit(solution)/shard_map/ppermute | solution.py:180
  3.2 38.5 %collective-permute-start.3 = (bf16[128,4608]{1,0:T(8,128)(2,1)}, bf16[128,4608]{1,0:T(8,128)(2,1)S(1)}, u32[]{:S(2)}, u32[]{:S(2)}) collective-permute-start(bf16[128,4608]{1,0:T(8,128)(2,1)} %get-tuple-element.21.refs_8_.refs_9_.refs_10_.refs_11_.refs_12_.refs_13_.refs_14_.refs_15_.refs_5_.refs_6_.refs_7_.r, ...), channel_id=1, source_target_pairs={{0,2},{2,0},{4,6},{6,4},{8,10},{10,8},{12,14},{14,12},{1,3},{3,1},... | collective-permute-start | bytes 3538952 | tf_op jit(solution)/shard_map/ppermute | solution.py:177
  5.8 35.6 %collective-permute-start = (bf16[128,2048]{1,0:T(8,128)(2,1)}, bf16[128,2048]{1,0:T(8,128)(2,1)}, u32[]{:S(2)}, u32[]{:S(2)}) collective-permute-start(bf16[128,2048]{1,0:T(8,128)(2,1)} %get-tuple-element.20), channel_id=1, source_target_pairs={{0,8},{2,10},{4,12},{6,14},{8,0},{10,2},{12,4},{14,6},{1,9},{3,11}... | collective-permute-start | bytes 1572872 | tf_op jit(solution)/shard_map/ppermute | solution.py:177
  8.4 47.1 %collective-permute-start.2 = (bf16[128,1536]{1,0:T(8,128)(2,1)}, bf16[128,1536]{1,0:T(8,128)(2,1)S(1)}, u32[]{:S(2)}, u32[]{:S(2)}) collective-permute-start(bf16[128,1536]{1,0:T(8,128)(2,1)} %get-tuple-element.27), channel_id=1, source_target_pairs={{0,8},{2,10},{4,12},{6,14},{8,0},{10,2},{12,4},{14,6},{1,9},{3,11}... | collective-permute-start | bytes 1179656 | tf_op jit(solution)/shard_map/ppermute | solution.py:177
  11.8 33.5 %copy-start = (bf16[128,4608]{1,0:T(8,128)(2,1)S(1)}, bf16[128,4608]{1,0:T(8,128)(2,1)}, u32[]{:S(2)}) copy-start(bf16[128,4608]{1,0:T(8,128)(2,1)} %get-tuple-element.21.refs_8_.refs_9_.refs_10_.refs_11_.refs_12_.refs_13_.refs_14_.refs_15_.refs_5_.refs_6_.refs_7_.refs_3_.refs_2_) | copy-start | bytes 3538948
  11.8 33.5 %copy-start.1 = (s32[7]{0:T(128)S(1)}, s32[7]{0:T(128)}, u32[]{:S(2)}) copy-start(s32[7]{0:T(128)} %len_ref.17) | copy-start | bytes 88
  11.8 33.5 %copy-start.2 = (s32[7]{0:T(128)S(1)}, s32[7]{0:T(128)}, u32[]{:S(2)}) copy-start(s32[7]{0:T(128)} %id_ref.17) | copy-start | bytes 88
  11.8 55.7 %collective-permute-start.8 = (bf16[168,2048]{1,0:T(8,128)(2,1)}, bf16[168,2048]{1,0:T(8,128)(2,1)S(1)}, u32[]{:S(2)}, u32[]{:S(2)}) collective-permute-start(bf16[168,2048]{1,0:T(8,128)(2,1)} %get-tuple-element.32), channel_id=1, source_target_pairs={{0,4},{2,6},{4,0},{6,2},{8,12},{10,14},{12,8},{14,10},{1,5},{3,7},... | collective-permute-start | bytes 2064392 | tf_op jit(solution)/shard_map/ppermute | solution.py:177
  41.4 14.2 %slice-start = ((s8[8388608]{0:T(1024)(128)(4,1)}), s8[4194304]{0:T(1024)(128)(4,1)S(1)}, s32[]{:S(2)}) async-start(s8[8388608]{0:T(1024)(128)(4,1)} %bitcast.9), calls=%async_computation | async-start | bytes 8388608
  41.4 14.2 %slice-start.1 = ((s8[8388608]{0:T(1024)(128)(4,1)}), s8[4194304]{0:T(1024)(128)(4,1)S(1)}, s32[]{:S(2)}) async-start(s8[8388608]{0:T(1024)(128)(4,1)} %bitcast.9), calls=%async_computation.1 | async-start | bytes 8388608
  41.4 18.9 %collective-permute-start.5 = (bf16[128,1024]{1,0:T(8,128)(2,1)}, bf16[128,1024]{1,0:T(8,128)(2,1)S(1)}, u32[]{:S(2)}, u32[]{:S(2)}) collective-permute-start(bf16[128,1024]{1,0:T(8,128)(2,1)} %get-tuple-element.30), channel_id=1, source_target_pairs={{0,8},{2,10},{4,12},{6,14},{8,0},{10,2},{12,4},{14,6},{1,9},{3,11}... | collective-permute-start | bytes 786440 | tf_op jit(solution)/shard_map/ppermute | solution.py:177
  41.4 19.4 %collective-permute-start.1 = (bf16[128,2048]{1,0:T(8,128)(2,1)}, bf16[128,2048]{1,0:T(8,128)(2,1)S(1)}, u32[]{:S(2)}, u32[]{:S(2)}) collective-permute-start(bf16[128,2048]{1,0:T(8,128)(2,1)} %collective-permute-done.refs_24_.refs_25_.refs_26_.refs_13_.refs_14_.refs_15_.refs_4_.refs_3_), channel_id=1, source_target_pairs={{0,2},{2,0},{4,6},{6,4},{8,10},{10,8},{12,14},{14,12},{1,3},{3,1},... | collective-permute-start | bytes 1572872 | tf_op jit(solution)/shard_map/ppermute | solution.py:177
  41.7 28.1 %collective-permute-start.9 = (bf16[168,2048]{1,0:T(8,128)(2,1)}, bf16[168,2048]{1,0:T(8,128)(2,1)S(1)}, u32[]{:S(2)}, u32[]{:S(2)}) collective-permute-start(bf16[168,2048]{1,0:T(8,128)(2,1)} %get-tuple-element.33), channel_id=1, source_target_pairs={{0,4},{2,6},{4,0},{6,2},{8,12},{10,14},{12,8},{14,10},{1,5},{3,7},... | collective-permute-start | bytes 2064392 | tf_op jit(solution)/shard_map/ppermute | solution.py:177
  55.5 12.1 %collective-permute-start.4 = (bf16[128,1536]{1,0:T(8,128)(2,1)S(1)}, bf16[128,1536]{1,0:T(8,128)(2,1)S(1)}, u32[]{:S(2)}, u32[]{:S(2)}) collective-permute-start(bf16[128,1536]{1,0:T(8,128)(2,1)S(1)} %collective-permute-done.2.refs_19_.refs_13_.refs_14_.refs_11_.refs_12_), channel_id=1, source_target_pairs={{0,2},{2,0},{4,6},{6,4},{8,10},{10,8},{12,14},{14,12},{1,3},{3,1},... | collective-permute-start | bytes 1179656 | tf_op jit(solution)/shard_map/ppermute | solution.py:177
  60.3 10.8 %collective-permute-start.7 = (bf16[128,1024]{1,0:T(8,128)(2,1)S(1)}, bf16[128,1024]{1,0:T(8,128)(2,1)S(1)}, u32[]{:S(2)}, u32[]{:S(2)}) collective-permute-start(bf16[128,1024]{1,0:T(8,128)(2,1)S(1)} %collective-permute-done.5.refs_2_.refs_17_.refs_18_), channel_id=1, source_target_pairs={{0,2},{2,0},{4,6},{6,4},{8,10},{10,8},{12,14},{14,12},{1,3},{3,1},... | collective-permute-start | bytes 786440 | tf_op jit(solution)/shard_map/ppermute | solution.py:177
  72.0 1.3 %collective-permute-start.10 = (f32[168,128]{1,0:T(8,128)S(1)}, f32[168,128]{1,0:T(8,128)S(1)}, u32[]{:S(2)}, u32[]{:S(2)}) collective-permute-start(f32[168,128]{1,0:T(8,128)S(1)} %low.8.refs_1_), channel_id=1, source_target_pairs={{0,1},{1,0},{2,3},{3,2},{4,5},{5,4},{6,7},{7,6},{8,9},{9,8},{10,11... | collective-permute-start | bytes 258056 | tf_op jit(solution)/shard_map/ppermute | solution.py:180
  74.7 7.2 %collective-permute-start.12 = (bf16[168,512]{1,0:T(8,128)(2,1)S(1)}, bf16[168,512]{1,0:T(8,128)(2,1)S(1)}, u32[]{:S(2)}, u32[]{:S(2)}) collective-permute-start(bf16[168,512]{1,0:T(8,128)(2,1)S(1)} %up.2), channel_id=1, source_target_pairs={{0,4},{2,6},{4,0},{6,2},{8,12},{10,14},{12,8},{14,10},{1,5},{3,7},... | collective-permute-start | bytes 516104 | tf_op jit(solution)/shard_map/ppermute | solution.py:177
  78.9 1.4 %collective-permute-start.11 = (f32[256,128]{1,0:T(8,128)S(1)}, f32[256,128]{1,0:T(8,128)S(1)}, u32[]{:S(2)}, u32[]{:S(2)}) collective-permute-start(f32[256,128]{1,0:T(8,128)S(1)} %low.9.refs_0_), channel_id=1, source_target_pairs={{0,1},{1,0},{2,3},{3,2},{4,5},{5,4},{6,7},{7,6},{8,9},{9,8},{10,11... | collective-permute-start | bytes 393224 | tf_op jit(solution)/shard_map/ppermute | solution.py:180

commit v6 on v5

--- a/solution.py
+++ b/solution.py
@@ -15,7 +15,7 @@
 swap_bit = 2
 chunk_parts = (6, 6, 4)
 halves = 2
-vmem_limit = 48 * 1024 * 1024
+vmem_limit = 24 * 1024 * 1024
 smem = pl.BlockSpec(memory_space=pltpu.SMEM)
 
 
@@ -45,19 +45,23 @@
     cores = lax.axis_size("tensor")
     heads, half = up_ref.shape[1] // cores, down_ref.shape[1] // cores
     core = lax.axis_index("tensor")
-    features = down_ref.at[:, pl.ds(pl.multiple_of(core * half, 128), half)]
     up = up_ref.at[:, pl.ds(pl.multiple_of(core * heads, 128), heads)]
-    moves = [(features, stage_ref.at[:, pl.ds(heads, half)]), (up, stage_ref.at[:, pl.ds(0, heads)])]
-    for (start, size), out_ref in zip(cuts, out_refs):
-        moves.append((stage_ref.at[:, pl.ds(start, size)], out_ref))
-    copies = [pltpu.make_async_copy(source, target, sems.at[k]) for k, (source, target) in enumerate(moves)]
-    for copy in copies[:2]:
+    ins = [(up, stage_ref.at[:, pl.ds(0, heads)])]
+    for c, (start, size) in enumerate(cuts[:-1]):
+        ahead = 0 if c else heads
+        at, size = start + ahead, size - ahead
+        source = down_ref.at[:, pl.ds(pl.multiple_of(core * half + at - heads, 128), size)]
+        ins.append((source, stage_ref.at[:, pl.ds(at, size)]))
+    outs = [(stage_ref.at[:, pl.ds(start, size)], out_ref) for (start, size), out_ref in zip(cuts, out_refs)]
+    copies = [pltpu.make_async_copy(source, target, sems.at[k]) for k, (source, target) in enumerate(ins + outs)]
+    for copy in copies[: len(ins)]:
         copy.start()
-    for copy in copies[:2]:
-        copy.wait()
-    for copy in copies[2:]:
-        copy.start()
-    for copy in copies[2:]:
+    copies[0].wait()
+    for arrived, leaving in zip(copies[1 : len(ins)], copies[len(ins) :]):
+        arrived.wait()
+        leaving.start()
+    copies[-1].start()
+    for copy in copies[len(ins) :]:
         copy.wait()
 
 
@@ -188,7 +192,7 @@
         out_shape=[jax.ShapeDtypeStruct((both, w), bf16) for _, w in cuts],
         in_specs=[pl.BlockSpec(memory_space=pl.ANY)] * 2,
         out_specs=[pl.BlockSpec(memory_space=pl.ANY)] * len(cuts),
-        scratch_shapes=[pltpu.VMEM((both, heads + half), bf16), pltpu.SemaphoreType.DMA((2 + len(cuts),))],
+        scratch_shapes=[pltpu.VMEM((both, heads + half), bf16), pltpu.SemaphoreType.DMA((2 * len(cuts),))],
         compiler_params=pltpu.CompilerParams(vmem_limit_bytes=60 * 1024 * 1024),
         name="cut",
     )(jnp.transpose(down_a, (0, 2, 1)).reshape(both, width), up_weight.reshape(both, -1))

time: 83.8 us -> 83.6 us (level)
  transfers between devices with their start and end apart: 13 -> 13, of which waited for: 7 -> 7; matrix products, arithmetic and copies ran while one was open for 9% -> 9% of each run, Pallas kernels for 16% -> 17%
where the time goes in v6:
time: 83.6 us; the launch traced here: 83.3 us
  waiting for transfers between devices  41.4 us (50%)
  Pallas kernels  20.2 us (24%)
  starting transfers between devices  13.8 us (17%)
  matrix products  7.72 us (9%)
    ppermute x10, waiting for transfers between devices, flip(): return lax.ppermute(x, 'adapter', [(j, j ^ bit) for j in range(owners)])  38.8 us
    ppermute x10, starting transfers between devices, flip(): return lax.ppermute(x, 'adapter', [(j, j ^ bit) for j in range(owners)])  13.2 us
    pallas_call x5, Pallas kernels, add_low(): pl.pallas_call(functools.partial(low_kernel, adapt_dev, rank, plan, len(h...  10.1 us
    dot_general x2, matrix products, dot(): lax.dot_general(left, right, ((contract[:1], contract[1:]), ((), ())), pr...  7.72 us
    pallas_call x1, Pallas kernels, shards(): pl.pallas_call(functools.partial(pack_kernel, adapt_dev), grid=(1,), out_...  3.08 us
    pallas_call x2, Pallas kernels, up(): pl.pallas_call(functools.partial(up_kernel, adapt_dev, list(pieces), len(...  2.84 us
    ppermute x3, waiting for transfers between devices, other_core(): return lax.ppermute(x, 'tensor', [(0, 1), (1, 0)])  2.61 us
    pallas_call x1, Pallas kernels, shards(): pl.pallas_call(functools.partial(cut_kernel, cuts), out_shape=[jax.ShapeD...  2.54 us
  transfers between devices with their start and end apart: 13, of which 7 were waited for; matrix products, arithmetic and copies ran while one was open for 9% of the time, Pallas kernels for 17%

profile of v6, /device:TPU:0, one launch (start us, length us, event | category | flops | bytes accessed | tf_op | source)
XLA Modules:
  0.0 83.3 jit_solution(13529125424211407276)
XLA Ops:
  0.0 2.5 %cut.1 = (bf16[128,2048]{1,0:T(8,128)(2,1)}, bf16[128,1536]{1,0:T(8,128)(2,1)}, bf16[128,1024]{1,0:T(8,128)(2,1)}, bf16[128,4608]{1,0:T(8,128)(2,1)}) custom-call(bf16[128,8192]{1,0:T(8,128)(2,1)} %bitcast.7, bf16[128,1024]{1,0:T(8,128)(2,1)} %bitcast.8), custom_call_target="tpu_custom_call" | custom-call | tf_op jit(solution)/shard_map/cut/pallas_call | solution.py:190
  2.5 0.5 collective-permute-start.6
  3.1 2.6 %collective-permute-start.3 = (bf16[128,4608]{1,0:T(8,128)(2,1)}, bf16[128,4608]{1,0:T(8,128)(2,1)S(1)}, u32[]{:S(2)}, u32[]{:S(2)}) collective-permute-start(bf16[128,4608]{1,0:T(8,128)(2,1)} %get-tuple-element.21.refs_8_.refs_9_.refs_10_.refs_11_.refs_12_.refs_13_.refs_14_.refs_15_.refs_5_.refs_6_.refs_7_.r, ...), channel_id=1, source_target_pairs={{0,2},{2,0},{4,6},{6,4},{8,10},{10,8},{12,14},{14,12},{1,3},{3,1},... | collective-permute-start | bytes 3538952 | tf_op jit(solution)/shard_map/ppermute | solution.py:181
  5.6 2.6 %collective-permute-start = (bf16[128,2048]{1,0:T(8,128)(2,1)}, bf16[128,2048]{1,0:T(8,128)(2,1)}, u32[]{:S(2)}, u32[]{:S(2)}) collective-permute-start(bf16[128,2048]{1,0:T(8,128)(2,1)} %get-tuple-element.20), channel_id=1, source_target_pairs={{0,8},{2,10},{4,12},{6,14},{8,0},{10,2},{12,4},{14,6},{1,9},{3,11}... | collective-permute-start | bytes 1572872 | tf_op jit(solution)/shard_map/ppermute | solution.py:181
  8.2 0.3 collective-permute-start.2
  8.6 3.1 %pack.1 = (bf16[168,2048]{1,0:T(8,128)(2,1)}, bf16[168,2048]{1,0:T(8,128)(2,1)}) custom-call(s32[1]{0:T(128)} %bitcast.me_ref, s32[7]{0:T(128)} %len_ref.17, s32[7]{0:T(128)} %id_ref.17, bf16[256,4096]{1,0:T(8,128)(2,1)} %refs_7_.3), custom_call_target="tpu_custom_call" | custom-call | tf_op jit(solution)/shard_map/pack/pallas_call | solution.py:200
  11.7 0.0 collective-permute-done.6
  11.7 1.6 %collective-permute-start.8 = (bf16[168,2048]{1,0:T(8,128)(2,1)}, bf16[168,2048]{1,0:T(8,128)(2,1)S(1)}, u32[]{:S(2)}, u32[]{:S(2)}) collective-permute-start(bf16[168,2048]{1,0:T(8,128)(2,1)} %get-tuple-element.32), channel_id=1, source_target_pairs={{0,4},{2,6},{4,0},{6,2},{8,12},{10,14},{12,8},{14,10},{1,5},{3,7},... | collective-permute-start | bytes 2064392 | tf_op jit(solution)/shard_map/ppermute | solution.py:181
  13.3 4.9 %fusion.2 = f32[256,512]{1,0:T(8,128)} fusion(bf16[256,4096]{1,0:T(8,128)(2,1)} %refs_7_.3, bf16[8192,512]{1,0:T(8,128)(2,1)} %param.7, s32[]{:T(128)S(6)} %select_n.6), kind=kOutput, calls=%fused_computation.2 | convolution fusion | flops 1073741824 | bytes 6815748 | tf_op jit(solution)/shard_map/dot_general | solution.py:23
  18.2 23.1 %collective-permute-done.refs_24_.refs_25_.refs_26_.refs_13_.refs_14_.refs_15_.refs_4_.refs_3_ = bf16[128,2048]{1,0:T(8,128)(2,1)} collective-permute-done((bf16[128,2048]{1,0:T(8,128)(2,1)}, bf16[128,2048]{1,0:T(8,128)(2,1)}, u32[]{:S(2)}, u32[]{:S(2)}) %collective-permute-start) | collective-permute-done | bytes 524320 | tf_op jit(solution)/shard_map/ppermute | solution.py:181
  41.3 0.2 collective-permute-start.1
  41.5 3.6 %collective-permute-start.9 = (bf16[168,2048]{1,0:T(8,128)(2,1)}, bf16[168,2048]{1,0:T(8,128)(2,1)S(1)}, u32[]{:S(2)}, u32[]{:S(2)}) collective-permute-start(bf16[168,2048]{1,0:T(8,128)(2,1)} %get-tuple-element.33), channel_id=1, source_target_pairs={{0,4},{2,6},{4,0},{6,2},{8,12},{10,14},{12,8},{14,10},{1,5},{3,7},... | collective-permute-start | bytes 2064392 | tf_op jit(solution)/shard_map/ppermute | solution.py:181
  45.2 3.2 %low.5.refs_21_ = f32[256,128]{1,0:T(8,128)S(1)} custom-call(s32[1]{0:T(128)} %bitcast.me_ref, s32[7]{0:T(128)S(1)} %copy-done.1, s32[7]{0:T(128)S(1)} %copy-done.2, bf16[256,4096]{1,0:T(8,128)(2,1)} %refs_7_.3, bf16[256,4096]{1,0:T(8,128)(2,1)} %refs_7_.3, bf16[256,4096]{1,0:T(8,128)(2,1)} %refs_7_.3, bf16[256,4096]{1,0:T(8,128)(2,1)} %refs_7_.3, ...), custom_call_target="tpu_custom_call" | custom-call | flops 2550136832 | bytes 9961472 | tf_op jit(solution)/shard_map/low/pallas_call | solution.py:250
  48.4 6.9 %collective-permute-done.2.refs_19_.refs_13_.refs_14_.refs_11_.refs_12_ = bf16[128,1536]{1,0:T(8,128)(2,1)S(1)} collective-permute-done((bf16[128,1536]{1,0:T(8,128)(2,1)}, bf16[128,1536]{1,0:T(8,128)(2,1)S(1)}, u32[]{:S(2)}, u32[]{:S(2)}) %collective-permute-start.2) | collective-permute-done | bytes 393248 | tf_op jit(solution)/shard_map/ppermute | solution.py:181
  55.3 0.2 collective-permute-start.4
  55.5 2.8 %fusion.4.refs_6_ = f32[256,512]{1,0:T(8,128)S(1)} fusion(f32[256,512]{1,0:T(8,128)S(1)} %copy-done.3, bf16[256,4096]{1,0:T(8,128)(2,1)} %collective-permute-done.6, bf16[8192,512]{1,0:T(8,128)(2,1)S(1)} %bitcast.10, s32[]{:T(128)S(6)} %select_n.7), kind=kOutput, calls=%fused_computation.4 | convolution fusion | flops 1073872896 | bytes 7340036 | tf_op jit(solution)/shard_map/dot_general | solution.py:23
  58.3 1.8 %collective-permute-done.5.refs_2_.refs_17_.refs_18_ = bf16[128,1024]{1,0:T(8,128)(2,1)S(1)} collective-permute-done((bf16[128,1024]{1,0:T(8,128)(2,1)}, bf16[128,1024]{1,0:T(8,128)(2,1)S(1)}, u32[]{:S(2)}, u32[]{:S(2)}) %collective-permute-start.5) | collective-permute-done | bytes 262176 | tf_op jit(solution)/shard_map/ppermute | solution.py:181
  60.2 0.5 collective-permute-start.7
  60.7 6.7 %collective-permute-done.4.refs_20_.refs_15_.refs_16_.refs_14_ = bf16[128,1536]{1,0:T(8,128)(2,1)S(1)} collective-permute-done((bf16[128,1536]{1,0:T(8,128)(2,1)S(1)}, bf16[128,1536]{1,0:T(8,128)(2,1)S(1)}, u32[]{:S(2)}, u32[]{:S(2)}) %collective-permute-start.4) | collective-permute-done | bytes 393248 | tf_op jit(solution)/shard_map/ppermute | solution.py:181
  67.4 2.0 %low.6.refs_17_ = f32[168,128]{1,0:T(8,128)S(1)} custom-call(s32[1]{0:T(128)} %bitcast.me_ref, s32[7]{0:T(128)S(1)} %copy-done.1, s32[7]{0:T(128)S(1)} %copy-done.2, bf16[168,2048]{1,0:T(8,128)(2,1)S(1)} %collective-permute-done.8.refs_0_.refs_1_.refs_2_.refs_3_.refs_4_, bf16[168,2048]{1,0:T(8,128)(2,1)S(1)} %collective-permute-done.8.refs_0_.refs_1_.refs_2_.refs_3_.refs_4_, ...), custom_call_target="tpu_custom_call" | custom-call | flops 1409286144 | bytes 5505024 | tf_op jit(solution)/shard_map/low/pallas_call | solution.py:250
  69.4 0.2 collective-permute-done.9.refs_1_.refs_2_.refs_3_.refs_4_
  69.6 1.3 %low.7.refs_4_ = f32[168,128]{1,0:T(8,128)S(1)} custom-call(s32[1]{0:T(128)} %bitcast.me_ref, s32[7]{0:T(128)S(1)} %copy-done.1, s32[7]{0:T(128)S(1)} %copy-done.2, bf16[168,2048]{1,0:T(8,128)(2,1)S(1)} %collective-permute-done.8.refs_0_.refs_1_.refs_2_.refs_3_.refs_4_, bf16[168,2048]{1,0:T(8,128)(2,1)S(1)} %collective-permute-done.9.refs_1_.refs_2_.refs_3_.refs_4_, ...), custom_call_target="tpu_custom_call" | custom-call | flops 1056964608 | bytes 4128768 | tf_op jit(solution)/shard_map/low/pallas_call | solution.py:250
  70.9 0.9 %low.8.refs_1_ = f32[168,128]{1,0:T(8,128)S(1)} custom-call(s32[1]{0:T(128)} %bitcast.me_ref, s32[7]{0:T(128)S(1)} %copy-done.1, s32[7]{0:T(128)S(1)} %copy-done.2, bf16[168,2048]{1,0:T(8,128)(2,1)S(1)} %collective-permute-done.8.refs_0_.refs_1_.refs_2_.refs_3_.refs_4_, bf16[168,2048]{1,0:T(8,128)(2,1)S(1)} %collective-permute-done.9.refs_1_.refs_2_.refs_3_.refs_4_, ...), custom_call_target="tpu_custom_call" | custom-call | flops 352321536 | bytes 1376256 | tf_op jit(solution)/shard_map/low/pallas_call | solution.py:250
  71.8 0.1 collective-permute-start.10
  71.9 1.3 %collective-permute-done.10.refs_2_ = f32[168,128]{1,0:T(8,128)S(1)} collective-permute-done((f32[168,128]{1,0:T(8,128)S(1)}, f32[168,128]{1,0:T(8,128)S(1)}, u32[]{:S(2)}, u32[]{:S(2)}) %collective-permute-start.10) | collective-permute-done | bytes 86048 | tf_op jit(solution)/shard_map/ppermute | solution.py:184
  73.2 1.4 %up.2 = bf16[168,512]{1,0:T(8,128)(2,1)S(1)} custom-call(s32[1]{0:T(128)} %bitcast.me_ref, s32[7]{0:T(128)S(1)} %copy-done.1, s32[7]{0:T(128)S(1)} %copy-done.2, bf16[168,2048]{1,0:T(8,128)(2,1)S(1)} %collective-permute-done.8.refs_0_.refs_1_.refs_2_.refs_3_.refs_4_, f32[168,128]{1,0:T(8,128)S(1)} %low.8.refs_1_, ...), custom_call_target="tpu_custom_call" | custom-call | tf_op jit(solution)/shard_map/up/pallas_call | solution.py:287
  74.6 1.5 %collective-permute-start.12 = (bf16[168,512]{1,0:T(8,128)(2,1)S(1)}, bf16[168,512]{1,0:T(8,128)(2,1)S(1)}, u32[]{:S(2)}, u32[]{:S(2)}) collective-permute-start(bf16[168,512]{1,0:T(8,128)(2,1)S(1)} %up.2), channel_id=1, source_target_pairs={{0,4},{2,6},{4,0},{6,2},{8,12},{10,14},{12,8},{14,10},{1,5},{3,7},... | collective-permute-start | bytes 516104 | tf_op jit(solution)/shard_map/ppermute | solution.py:181
  76.1 2.7 %low.9.refs_0_ = f32[256,128]{1,0:T(8,128)S(1)} custom-call(s32[1]{0:T(128)} %bitcast.me_ref, s32[7]{0:T(128)S(1)} %copy-done.1, s32[7]{0:T(128)S(1)} %copy-done.2, bf16[256,4096]{1,0:T(8,128)(2,1)} %refs_7_.3, bf16[256,4096]{1,0:T(8,128)(2,1)} %refs_7_.3, bf16[256,4096]{1,0:T(8,128)(2,1)} %refs_7_.3, bf16[256,4096]{1,0:T(8,128)(2,1)} %refs_7_.3, ...), custom_call_target="tpu_custom_call" | custom-call | flops 1744830464 | bytes 6815744 | tf_op jit(solution)/shard_map/low/pallas_call | solution.py:250
  78.8 0.1 collective-permute-start.11
  78.9 1.3 %collective-permute-done.11.refs_1_ = f32[256,128]{1,0:T(8,128)S(1)} collective-permute-done((f32[256,128]{1,0:T(8,128)S(1)}, f32[256,128]{1,0:T(8,128)S(1)}, u32[]{:S(2)}, u32[]{:S(2)}) %collective-permute-start.11) | collective-permute-done | bytes 131104 | tf_op jit(solution)/shard_map/ppermute | solution.py:184
  80.2 1.5 %up.3.sum_ref = f32[256,512]{1,0:T(8,128)S(1)} custom-call(s32[1]{0:T(128)} %bitcast.me_ref, s32[7]{0:T(128)S(1)} %copy-done.1, s32[7]{0:T(128)S(1)} %copy-done.2, f32[256,128]{1,0:T(8,128)S(1)} %low.9.refs_0_, f32[256,128]{1,0:T(8,128)S(1)} %collective-permute-done.11.refs_1_, bf16[128,4608]{1,0:T(8,128)(2,1)S(1)} %copy-done, ...), custom_call_target="tpu_custom_call" | custom-call | tf_op jit(solution)/shard_map/up/pallas_call | solution.py:287
  81.7 1.6 %last.1 = bf16[256,512]{1,0:T(8,128)(2,1)} custom-call(s32[1]{0:T(128)} %bitcast.me_ref, s32[7]{0:T(128)S(1)} %copy-done.1, s32[7]{0:T(128)S(1)} %copy-done.2, f32[256,512]{1,0:T(8,128)S(1)} %up.3.sum_ref, bf16[168,512]{1,0:T(8,128)(2,1)S(1)} %collective-permute-done.12.back_ref), custom_call_target="tpu_custom_call" | custom-call | tf_op jit(solution)/shard_map/last/pallas_call | solution.py:306
  (19 shorter events, 0.0 us)
Async XLA Ops:
  2.5 9.1 %collective-permute-start.6 = (bf16[256,4096]{1,0:T(8,128)(2,1)}, bf16[256,4096]{1,0:T(8,128)(2,1)}, u32[]{:S(2)}, u32[]{:S(2)}) collective-permute-start(bf16[256,4096]{1,0:T(8,128)(2,1)} %refs_7_.3), channel_id=1, source_target_pairs={{0,1},{1,0},{2,3},{3,2},{4,5},{5,4},{6,7},{7,6},{8,9},{9,8},{10,11... | collective-permute-start | bytes 6291464 | tf_op jit(solution)/shard_map/ppermute | solution.py:184
  3.1 38.5 %collective-permute-start.3 = (bf16[128,4608]{1,0:T(8,128)(2,1)}, bf16[128,4608]{1,0:T(8,128)(2,1)S(1)}, u32[]{:S(2)}, u32[]{:S(2)}) collective-permute-start(bf16[128,4608]{1,0:T(8,128)(2,1)} %get-tuple-element.21.refs_8_.refs_9_.refs_10_.refs_11_.refs_12_.refs_13_.refs_14_.refs_15_.refs_5_.refs_6_.refs_7_.r, ...), channel_id=1, source_target_pairs={{0,2},{2,0},{4,6},{6,4},{8,10},{10,8},{12,14},{14,12},{1,3},{3,1},... | collective-permute-start | bytes 3538952 | tf_op jit(solution)/shard_map/ppermute | solution.py:181
  5.6 35.6 %collective-permute-start = (bf16[128,2048]{1,0:T(8,128)(2,1)}, bf16[128,2048]{1,0:T(8,128)(2,1)}, u32[]{:S(2)}, u32[]{:S(2)}) collective-permute-start(bf16[128,2048]{1,0:T(8,128)(2,1)} %get-tuple-element.20), channel_id=1, source_target_pairs={{0,8},{2,10},{4,12},{6,14},{8,0},{10,2},{12,4},{14,6},{1,9},{3,11}... | collective-permute-start | bytes 1572872 | tf_op jit(solution)/shard_map/ppermute | solution.py:181
  8.2 47.1 %collective-permute-start.2 = (bf16[128,1536]{1,0:T(8,128)(2,1)}, bf16[128,1536]{1,0:T(8,128)(2,1)S(1)}, u32[]{:S(2)}, u32[]{:S(2)}) collective-permute-start(bf16[128,1536]{1,0:T(8,128)(2,1)} %get-tuple-element.27), channel_id=1, source_target_pairs={{0,8},{2,10},{4,12},{6,14},{8,0},{10,2},{12,4},{14,6},{1,9},{3,11}... | collective-permute-start | bytes 1179656 | tf_op jit(solution)/shard_map/ppermute | solution.py:181
  11.6 33.5 %copy-start = (bf16[128,4608]{1,0:T(8,128)(2,1)S(1)}, bf16[128,4608]{1,0:T(8,128)(2,1)}, u32[]{:S(2)}) copy-start(bf16[128,4608]{1,0:T(8,128)(2,1)} %get-tuple-element.21.refs_8_.refs_9_.refs_10_.refs_11_.refs_12_.refs_13_.refs_14_.refs_15_.refs_5_.refs_6_.refs_7_.refs_3_.refs_2_) | copy-start | bytes 3538948
  11.6 33.5 %copy-start.1 = (s32[7]{0:T(128)S(1)}, s32[7]{0:T(128)}, u32[]{:S(2)}) copy-start(s32[7]{0:T(128)} %len_ref.17) | copy-start | bytes 88
  11.7 33.5 %copy-start.2 = (s32[7]{0:T(128)S(1)}, s32[7]{0:T(128)}, u32[]{:S(2)}) copy-start(s32[7]{0:T(128)} %id_ref.17) | copy-start | bytes 88
  11.7 55.7 %collective-permute-start.8 = (bf16[168,2048]{1,0:T(8,128)(2,1)}, bf16[168,2048]{1,0:T(8,128)(2,1)S(1)}, u32[]{:S(2)}, u32[]{:S(2)}) collective-permute-start(bf16[168,2048]{1,0:T(8,128)(2,1)} %get-tuple-element.32), channel_id=1, source_target_pairs={{0,4},{2,6},{4,0},{6,2},{8,12},{10,14},{12,8},{14,10},{1,5},{3,7},... | collective-permute-start | bytes 2064392 | tf_op jit(solution)/shard_map/ppermute | solution.py:181
  41.3 14.2 %slice-start = ((s8[8388608]{0:T(1024)(128)(4,1)}), s8[4194304]{0:T(1024)(128)(4,1)S(1)}, s32[]{:S(2)}) async-start(s8[8388608]{0:T(1024)(128)(4,1)} %bitcast.9), calls=%async_computation | async-start | bytes 8388608
  41.3 14.2 %slice-start.1 = ((s8[8388608]{0:T(1024)(128)(4,1)}), s8[4194304]{0:T(1024)(128)(4,1)S(1)}, s32[]{:S(2)}) async-start(s8[8388608]{0:T(1024)(128)(4,1)} %bitcast.9), calls=%async_computation.1 | async-start | bytes 8388608
  41.3 14.2 %copy-start.3 = (f32[256,512]{1,0:T(8,128)S(1)}, f32[256,512]{1,0:T(8,128)}, u32[]{:S(2)}) copy-start(f32[256,512]{1,0:T(8,128)} %fusion.2) | copy-start | bytes 1572868
  41.3 18.9 %collective-permute-start.5 = (bf16[128,1024]{1,0:T(8,128)(2,1)}, bf16[128,1024]{1,0:T(8,128)(2,1)S(1)}, u32[]{:S(2)}, u32[]{:S(2)}) collective-permute-start(bf16[128,1024]{1,0:T(8,128)(2,1)} %get-tuple-element.30), channel_id=1, source_target_pairs={{0,8},{2,10},{4,12},{6,14},{8,0},{10,2},{12,4},{14,6},{1,9},{3,11}... | collective-permute-start | bytes 786440 | tf_op jit(solution)/shard_map/ppermute | solution.py:181
  41.3 19.4 %collective-permute-start.1 = (bf16[128,2048]{1,0:T(8,128)(2,1)}, bf16[128,2048]{1,0:T(8,128)(2,1)S(1)}, u32[]{:S(2)}, u32[]{:S(2)}) collective-permute-start(bf16[128,2048]{1,0:T(8,128)(2,1)} %collective-permute-done.refs_24_.refs_25_.refs_26_.refs_13_.refs_14_.refs_15_.refs_4_.refs_3_), channel_id=1, source_target_pairs={{0,2},{2,0},{4,6},{6,4},{8,10},{10,8},{12,14},{14,12},{1,3},{3,1},... | collective-permute-start | bytes 1572872 | tf_op jit(solution)/shard_map/ppermute | solution.py:181
  41.5 28.1 %collective-permute-start.9 = (bf16[168,2048]{1,0:T(8,128)(2,1)}, bf16[168,2048]{1,0:T(8,128)(2,1)S(1)}, u32[]{:S(2)}, u32[]{:S(2)}) collective-permute-start(bf16[168,2048]{1,0:T(8,128)(2,1)} %get-tuple-element.33), channel_id=1, source_target_pairs={{0,4},{2,6},{4,0},{6,2},{8,12},{10,14},{12,8},{14,10},{1,5},{3,7},... | collective-permute-start | bytes 2064392 | tf_op jit(solution)/shard_map/ppermute | solution.py:181
  55.3 12.1 %collective-permute-start.4 = (bf16[128,1536]{1,0:T(8,128)(2,1)S(1)}, bf16[128,1536]{1,0:T(8,128)(2,1)S(1)}, u32[]{:S(2)}, u32[]{:S(2)}) collective-permute-start(bf16[128,1536]{1,0:T(8,128)(2,1)S(1)} %collective-permute-done.2.refs_19_.refs_13_.refs_14_.refs_11_.refs_12_), channel_id=1, source_target_pairs={{0,2},{2,0},{4,6},{6,4},{8,10},{10,8},{12,14},{14,12},{1,3},{3,1},... | collective-permute-start | bytes 1179656 | tf_op jit(solution)/shard_map/ppermute | solution.py:181
  60.2 10.8 %collective-permute-start.7 = (bf16[128,1024]{1,0:T(8,128)(2,1)S(1)}, bf16[128,1024]{1,0:T(8,128)(2,1)S(1)}, u32[]{:S(2)}, u32[]{:S(2)}) collective-permute-start(bf16[128,1024]{1,0:T(8,128)(2,1)S(1)} %collective-permute-done.5.refs_2_.refs_17_.refs_18_), channel_id=1, source_target_pairs={{0,2},{2,0},{4,6},{6,4},{8,10},{10,8},{12,14},{14,12},{1,3},{3,1},... | collective-permute-start | bytes 786440 | tf_op jit(solution)/shard_map/ppermute | solution.py:181
  71.8 1.3 %collective-permute-start.10 = (f32[168,128]{1,0:T(8,128)S(1)}, f32[168,128]{1,0:T(8,128)S(1)}, u32[]{:S(2)}, u32[]{:S(2)}) collective-permute-start(f32[168,128]{1,0:T(8,128)S(1)} %low.8.refs_1_), channel_id=1, source_target_pairs={{0,1},{1,0},{2,3},{3,2},{4,5},{5,4},{6,7},{7,6},{8,9},{9,8},{10,11... | collective-permute-start | bytes 258056 | tf_op jit(solution)/shard_map/ppermute | solution.py:184
  74.6 7.2 %collective-permute-start.12 = (bf16[168,512]{1,0:T(8,128)(2,1)S(1)}, bf16[168,512]{1,0:T(8,128)(2,1)S(1)}, u32[]{:S(2)}, u32[]{:S(2)}) collective-permute-start(bf16[168,512]{1,0:T(8,128)(2,1)S(1)} %up.2), channel_id=1, source_target_pairs={{0,4},{2,6},{4,0},{6,2},{8,12},{10,14},{12,8},{14,10},{1,5},{3,7},... | collective-permute-start | bytes 516104 | tf_op jit(solution)/shard_map/ppermute | solution.py:181
  78.8 1.4 %collective-permute-start.11 = (f32[256,128]{1,0:T(8,128)S(1)}, f32[256,128]{1,0:T(8,128)S(1)}, u32[]{:S(2)}, u32[]{:S(2)}) collective-permute-start(f32[256,128]{1,0:T(8,128)S(1)} %low.9.refs_0_), channel_id=1, source_target_pairs={{0,1},{1,0},{2,3},{3,2},{4,5},{5,4},{6,7},{7,6},{8,9},{9,8},{10,11... | collective-permute-start | bytes 393224 | tf_op jit(solution)/shard_map/ppermute | solution.py:184
